TPU v7x, 32 devices: a whole 2x2x4 slice. The times are simulated.
32 devices in a mesh: blk: 4 (over x, core), sub: 8 (over z, y).
Axes of the slice: x: 2, y: 2, z: 4, core: 2. Of those that a mesh axis runs over, the one named last changes fastest.
Arguments:
- images: bfloat16 [16384, 768], P(('blk', 'sub')), may hold values from -6 to 6
- texts: bfloat16 [16384, 768], P(('blk', 'sub')), may hold values from -6 to 6
- logit_scale: float32 [1], replicated, may hold values from 2 to 10
- logit_bias: float32 [1], replicated, may hold values from -4 to -1
Outputs:
- grad_images: float32 [16384, 768], P(('blk', 'sub'))
- grad_texts: float32 [16384, 768], P(('blk', 'sub'))
All inputs are finite; a program needn't handle non-finite values.
Results may differ from a plain program's by a relative error of at most 0.004.
Values may be sent and summed in bfloat16 or wider, within the bound.
No kernel may reach another device: no remote copies, remote signals or barrier semaphores. Data moves between devices by JAX's collectives and lax.ppermute only.
A program may use at most 64 MiB of HBM per device.

v0:
```python
import jax
import jax.numpy as jnp
from jax import lax
from jax.sharding import PartitionSpec as P


def passed_along(value, axis, steps):
    count = lax.axis_size(axis)
    pairs = [(source, (source + steps) % count) for source in range(count)]
    return lax.ppermute(value, axis, pairs)


def unit_rows(values_in):
    values = values_in.astype(jnp.float32)
    recip = lax.rsqrt(jnp.sum(values * values, axis=-1, keepdims=True) + 1e-06)
    return (values * recip, recip)


def tile_weights(left, right, scale, offset):
    logits = (
        scale
        * lax.dot_general(left, right, (((1,), (1,)), ((), ())), preferred_element_type=jnp.float32)
        + offset
    )
    return jax.nn.sigmoid(logits)


def contract_rows(weights, rows):
    return lax.dot_general(
        weights, rows, (((0,), (0,)), ((), ())), preferred_element_type=jnp.float32
    )


def back_norm(unit, recip, grad):
    return (grad - unit * jnp.sum(unit * grad, axis=-1, keepdims=True)) * recip


def shards(images, texts, logit_scale, logit_bias):
    unit_img, recip_img = unit_rows(images)
    unit_txt, recip_txt = unit_rows(texts)
    img_low = unit_img.astype(jnp.bfloat16)
    txt_low = unit_txt.astype(jnp.bfloat16)
    scale = logit_scale[0]
    offset = logit_bias[0]
    diagonal_one = jnp.eye(images.shape[0], dtype=jnp.float32)
    weight_own = (tile_weights(img_low, txt_low, scale, offset) - diagonal_one).astype(jnp.bfloat16)
    img_prev, txt_prev = passed_along((img_low, txt_low), ("blk", "sub"), 1)
    img_next, txt_next = passed_along((img_low, txt_low), ("blk", "sub"), -1)
    weight_prev = tile_weights(img_low, txt_prev, scale, offset).astype(jnp.bfloat16)
    weight_next = tile_weights(img_low, txt_next, scale, offset).astype(jnp.bfloat16)
    from_prev = tile_weights(img_prev, txt_low, scale, offset).astype(jnp.bfloat16)
    from_next = tile_weights(img_next, txt_low, scale, offset).astype(jnp.bfloat16)
    grad_txt = scale * (
        contract_rows(weight_own, img_low)
        + contract_rows(from_prev, img_prev)
        + contract_rows(from_next, img_next)
    )
    grad_img = scale * (
        jnp.dot(weight_own, txt_low, preferred_element_type=jnp.float32)
        + jnp.dot(weight_prev, txt_prev, preferred_element_type=jnp.float32)
        + jnp.dot(weight_next, txt_next, preferred_element_type=jnp.float32)
    )
    return (back_norm(unit_img, recip_img, grad_img), back_norm(unit_txt, recip_txt, grad_txt))


def solution(mesh):
    in_specs = (P(("blk", "sub"), None), P(("blk", "sub"), None), P(), P())
    out_specs = (P(("blk", "sub"), None), P(("blk", "sub"), None))
    return jax.shard_map(shards, mesh=mesh, in_specs=in_specs, out_specs=out_specs, check_vma=False)
```

profile of v0, /device:TPU:0, one launch (start us, length us, event | category | flops | bytes accessed | tf_op | source)
XLA Modules:
  0.0 87.2 jit_solution(5785008208727878490)
XLA Ops:
  0.6 0.0 copy-start
  0.6 1.4 %fusion.13 = f32[512]{0:T(512)S(1)} fusion(bf16[512,768]{1,0:T(8,128)(2,1)} %param.5), kind=kLoop, calls=%fused_computation.17 | loop fusion | flops 1179136 | bytes 788480 | tf_op jit(solution)/shard_map/reduce_sum | solution.py:15
  2.1 2.2 %fusion.2 = bf16[512,768]{1,0:T(8,128)(2,1)} fusion(bf16[512,768]{1,0:T(8,128)(2,1)} %param.5, f32[512]{0:T(512)S(1)} %add_rsqrt_fusion), kind=kLoop, calls=%fused_computation.4 | loop fusion | flops 1179648 | bytes 1574912 | tf_op jit(solution)/shard_map/convert_element_type | solution.py:42
  4.3 0.0 copy-start.1
  4.3 6.4 %collective-permute-start.1 = (bf16[512,768]{1,0:T(8,128)(2,1)}, bf16[512,768]{1,0:T(8,128)(2,1)}, u32[]{:S(2)}, u32[]{:S(2)}) collective-permute-start(bf16[512,768]{1,0:T(8,128)(2,1)} %fusion.2), channel_id=1, source_target_pairs={{0,31},{1,0},{2,1},{3,2},{4,3},{5,4},{6,5},{7,6},{8,7},{9,8},{10,9... | collective-permute-start | bytes 2359304 | tf_op jit(solution)/shard_map/ppermute | solution.py:10
  10.7 0.0 collective-permute-start
  10.7 0.0 copy-done
  10.7 0.2 fusion.9
  10.9 1.1 %fusion.5 = bf16[512,768]{1,0:T(8,128)(2,1)} fusion(bf16[512,768]{1,0:T(8,128)(2,1)S(1)} %copy-done, f32[512]{0:T(512)S(1)} %add_rsqrt_fusion.1), kind=kLoop, calls=%fused_computation.9 | loop fusion | flops 1179648 | bytes 1574912 | tf_op jit(solution)/shard_map/convert_element_type | solution.py:41
  12.0 5.3 %collective-permute-start.3 = (bf16[512,768]{1,0:T(8,128)(2,1)}, bf16[512,768]{1,0:T(8,128)(2,1)}, u32[]{:S(2)}, u32[]{:S(2)}) collective-permute-start(bf16[512,768]{1,0:T(8,128)(2,1)} %fusion.5), channel_id=1, source_target_pairs={{0,31},{1,0},{2,1},{3,2},{4,3},{5,4},{6,5},{7,6},{8,7},{9,8},{10,9... | collective-permute-start | bytes 2359304 | tf_op jit(solution)/shard_map/ppermute | solution.py:10
  17.3 0.0 collective-permute-start.2
  18.6 0.0 copy-done.1
  18.7 0.8 fusion.40
  19.5 1.9 %fusion.74 = f32[512,768]{1,0:T(8,128)} fusion(bf16[512,512]{1,0:T(8,128)(2,1)S(1)} %fusion.40, bf16[512,768]{1,0:T(8,128)(2,1)S(1)} %copy-done.1, f32[512]{0:T(512)S(1)} %add_rsqrt_fusion), kind=kOutput, calls=%fused_computation.78 | convolution fusion | flops 403832832 | bytes 2885632 | tf_op jit(solution)/shard_map/dot_general | solution.py:59
  21.4 0.7 fusion.63
  22.0 37.0 %collective-permute-done = bf16[512,768]{1,0:T(8,128)(2,1)} collective-permute-done((bf16[512,768]{1,0:T(8,128)(2,1)}, bf16[512,768]{1,0:T(8,128)(2,1)}, u32[]{:S(2)}, u32[]{:S(2)}) %collective-permute-start) | collective-permute-done | bytes 786464 | tf_op jit(solution)/shard_map/ppermute | solution.py:10
  59.1 3.7 %fusion.45 = f32[512,768]{1,0:T(8,128)} fusion(bf16[512,768]{1,0:T(8,128)(2,1)} %collective-permute-done, f32[]{:T(128)} %bitcast.21, f32[]{:T(128)} %bitcast.16, bf16[512,768]{1,0:T(8,128)(2,1)S(1)} %copy-done, f32[512]{0:T(512)S(1)} %add_rsqrt_fusion.1), kind=kOutput, calls=%fused_computation.56 | convolution fusion | flops 808058880 | bytes 3147784 | tf_op jit(solution)/shard_map/dot_general | solution.py:60
  62.8 0.0 collective-permute-done.1
  62.8 4.7 %fusion.6 = (f32[512]{0:T(512)S(1)}, f32[512,768]{1,0:T(8,128)}) fusion(bf16[512,768]{1,0:T(8,128)(2,1)S(1)} %copy-done, f32[512]{0:T(512)S(1)} %add_rsqrt_fusion.1, bf16[512,768]{1,0:T(8,128)(2,1)} %collective-permute-done.1, f32[]{:T(128)} %bitcast.20, f32[]{:T(128)} %bitcast.12, f32[512,768]{1,0:T(8,128)} %fusion.74, f32[512,768]{1,0:T(8,128)} %fusion.45), kind=kOutput, calls=%fused_computation.10 | convolution fusion | flops 810810880 | bytes 6295560 | tf_op jit(solution)/shard_map/dot_general | solution.py:61
  67.5 2.9 %fusion.8 = f32[512,768]{1,0:T(8,128)} fusion(f32[512,768]{1,0:T(8,128)} %get-tuple-element.3, bf16[512,768]{1,0:T(8,128)(2,1)S(1)} %copy-done, f32[512]{0:T(512)S(1)} %get-tuple-element.2, f32[512]{0:T(512)S(1)} %add_rsqrt_fusion.1), kind=kLoop, calls=%fused_computation.12 | loop fusion | flops 1966080 | bytes 3936256 | tf_op jit(solution)/shard_map/mul | solution.py:35
  70.4 5.5 %collective-permute-done.2 = bf16[512,768]{1,0:T(8,128)(2,1)} collective-permute-done((bf16[512,768]{1,0:T(8,128)(2,1)}, bf16[512,768]{1,0:T(8,128)(2,1)}, u32[]{:S(2)}, u32[]{:S(2)}) %collective-permute-start.2) | collective-permute-done | bytes 786464 | tf_op jit(solution)/shard_map/ppermute | solution.py:10
  75.8 3.9 %fusion.46 = f32[512,768]{1,0:T(8,128)} fusion(bf16[512,768]{1,0:T(8,128)(2,1)} %collective-permute-done.2, f32[]{:T(128)} %bitcast.19, f32[]{:T(128)} %bitcast.15, bf16[512,768]{1,0:T(8,128)(2,1)S(1)} %copy-done.1, f32[512]{0:T(512)S(1)} %add_rsqrt_fusion), kind=kOutput, calls=%fused_computation.57 | convolution fusion | flops 808058880 | bytes 3147784 | tf_op jit(solution)/shard_map/dot_general | solution.py:29
  79.8 0.0 collective-permute-done.3
  79.8 4.6 %fusion.10 = (f32[512]{0:T(512)S(1)}, f32[512,768]{1,0:T(8,128)}) fusion(bf16[512,768]{1,0:T(8,128)(2,1)S(1)} %copy-done.1, f32[512]{0:T(512)S(1)} %add_rsqrt_fusion, bf16[512,768]{1,0:T(8,128)(2,1)} %collective-permute-done.3, f32[]{:T(128)} %bitcast.18, f32[]{:T(128)} %bitcast.14, f32[512,768]{1,0:T(8,128)S(1)} %fusion.63, f32[512,768]{1,0:T(8,128)} %fusion.46), kind=kOutput, calls=%fused_computation.14 | convolution fusion | flops 810810880 | bytes 6295560 | tf_op jit(solution)/shard_map/dot_general | solution.py:29
  84.4 2.9 %fusion.12 = f32[512,768]{1,0:T(8,128)} fusion(f32[512,768]{1,0:T(8,128)} %get-tuple-element.5, bf16[512,768]{1,0:T(8,128)(2,1)S(1)} %copy-done.1, f32[512]{0:T(512)S(1)} %get-tuple-element.4, f32[512]{0:T(512)S(1)} %add_rsqrt_fusion), kind=kLoop, calls=%fused_computation.16 | loop fusion | flops 1966080 | bytes 3936256 | tf_op jit(solution)/shard_map/mul | solution.py:35
  (2 shorter events, 0.0 us)
Async XLA Ops:
  0.6 10.0 %copy-start = (bf16[512,768]{1,0:T(8,128)(2,1)S(1)}, bf16[512,768]{1,0:T(8,128)(2,1)}, u32[]{:S(2)}) copy-start(bf16[512,768]{1,0:T(8,128)(2,1)} %param.4) | copy-start | bytes 2359300
  4.3 14.4 %copy-start.1 = (bf16[512,768]{1,0:T(8,128)(2,1)S(1)}, bf16[512,768]{1,0:T(8,128)(2,1)}, u32[]{:S(2)}) copy-start(bf16[512,768]{1,0:T(8,128)(2,1)} %param.5) | copy-start | bytes 2359300
  4.3 58.5 %collective-permute-start.1 = (bf16[512,768]{1,0:T(8,128)(2,1)}, bf16[512,768]{1,0:T(8,128)(2,1)}, u32[]{:S(2)}, u32[]{:S(2)}) collective-permute-start(bf16[512,768]{1,0:T(8,128)(2,1)} %fusion.2), channel_id=1, source_target_pairs={{0,31},{1,0},{2,1},{3,2},{4,3},{5,4},{6,5},{7,6},{8,7},{9,8},{10,9... | collective-permute-start | bytes 2359304 | tf_op jit(solution)/shard_map/ppermute | solution.py:10
  10.7 48.4 %collective-permute-start = (bf16[512,768]{1,0:T(8,128)(2,1)}, bf16[512,768]{1,0:T(8,128)(2,1)}, u32[]{:S(2)}, u32[]{:S(2)}) collective-permute-start(bf16[512,768]{1,0:T(8,128)(2,1)} %fusion.2), channel_id=1, source_target_pairs={{0,1},{1,2},{2,3},{3,4},{4,5},{5,6},{6,7},{7,8},{8,9},{9,10},{10,1... | collective-permute-start | bytes 2359304 | tf_op jit(solution)/shard_map/ppermute | solution.py:10
  12.0 67.8 %collective-permute-start.3 = (bf16[512,768]{1,0:T(8,128)(2,1)}, bf16[512,768]{1,0:T(8,128)(2,1)}, u32[]{:S(2)}, u32[]{:S(2)}) collective-permute-start(bf16[512,768]{1,0:T(8,128)(2,1)} %fusion.5), channel_id=1, source_target_pairs={{0,31},{1,0},{2,1},{3,2},{4,3},{5,4},{6,5},{7,6},{8,7},{9,8},{10,9... | collective-permute-start | bytes 2359304 | tf_op jit(solution)/shard_map/ppermute | solution.py:10
  17.3 58.5 %collective-permute-start.2 = (bf16[512,768]{1,0:T(8,128)(2,1)}, bf16[512,768]{1,0:T(8,128)(2,1)}, u32[]{:S(2)}, u32[]{:S(2)}) collective-permute-start(bf16[512,768]{1,0:T(8,128)(2,1)} %fusion.5), channel_id=1, source_target_pairs={{0,1},{1,2},{2,3},{3,4},{4,5},{5,6},{6,7},{7,8},{8,9},{9,10},{10,1... | collective-permute-start | bytes 2359304 | tf_op jit(solution)/shard_map/ppermute | solution.py:10
where the time goes:
time: 87.6 us; the launch traced here: 87.2 us
  waiting for transfers between devices  42.5 us (49%)
  matrix products  20.3 us (23%)
  starting transfers between devices  11.7 us (13%)
  other arithmetic  10.7 us (12%)
  between operations  1.97 us (2%)
    ppermute x4, waiting for transfers between devices, passed_along(): return lax.ppermute(value, axis, pairs)  42.5 us
    ppermute x4, starting transfers between devices, passed_along(): return lax.ppermute(value, axis, pairs)  11.7 us
    dot_general x3, matrix products, contract_rows(): lax.dot_general(weights, rows, (((0,), (0,)), ((), ())), preferred_elemen...  9.2 us
    mul x2, other arithmetic, back_norm(): return (grad - unit * jnp.sum(unit * grad, axis=-1, keepdims=True)) * recip  5.77 us
    dot_general x1, matrix products, shards(): jnp.dot(weight_next, txt_next, preferred_element_type=jnp.float32)  4.72 us
    dot_general x1, matrix products, shards(): jnp.dot(weight_prev, txt_prev, preferred_element_type=jnp.float32)  3.68 us
    convert_element_type x1, other arithmetic, shards(): txt_low = unit_txt.astype(jnp.bfloat16)  2.21 us
    dot_general x1, matrix products, shards(): jnp.dot(weight_own, txt_low, preferred_element_type=jnp.float32)  1.86 us
  transfers between devices with their start and end apart: 4, of which 2 were waited for; matrix products, arithmetic and copies ran while one was open for 23% of the time, Pallas kernels for 0%

commit v1 on v0

v1 whole, which is shorter than its diff:
```python
import functools

import jax
import jax.numpy as jnp
from jax import lax
from jax.experimental import pallas as pl
from jax.experimental.pallas import tpu as pltpu
from jax.sharding import PartitionSpec as P

AXES = ("blk", "sub")
LAST = (((1,), (1,)), ((), ()))
FIRST = (((0,), (0,)), ((), ()))
VMEM_LIMIT = 24 * 1024 * 1024


def unit_rows(values_in):
    values = values_in.astype(jnp.float32)
    recip = lax.rsqrt(jnp.sum(values * values, axis=-1, keepdims=True) + 1e-06)
    return values * recip, recip


def dot32(left, right, dims):
    return lax.dot_general(left, right, dims, preferred_element_type=jnp.float32)


def band_term(own_low, other_low, scale, offset):
    weight = jax.nn.sigmoid(scale * dot32(own_low, other_low, LAST) + offset)
    return jnp.dot(
        weight.astype(jnp.bfloat16), other_low, preferred_element_type=jnp.float32
    )


def own_kernel(scale_ref, offset_ref, img_ref, txt_ref, img_low, txt_low, sum_img, sum_txt):
    scale, offset = scale_ref[0], offset_ref[0]
    img_low[...] = unit_rows(img_ref[...])[0].astype(jnp.bfloat16)
    txt_low[...] = unit_rows(txt_ref[...])[0].astype(jnp.bfloat16)
    logits = scale * dot32(img_low[...], txt_low[...], LAST) + offset
    rows = lax.broadcasted_iota(jnp.int32, logits.shape, 0)
    columns = lax.broadcasted_iota(jnp.int32, logits.shape, 1)
    weight = jax.nn.sigmoid(logits) - (rows == columns).astype(jnp.float32)
    weight = weight.astype(jnp.bfloat16)
    sum_img[...] = jnp.dot(weight, txt_low[...], preferred_element_type=jnp.float32)
    sum_txt[...] = dot32(weight, img_low[...], FIRST)


def add_kernel(scale_ref, offset_ref, low_ref, other_ref, sum_in, sum_out, other_low):
    scale, offset = scale_ref[0], offset_ref[0]
    other_low[...] = unit_rows(other_ref[...])[0].astype(jnp.bfloat16)
    sum_out[...] = sum_in[...] + band_term(low_ref[...], other_low[...], scale, offset)


def last_kernel(count, scale_ref, offset_ref, raw_ref, low_ref, sum_ref, *rest):
    others, (out_ref, other_low) = rest[:count], rest[count:]
    scale, offset = scale_ref[0], offset_ref[0]

    @pl.when(pl.program_id(0) == 0)
    def _():
        at = 0
        for other in others:
            rows = other.shape[0]
            other_low[at : at + rows, :] = unit_rows(other[...])[0].astype(jnp.bfloat16)
            at += rows

    total = sum_ref[...] + band_term(low_ref[...], other_low[...], scale, offset)
    grad = scale * total
    unit, recip = unit_rows(raw_ref[...])
    out_ref[...] = (grad - unit * jnp.sum(unit * grad, axis=-1, keepdims=True)) * recip


def cost(own, others, width, flops_scale=1.0):
    return pl.CostEstimate(
        flops=int(4 * own * others * width * flops_scale),
        bytes_accessed=own * width * 10 + others * width * 2,
        transcendentals=own * others,
    )


SMEM = pl.BlockSpec(memory_space=pltpu.SMEM)
VMEM = pl.BlockSpec(memory_space=pltpu.VMEM)
PARAMS = pltpu.CompilerParams(vmem_limit_bytes=VMEM_LIMIT)


def own_call(scale, offset, images, texts):
    rows, width = images.shape
    low = jax.ShapeDtypeStruct((rows, width), jnp.bfloat16)
    total = jax.ShapeDtypeStruct((rows, width), jnp.float32)
    return pl.pallas_call(
        own_kernel,
        out_shape=(low, low, total, total),
        in_specs=[SMEM, SMEM, VMEM, VMEM],
        out_specs=(VMEM,) * 4,
        compiler_params=PARAMS,
        cost_estimate=cost(rows, rows, width, 1.5),
    )(scale, offset, images, texts)


def add_call(scale, offset, low, other, total):
    rows, width = low.shape
    return pl.pallas_call(
        add_kernel,
        out_shape=jax.ShapeDtypeStruct((rows, width), jnp.float32),
        in_specs=[SMEM, SMEM, VMEM, VMEM, VMEM],
        out_specs=VMEM,
        scratch_shapes=[pltpu.VMEM(other.shape, jnp.bfloat16)],
        input_output_aliases={4: 0},
        compiler_params=PARAMS,
        cost_estimate=cost(rows, other.shape[0], width),
    )(scale, offset, low, other, total)


def last_call(scale, offset, raw, low, total, others):
    rows, width = raw.shape
    steps = 4 if rows % 64 == 0 else 1
    block = pl.BlockSpec((rows // steps, width), lambda step: (step, 0))
    count = sum(other.shape[0] for other in others)
    return pl.pallas_call(
        functools.partial(last_kernel, len(others)),
        grid=(steps,),
        out_shape=jax.ShapeDtypeStruct((rows, width), jnp.float32),
        in_specs=[SMEM, SMEM, block, block, block] + [VMEM] * len(others),
        out_specs=block,
        scratch_shapes=[pltpu.VMEM((count, width), jnp.bfloat16)],
        compiler_params=PARAMS,
        cost_estimate=cost(rows, count, width),
    )(scale, offset, raw, low, total, *others)


def exchange(value, target):
    count = lax.axis_size(AXES)
    return lax.ppermute(value, AXES, [(at, target(at) % count) for at in range(count)])


def partner(at):
    return at ^ 1


def onward(at):
    return at + 2 if at % 2 == 0 else at - 2


def backward(at):
    return at - 2 if at % 2 == 0 else at + 2


def tied(value, *others):
    return lax.optimization_barrier((value, *others))[0]


def shards(images, texts, logit_scale, logit_bias):
    rows = images.shape[0]
    cut = rows * 3 // 4
    rest = rows - cut
    args = (logit_scale, logit_bias)
    txt_head, img_head = texts[:cut], images[:cut]
    tails = jnp.concatenate([texts[cut:], images[cut:]], axis=0)

    near_txt = exchange(txt_head, partner)
    near_img = exchange(img_head, partner)
    side = exchange(tails, backward)

    img_low, txt_low, sum_img, sum_txt = own_call(*args, images, texts)

    far_txt = exchange(near_txt, onward)
    near_tails = exchange(tied(tails, near_txt), partner)
    far_tails = exchange(tied(side, near_txt), partner)
    sum_img = add_call(*args, img_low, near_txt, sum_img)

    far_img = exchange(near_img, onward)
    sum_txt = add_call(*args, txt_low, near_img, sum_txt)
    sum_img = add_call(*args, img_low, far_txt, sum_img)

    grad_img = last_call(
        *args, images, img_low, sum_img, (near_tails[:rest], far_tails[:rest])
    )
    grad_txt = last_call(
        *args, texts, txt_low, sum_txt, (near_tails[rest:], far_tails[rest:], far_img)
    )
    return grad_img, grad_txt


def solution(mesh):
    split = P(AXES, None)
    return jax.shard_map(
        shards,
        mesh=mesh,
        in_specs=(split, split, P(), P()),
        out_specs=(split, split),
        check_vma=False,
    )
```

time: 87.6 us -> 59.1 us (0.67)
  matrix products: 20.3 us -> 0 us
  waiting for transfers between devices: 42.5 us -> 28.5 us
  Pallas kernels: 0 us -> 13.6 us
  other arithmetic: 10.7 us -> 0.03 us
  starting transfers between devices: 11.7 us -> 13.4 us
  local copies, waits for them, and re-layouts: 0.01 us -> 1.31 us
    dot_general x7 -> x0, matrix products: 20.3 us -> none  [the longest x3 9.2 us: contract_rows(): lax.dot_general(weights, rows, (((0,), (0,)), ((), ())), preferred_elemen...]
    ppermute x4 -> x7, waiting for transfers between devices: 42.5 us -> 28.5 us  [exchange(): lax.ppermute(value, AXES, [(at, target(at) % count) for at in range(count)])]
    pallas_call x0 -> x6, Pallas kernels: none -> 13.6 us  [the longest x2 7.93 us: last_call(): pl.pallas_call(functools.partial(last_kernel, len(others)), grid=(steps,)...]
    mul x2 -> x0, other arithmetic: 5.77 us -> none  [back_norm(): return (grad - unit * jnp.sum(unit * grad, axis=-1, keepdims=True)) * recip]
    convert_element_type x2 -> x0, other arithmetic: 3.3 us -> none  [the longest x1 2.21 us: shards(): txt_low = unit_txt.astype(jnp.bfloat16)]
    ppermute x4 -> x7, starting transfers between devices: 11.7 us -> 13.4 us  [exchange(): lax.ppermute(value, AXES, [(at, target(at) % count) for at in range(count)])]
    reduce_sum x2 -> x0, other arithmetic: 1.66 us -> none  [unit_rows(): recip = lax.rsqrt(jnp.sum(values * values, axis=-1, keepdims=True) + 1e-06)]
    slice x0 -> x8, local copies, waits for them, and re-layouts: none -> 1.3 us  [the longest x2 1.24 us: shards(): txt_head, img_head = (texts[:cut], images[:cut])]
  transfers between devices with their start and end apart: 4 -> 7, of which waited for: 2 -> 5; matrix products, arithmetic and copies ran while one was open for 23% -> 0% of each run, Pallas kernels for 0% -> 16%
where the time goes in v1:
time: 59.1 us; the launch traced here: 58.9 us
  waiting for transfers between devices  28.5 us (48%)
  Pallas kernels  13.6 us (23%)
  starting transfers between devices  13.4 us (23%)
  between operations  2.05 us (3%)
  local copies, waits for them, and re-layouts  1.31 us (2%)
    ppermute x7, waiting for transfers between devices, exchange(): lax.ppermute(value, AXES, [(at, target(at) % count) for at in range(count)])  28.5 us
    ppermute x7, starting transfers between devices, exchange(): lax.ppermute(value, AXES, [(at, target(at) % count) for at in range(count)])  13.4 us
    pallas_call x2, Pallas kernels, last_call(): pl.pallas_call(functools.partial(last_kernel, len(others)), grid=(steps,)...  7.93 us
    pallas_call x3, Pallas kernels, add_call(): pl.pallas_call(add_kernel, out_shape=jax.ShapeDtypeStruct((rows, width),...  3.93 us
    pallas_call x1, Pallas kernels, own_call(): pl.pallas_call(own_kernel, out_shape=(low, low, total, total), in_specs=[...  1.74 us
    slice x2, local copies, waits for them, and re-layouts, shards(): txt_head, img_head = (texts[:cut], images[:cut])  1.24 us
  transfers between devices with their start and end apart: 7, of which 5 were waited for; matrix products, arithmetic and copies ran while one was open for 0% of the time, Pallas kernels for 16%

profile of v1, /device:TPU:0, one launch (start us, length us, event | category | flops | bytes accessed | tf_op | source)
XLA Modules:
  0.0 58.9 jit_solution(8835298085837030568)
XLA Ops:
  0.6 0.0 slice-start
  0.6 0.0 copy-start.1
  0.7 0.0 slice-start.1
  0.7 1.2 %slice.24 = bf16[384,768]{1,0:T(8,128)(2,1)S(1)} slice(bf16[512,768]{1,0:T(8,128)(2,1)} %raw_ref.3), slice={[0:384], [0:768]} | slice | bytes 1179648 | tf_op jit(solution)/shard_map/slice | solution.py:154
  1.9 0.0 copy-start
  1.9 3.0 %collective-permute-start = (bf16[384,768]{1,0:T(8,128)(2,1)S(1)}, bf16[384,768]{1,0:T(8,128)(2,1)S(1)}, u32[]{:S(2)}, u32[]{:S(2)}) collective-permute-start(bf16[384,768]{1,0:T(8,128)(2,1)S(1)} %slice.24), channel_id=1, source_target_pairs={{0,1},{1,0},{2,3},{3,2},{4,5},{5,4},{6,7},{7,6},{8,9},{9,8},{10,11... | collective-permute-start | bytes 1769480 | tf_op jit(solution)/shard_map/ppermute | solution.py:130
  4.9 0.0 copy-done.1
  5.0 0.1 collective-permute-start.5
  5.1 0.0 slice-done
  5.1 0.0 slice-done.1
  5.1 3.9 %collective-permute-start.3 = (bf16[256,768]{1,0:T(8,128)(2,1)S(1)}, bf16[256,768]{1,0:T(8,128)(2,1)S(1)}, u32[]{:S(2)}, u32[]{:S(2)}) collective-permute-start(bf16[256,768]{1,0:T(8,128)(2,1)S(1)} %pad_maximum_fusion), channel_id=1, source_target_pairs={{0,30},{1,3},{2,0},{3,5},{4,2},{5,7},{6,4},{7,9},{8,6},{9,11},{10,... | collective-permute-start | bytes 1179656 | tf_op jit(solution)/shard_map/ppermute | solution.py:130
  9.0 10.0 %collective-permute-done.other_ref = bf16[384,768]{1,0:T(8,128)(2,1)S(1)} collective-permute-done((bf16[384,768]{1,0:T(8,128)(2,1)S(1)}, bf16[384,768]{1,0:T(8,128)(2,1)S(1)}, u32[]{:S(2)}, u32[]{:S(2)}) %collective-permute-start) | collective-permute-done | bytes 589856 | tf_op jit(solution)/shard_map/ppermute | solution.py:130
  19.1 2.1 %collective-permute-start.2 = (bf16[256,768]{1,0:T(8,128)(2,1)S(1)}, bf16[256,768]{1,0:T(8,128)(2,1)S(1)}, u32[]{:S(2)}, u32[]{:S(2)}) collective-permute-start(bf16[256,768]{1,0:T(8,128)(2,1)S(1)} %pad_maximum_fusion), channel_id=1, source_target_pairs={{0,1},{1,0},{2,3},{3,2},{4,5},{5,4},{6,7},{7,6},{8,9},{9,8},{10,11... | collective-permute-start | bytes 1179656 | tf_op jit(solution)/shard_map/ppermute | solution.py:130
  22.4 0.0 collective-permute-done.3
  22.4 0.1 collective-permute-start.4
  22.5 0.0 copy-done
  22.5 1.7 %shard_map.59 = (bf16[512,768]{1,0:T(8,128)(2,1)S(1)}, bf16[512,768]{1,0:T(8,128)(2,1)S(1)}, f32[512,768]{1,0:T(8,128)S(1)}, f32[512,768]{1,0:T(8,128)S(1)}) custom-call(f32[1]{0:T(128)S(6)} %copy.12.scale_ref, f32[1]{0:T(128)S(6)} %copy.13.offset_ref, bf16[512,768]{1,0:T(8,128)(2,1)S(1)} %copy-done.1, bf16[512,768]{1,0:T(8,128)(2,1)S(1)} %copy-done), custom_call_target="tpu_custom_call" | custom-call | flops 1207959552 | bytes 4718592 | tf_op jit(solution)/shard_map/pallas_call | solution.py:87
  24.3 2.1 %collective-permute-start.1 = (bf16[384,768]{1,0:T(8,128)(2,1)S(1)}, bf16[384,768]{1,0:T(8,128)(2,1)S(1)}, u32[]{:S(2)}, u32[]{:S(2)}) collective-permute-start(bf16[384,768]{1,0:T(8,128)(2,1)S(1)} %collective-permute-done.other_ref), channel_id=1, source_target_pairs={{0,2},{1,31},{2,4},{3,1},{4,6},{5,3},{6,8},{7,5},{8,10},{9,7},{10,... | collective-permute-start | bytes 1769480 | tf_op jit(solution)/shard_map/ppermute | solution.py:130
  26.4 5.3 %collective-permute-done.5.other_ref = bf16[384,768]{1,0:T(8,128)(2,1)S(1)} collective-permute-done((bf16[384,768]{1,0:T(8,128)(2,1)S(1)}, bf16[384,768]{1,0:T(8,128)(2,1)S(1)}, u32[]{:S(2)}, u32[]{:S(2)}) %collective-permute-start.5) | collective-permute-done | bytes 589856 | tf_op jit(solution)/shard_map/ppermute | solution.py:130
  31.7 2.1 %collective-permute-start.6 = (bf16[384,768]{1,0:T(8,128)(2,1)S(1)}, bf16[384,768]{1,0:T(8,128)(2,1)S(1)}, u32[]{:S(2)}, u32[]{:S(2)}) collective-permute-start(bf16[384,768]{1,0:T(8,128)(2,1)S(1)} %collective-permute-done.5.other_ref), channel_id=1, source_target_pairs={{0,2},{1,31},{2,4},{3,1},{4,6},{5,3},{6,8},{7,5},{8,10},{9,7},{10,... | collective-permute-start | bytes 1769480 | tf_op jit(solution)/shard_map/ppermute | solution.py:130
  33.8 1.3 %shard_map.60.sum_in = f32[512,768]{1,0:T(8,128)S(1)} custom-call(f32[1]{0:T(128)S(6)} %copy.12.scale_ref, f32[1]{0:T(128)S(6)} %copy.13.offset_ref, bf16[512,768]{1,0:T(8,128)(2,1)S(1)} %get-tuple-element.8.low_ref, bf16[384,768]{1,0:T(8,128)(2,1)S(1)} %collective-permute-done.other_ref, ...), custom_call_target="tpu_custom_call", output_to_operand_aliasing={{}: (4, {})} | custom-call | flops 603979776 | bytes 4521984 | tf_op jit(solution)/shard_map/pallas_call | solution.py:99
  35.1 1.3 %shard_map.63.sum_ref = f32[512,768]{1,0:T(8,128)S(1)} custom-call(f32[1]{0:T(128)S(6)} %copy.12.scale_ref, f32[1]{0:T(128)S(6)} %copy.13.offset_ref, bf16[512,768]{1,0:T(8,128)(2,1)S(1)} %get-tuple-element.12.low_ref, bf16[384,768]{1,0:T(8,128)(2,1)S(1)} %collective-permute-done.5.other_ref, ...), custom_call_target="tpu_custom_call", output_to_operand_aliasing={{}: (4, {})} | custom-call | flops 603979776 | bytes 4521984 | tf_op jit(solution)/shard_map/pallas_call | solution.py:99
  36.5 3.7 %collective-permute-done.2 = bf16[256,768]{1,0:T(8,128)(2,1)S(1)} collective-permute-done((bf16[256,768]{1,0:T(8,128)(2,1)S(1)}, bf16[256,768]{1,0:T(8,128)(2,1)S(1)}, u32[]{:S(2)}, u32[]{:S(2)}) %collective-permute-start.2) | collective-permute-done | bytes 393248 | tf_op jit(solution)/shard_map/ppermute | solution.py:130
  40.2 7.6 %collective-permute-done.4 = bf16[256,768]{1,0:T(8,128)(2,1)S(1)} collective-permute-done((bf16[256,768]{1,0:T(8,128)(2,1)S(1)}, bf16[256,768]{1,0:T(8,128)(2,1)S(1)}, u32[]{:S(2)}, u32[]{:S(2)}) %collective-permute-start.4) | collective-permute-done | bytes 393248 | tf_op jit(solution)/shard_map/ppermute | solution.py:130
  47.8 0.0 collective-permute-done.1.other_ref
  47.8 1.3 %shard_map.61.sum_ref = f32[512,768]{1,0:T(8,128)S(1)} custom-call(f32[1]{0:T(128)S(6)} %copy.12.scale_ref, f32[1]{0:T(128)S(6)} %copy.13.offset_ref, bf16[512,768]{1,0:T(8,128)(2,1)S(1)} %get-tuple-element.8.low_ref, bf16[384,768]{1,0:T(8,128)(2,1)S(1)} %collective-permute-done.1.other_ref, ...), custom_call_target="tpu_custom_call", output_to_operand_aliasing={{}: (4, {})} | custom-call | flops 603979776 | bytes 4521984 | tf_op jit(solution)/shard_map/pallas_call | solution.py:99
  49.1 3.5 %shard_map.62 = f32[512,768]{1,0:T(8,128)} custom-call(f32[1]{0:T(128)S(6)} %copy.12.scale_ref, f32[1]{0:T(128)S(6)} %copy.13.offset_ref, bf16[512,768]{1,0:T(8,128)(2,1)S(1)} %copy-done.1, bf16[512,768]{1,0:T(8,128)(2,1)S(1)} %get-tuple-element.8.low_ref, f32[512,768]{1,0:T(8,128)S(1)} %shard_map.61.sum_ref, ...), custom_call_target="tpu_custom_call" | custom-call | flops 402653184 | bytes 4325376 | tf_op jit(solution)/shard_map/pallas_call | solution.py:116
  52.6 1.9 %collective-permute-done.6.rest_2_ = bf16[384,768]{1,0:T(8,128)(2,1)S(1)} collective-permute-done((bf16[384,768]{1,0:T(8,128)(2,1)S(1)}, bf16[384,768]{1,0:T(8,128)(2,1)S(1)}, u32[]{:S(2)}, u32[]{:S(2)}) %collective-permute-start.6) | collective-permute-done | bytes 589856 | tf_op jit(solution)/shard_map/ppermute | solution.py:130
  54.4 4.5 %shard_map.64 = f32[512,768]{1,0:T(8,128)} custom-call(f32[1]{0:T(128)S(6)} %copy.12.scale_ref, f32[1]{0:T(128)S(6)} %copy.13.offset_ref, bf16[512,768]{1,0:T(8,128)(2,1)S(1)} %copy-done, bf16[512,768]{1,0:T(8,128)(2,1)S(1)} %get-tuple-element.12.low_ref, f32[512,768]{1,0:T(8,128)S(1)} %shard_map.63.sum_ref, bf16[128,768]{1,0:T(8,128)(2,1)S(1)} %get-tuple-element.16.rest_0_, ...), custom_call_target="tpu_custom_call" | custom-call | flops 1006632960 | bytes 4915200 | tf_op jit(solution)/shard_map/pallas_call | solution.py:116
  (4 shorter events, 0.1 us)
Async XLA Ops:
  0.6 4.4 %slice-start = ((bf16[512,768]{1,0:T(8,128)(2,1)}), bf16[128,768]{1,0:T(8,128)(2,1)S(1)}, s32[]{:S(2)}) async-start(bf16[512,768]{1,0:T(8,128)(2,1)} %raw_ref.3), calls=%async_computation | async-start | bytes 393216 | tf_op jit(solution)/shard_map/slice | solution.py:155
  0.6 4.3 %copy-start.1 = (bf16[512,768]{1,0:T(8,128)(2,1)S(1)}, bf16[512,768]{1,0:T(8,128)(2,1)}, u32[]{:S(2)}) copy-start(bf16[512,768]{1,0:T(8,128)(2,1)} %raw_ref.2) | copy-start | bytes 2359300
  0.7 4.4 %slice-start.1 = ((bf16[512,768]{1,0:T(8,128)(2,1)}), bf16[128,768]{1,0:T(8,128)(2,1)S(1)}, s32[]{:S(2)}) async-start(bf16[512,768]{1,0:T(8,128)(2,1)} %raw_ref.2), calls=%async_computation.1 | async-start | bytes 393216 | tf_op jit(solution)/shard_map/slice | solution.py:155
  1.9 20.7 %copy-start = (bf16[512,768]{1,0:T(8,128)(2,1)S(1)}, bf16[512,768]{1,0:T(8,128)(2,1)}, u32[]{:S(2)}) copy-start(bf16[512,768]{1,0:T(8,128)(2,1)} %raw_ref.3) | copy-start | bytes 2359300
  1.9 17.2 %collective-permute-start = (bf16[384,768]{1,0:T(8,128)(2,1)S(1)}, bf16[384,768]{1,0:T(8,128)(2,1)S(1)}, u32[]{:S(2)}, u32[]{:S(2)}) collective-permute-start(bf16[384,768]{1,0:T(8,128)(2,1)S(1)} %slice.24), channel_id=1, source_target_pairs={{0,1},{1,0},{2,3},{3,2},{4,5},{5,4},{6,7},{7,6},{8,9},{9,8},{10,11... | collective-permute-start | bytes 1769480 | tf_op jit(solution)/shard_map/ppermute | solution.py:130
  5.0 26.8 %collective-permute-start.5 = (bf16[384,768]{1,0:T(8,128)(2,1)S(1)}, bf16[384,768]{1,0:T(8,128)(2,1)S(1)}, u32[]{:S(2)}, u32[]{:S(2)}) collective-permute-start(bf16[384,768]{1,0:T(8,128)(2,1)S(1)} %slice.29), channel_id=1, source_target_pairs={{0,1},{1,0},{2,3},{3,2},{4,5},{5,4},{6,7},{7,6},{8,9},{9,8},{10,11... | collective-permute-start | bytes 1769480 | tf_op jit(solution)/shard_map/ppermute | solution.py:130
  5.1 17.3 %collective-permute-start.3 = (bf16[256,768]{1,0:T(8,128)(2,1)S(1)}, bf16[256,768]{1,0:T(8,128)(2,1)S(1)}, u32[]{:S(2)}, u32[]{:S(2)}) collective-permute-start(bf16[256,768]{1,0:T(8,128)(2,1)S(1)} %pad_maximum_fusion), channel_id=1, source_target_pairs={{0,30},{1,3},{2,0},{3,5},{4,2},{5,7},{6,4},{7,9},{8,6},{9,11},{10,... | collective-permute-start | bytes 1179656 | tf_op jit(solution)/shard_map/ppermute | solution.py:130
  19.1 21.1 %collective-permute-start.2 = (bf16[256,768]{1,0:T(8,128)(2,1)S(1)}, bf16[256,768]{1,0:T(8,128)(2,1)S(1)}, u32[]{:S(2)}, u32[]{:S(2)}) collective-permute-start(bf16[256,768]{1,0:T(8,128)(2,1)S(1)} %pad_maximum_fusion), channel_id=1, source_target_pairs={{0,1},{1,0},{2,3},{3,2},{4,5},{5,4},{6,7},{7,6},{8,9},{9,8},{10,11... | collective-permute-start | bytes 1179656 | tf_op jit(solution)/shard_map/ppermute | solution.py:130
  22.4 25.3 %collective-permute-start.4 = (bf16[256,768]{1,0:T(8,128)(2,1)S(1)}, bf16[256,768]{1,0:T(8,128)(2,1)S(1)}, u32[]{:S(2)}, u32[]{:S(2)}) collective-permute-start(bf16[256,768]{1,0:T(8,128)(2,1)S(1)} %collective-permute-done.3), channel_id=1, source_target_pairs={{0,1},{1,0},{2,3},{3,2},{4,5},{5,4},{6,7},{7,6},{8,9},{9,8},{10,11... | collective-permute-start | bytes 1179656 | tf_op jit(solution)/shard_map/ppermute | solution.py:130
  24.3 23.5 %collective-permute-start.1 = (bf16[384,768]{1,0:T(8,128)(2,1)S(1)}, bf16[384,768]{1,0:T(8,128)(2,1)S(1)}, u32[]{:S(2)}, u32[]{:S(2)}) collective-permute-start(bf16[384,768]{1,0:T(8,128)(2,1)S(1)} %collective-permute-done.other_ref), channel_id=1, source_target_pairs={{0,2},{1,31},{2,4},{3,1},{4,6},{5,3},{6,8},{7,5},{8,10},{9,7},{10,... | collective-permute-start | bytes 1769480 | tf_op jit(solution)/shard_map/ppermute | solution.py:130
  31.7 22.7 %collective-permute-start.6 = (bf16[384,768]{1,0:T(8,128)(2,1)S(1)}, bf16[384,768]{1,0:T(8,128)(2,1)S(1)}, u32[]{:S(2)}, u32[]{:S(2)}) collective-permute-start(bf16[384,768]{1,0:T(8,128)(2,1)S(1)} %collective-permute-done.5.other_ref), channel_id=1, source_target_pairs={{0,2},{1,31},{2,4},{3,1},{4,6},{5,3},{6,8},{7,5},{8,10},{9,7},{10,... | collective-permute-start | bytes 1769480 | tf_op jit(solution)/shard_map/ppermute | solution.py:130

commit v2 on v1

v2 whole, which is shorter than its diff:
```python
import functools

import jax
import jax.numpy as jnp
from jax import lax
from jax.experimental import pallas as pl
from jax.experimental.pallas import tpu as pltpu
from jax.sharding import PartitionSpec as P

AXES = ("blk", "sub")
LAST = (((1,), (1,)), ((), ()))
FIRST = (((0,), (0,)), ((), ()))
VMEM_LIMIT = 24 * 1024 * 1024


def unit_rows(values_in):
    values = values_in.astype(jnp.float32)
    recip = lax.rsqrt(jnp.sum(values * values, axis=-1, keepdims=True) + 1e-06)
    return values * recip, recip


def dot32(left, right, dims):
    return lax.dot_general(left, right, dims, preferred_element_type=jnp.float32)


def band_term(own_low, other_low, scale, offset):
    weight = jax.nn.sigmoid(scale * dot32(own_low, other_low, LAST) + offset)
    return jnp.dot(
        weight.astype(jnp.bfloat16), other_low, preferred_element_type=jnp.float32
    )


def take_kernel(value_ref, out_ref, sem):
    copy = pltpu.make_async_copy(value_ref.at[pl.ds(0, out_ref.shape[0]), :], out_ref, sem)
    copy.start()
    copy.wait()


def own_kernel(scale_ref, offset_ref, img_ref, txt_ref, img_low, txt_low, sum_img, sum_txt):
    scale, offset = scale_ref[0], offset_ref[0]
    lower_rows((img_ref,), img_low)
    lower_rows((txt_ref,), txt_low)
    logits = scale * dot32(img_low[...], txt_low[...], LAST) + offset
    rows = lax.broadcasted_iota(jnp.int32, logits.shape, 0)
    columns = lax.broadcasted_iota(jnp.int32, logits.shape, 1)
    weight = jax.nn.sigmoid(logits) - (rows == columns).astype(jnp.float32)
    weight = weight.astype(jnp.bfloat16)
    sum_img[...] = jnp.dot(weight, txt_low[...], preferred_element_type=jnp.float32)
    sum_txt[...] = dot32(weight, img_low[...], FIRST)


def lower_rows(others, other_low):
    at = 0
    for other in others:
        rows = other.shape[0]
        other_low[at : at + rows, :] = unit_rows(other[...])[0].astype(jnp.bfloat16)
        at += rows


def add_kernel(count, scale_ref, offset_ref, low_ref, sum_in, *rest):
    others, (sum_out, other_low) = rest[:count], rest[count:]
    scale, offset = scale_ref[0], offset_ref[0]
    lower_rows(others, other_low)
    sum_out[...] = sum_in[...] + band_term(low_ref[...], other_low[...], scale, offset)


def last_kernel(count, blocks, scale_ref, offset_ref, raw_ref, low_ref, sum_ref, *rest):
    others, (out_ref, other_low, held, sems) = rest[:count], rest[count:]
    scale, offset = scale_ref[0], offset_ref[0]
    lower_rows(others, other_low)
    size = held.shape[0] // blocks
    copies = []
    for block in range(blocks):
        at = pl.ds(block * size, size)
        unit, recip = unit_rows(raw_ref[at, :])
        total = sum_ref[at, :] + band_term(low_ref[at, :], other_low[...], scale, offset)
        grad = scale * total
        along = jnp.sum(unit * grad, axis=-1, keepdims=True)
        held[at, :] = (grad - unit * along) * recip
        copy = pltpu.make_async_copy(held.at[at, :], out_ref.at[at, :], sems.at[block])
        copy.start()
        copies.append(copy)
    for copy in copies:
        copy.wait()


def cost(micros):
    return pl.CostEstimate(flops=int(micros * 1e9), bytes_accessed=1024, transcendentals=0)


SMEM = pl.BlockSpec(memory_space=pltpu.SMEM)
VMEM = pl.BlockSpec(memory_space=pltpu.VMEM)
PARAMS = pltpu.CompilerParams(vmem_limit_bytes=VMEM_LIMIT)


def take_call(value, count):
    return pl.pallas_call(
        take_kernel,
        out_shape=jax.ShapeDtypeStruct((count, value.shape[1]), value.dtype),
        in_specs=[pl.BlockSpec(memory_space=pl.ANY)],
        out_specs=VMEM,
        scratch_shapes=[pltpu.SemaphoreType.DMA],
        compiler_params=PARAMS,
        cost_estimate=cost(0.05),
    )(value)


def own_call(scale, offset, images, texts):
    rows, width = texts.shape
    low = jax.ShapeDtypeStruct((rows, width), jnp.bfloat16)
    total = jax.ShapeDtypeStruct((rows, width), jnp.float32)
    return pl.pallas_call(
        own_kernel,
        out_shape=(low, low, total, total),
        in_specs=[SMEM, SMEM, VMEM, VMEM],
        out_specs=(VMEM,) * 4,
        compiler_params=PARAMS,
        cost_estimate=cost(0.05),
    )(scale, offset, images, texts)


def add_call(scale, offset, low, total, others, micros):
    rows, width = low.shape
    count = sum(other.shape[0] for other in others)
    return pl.pallas_call(
        functools.partial(add_kernel, len(others)),
        out_shape=jax.ShapeDtypeStruct((rows, width), jnp.float32),
        in_specs=[SMEM, SMEM] + [VMEM] * (2 + len(others)),
        out_specs=VMEM,
        scratch_shapes=[pltpu.VMEM((count, width), jnp.bfloat16)],
        input_output_aliases={3: 0},
        compiler_params=PARAMS,
        cost_estimate=cost(micros),
    )(scale, offset, low, total, *others)


def last_call(scale, offset, raw, low, total, others, micros):
    rows, width = raw.shape
    count = sum(other.shape[0] for other in others)
    blocks = 2 if rows % 32 == 0 else 1
    return pl.pallas_call(
        functools.partial(last_kernel, len(others), blocks),
        out_shape=jax.ShapeDtypeStruct((rows, width), jnp.float32),
        in_specs=[SMEM, SMEM] + [VMEM] * (3 + len(others)),
        out_specs=pl.BlockSpec(memory_space=pl.ANY),
        scratch_shapes=[
            pltpu.VMEM((count, width), jnp.bfloat16),
            pltpu.VMEM((rows, width), jnp.float32),
            pltpu.SemaphoreType.DMA((blocks,)),
        ],
        compiler_params=PARAMS,
        cost_estimate=cost(micros),
    )(scale, offset, raw, low, total, *others)


def exchange(value, target):
    count = lax.axis_size(AXES)
    return lax.ppermute(value, AXES, [(at, target(at) % count) for at in range(count)])


def partner(at):
    return at ^ 1


def onward(at):
    return at + 2 if at % 2 == 0 else at - 2


def backward(at):
    return at - 2 if at % 2 == 0 else at + 2


def tied(value, *others):
    return lax.optimization_barrier((value, *others))[0]


def shards(images, texts, logit_scale, logit_bias):
    rows = images.shape[0]
    args = (logit_scale, logit_bias)

    def cut(value, start, stop):
        return value[rows * start // 32 : rows * stop // 32]

    tail = cut(images, 24, 32)
    near0 = exchange(take_call(texts, rows * 16 // 32), partner)
    near1 = exchange(cut(texts, 16, 32), partner)
    side = exchange(tail, backward)
    img_low, txt_low, sum_img, sum_txt = own_call(*args, images, texts)
    far0 = exchange(tied(near0, img_low, side), onward)
    near2 = exchange(tied(cut(images, 0, 13), near0), partner)
    sum_img = add_call(*args, img_low, sum_img, (near0,), 0.8)
    far1 = exchange(tied(near1, sum_img), onward)
    near3 = exchange(tied(cut(images, 13, 24), near1), partner)
    sum_img = add_call(*args, img_low, sum_img, (near1,), 0.8)
    far2 = exchange(tied(near2, sum_img, far0), onward)
    near_tail = exchange(tied(tail, near2), partner)
    sum_txt = add_call(*args, txt_low, sum_txt, (near2,), 0.8)
    far3 = exchange(tied(near3, sum_txt, far1), onward)
    far_tail = exchange(tied(side, near3), partner)
    sum_txt = add_call(*args, txt_low, sum_txt, (near3,), 0.3)
    grad_img = last_call(*args, images, img_low, sum_img, (far0, far1,), 0.05)
    sum_txt = add_call(*args, txt_low, tied(sum_txt, far2, grad_img), (far2, near_tail,), 1.0)
    grad_txt = last_call(*args, texts, txt_low, sum_txt, (far3, far_tail), 0.05)
    return grad_img, grad_txt


def solution(mesh):
    split = P(AXES, None)
    return jax.shard_map(
        shards,
        mesh=mesh,
        in_specs=(split, split, P(), P()),
        out_specs=(split, split),
        check_vma=False,
    )
```

time: 59.1 us -> 51.8 us (0.88)
  waiting for transfers between devices: 28.5 us -> 12 us
  starting transfers between devices: 13.4 us -> 23.9 us
  Pallas kernels: 13.6 us -> 12.5 us
    ppermute x7 -> x11, waiting for transfers between devices: 28.5 us -> 12 us  [exchange(): lax.ppermute(value, AXES, [(at, target(at) % count) for at in range(count)])]
    ppermute x7 -> x11, starting transfers between devices: 13.4 us -> 23.9 us  [exchange(): lax.ppermute(value, AXES, [(at, target(at) % count) for at in range(count)])]
    slice x8 -> x4, local copies, waits for them, and re-layouts: 1.3 us -> 0.08 us  [cut(): return value[rows * start // 32:rows * stop // 32]]
    pallas_call x5 -> x8, Pallas kernels: 11.9 us -> 10.7 us  [the longest x5 5.67 us: add_call(): pl.pallas_call(functools.partial(add_kernel, len(others)), out_shape=jax....]
    unnamed x4 -> x6, local copies, waits for them, and re-layouts: 0.01 us -> 1.13 us
  transfers between devices with their start and end apart: 7 -> 11, of which waited for: 5 -> 6; matrix products, arithmetic and copies ran while one was open for 0% -> 0% of each run, Pallas kernels for 16% -> 19%
where the time goes in v2:
time: 51.8 us; the launch traced here: 51.6 us
  starting transfers between devices  23.9 us (46%)
  Pallas kernels  12.5 us (24%)
  waiting for transfers between devices  12 us (23%)
  between operations  2.07 us (4%)
  local copies, waits for them, and re-layouts  1.21 us (2%)
    ppermute x11, starting transfers between devices, exchange(): lax.ppermute(value, AXES, [(at, target(at) % count) for at in range(count)])  23.9 us
    ppermute x11, waiting for transfers between devices, exchange(): lax.ppermute(value, AXES, [(at, target(at) % count) for at in range(count)])  12 us
    pallas_call x5, Pallas kernels, add_call(): pl.pallas_call(functools.partial(add_kernel, len(others)), out_shape=jax....  5.67 us
    pallas_call x2, Pallas kernels, last_call(): pl.pallas_call(functools.partial(last_kernel, len(others), blocks), out_s...  4.86 us
    pallas_call x1, Pallas kernels, own_call(): pl.pallas_call(own_kernel, out_shape=(low, low, total, total), in_specs=[...  1.74 us
    unnamed x6, local copies, waits for them, and re-layouts  1.13 us
  transfers between devices with their start and end apart: 11, of which 6 were waited for; matrix products, arithmetic and copies ran while one was open for 0% of the time, Pallas kernels for 19%

profile of v2, /device:TPU:0, one launch (start us, length us, event | category | flops | bytes accessed | tf_op | source)
XLA Modules:
  0.0 51.6 jit_solution(5843524491766747924)
XLA Ops:
  0.6 1.1 %copy-done = bf16[512,768]{1,0:T(8,128)(2,1)S(1)} copy-done((bf16[512,768]{1,0:T(8,128)(2,1)S(1)}, bf16[512,768]{1,0:T(8,128)(2,1)}, u32[]{:S(2)}) %copy-start) | copy-done | bytes 786456
  1.8 0.2 shard_map.60
  2.0 3.0 %collective-permute-start = (bf16[256,768]{1,0:T(8,128)(2,1)S(1)}, bf16[256,768]{1,0:T(8,128)(2,1)S(1)}, u32[]{:S(2)}, u32[]{:S(2)}) collective-permute-start(bf16[256,768]{1,0:T(8,128)(2,1)S(1)} %shard_map.60), channel_id=1, source_target_pairs={{0,1},{1,0},{2,3},{3,2},{4,5},{5,4},{6,7},{7,6},{8,9},{9,8},{10,11... | collective-permute-start | bytes 1179656 | tf_op jit(solution)/shard_map/ppermute | solution.py:158
  5.0 0.1 collective-permute-start.1
  5.1 3.9 %collective-permute-start.2 = (bf16[128,768]{1,0:T(8,128)(2,1)S(1)}, bf16[128,768]{1,0:T(8,128)(2,1)S(1)}, u32[]{:S(2)}, u32[]{:S(2)}) collective-permute-start(bf16[128,768]{1,0:T(8,128)(2,1)S(1)} %slice.13), channel_id=1, source_target_pairs={{0,30},{1,3},{2,0},{3,5},{4,2},{5,7},{6,4},{7,9},{8,6},{9,11},{10,... | collective-permute-start | bytes 589832 | tf_op jit(solution)/shard_map/ppermute | solution.py:158
  10.4 1.7 %shard_map.59 = (bf16[512,768]{1,0:T(8,128)(2,1)S(1)}, bf16[512,768]{1,0:T(8,128)(2,1)S(1)}, f32[512,768]{1,0:T(8,128)S(1)}, f32[512,768]{1,0:T(8,128)S(1)}) custom-call(f32[1]{0:T(128)S(6)} %copy.16.scale_ref, f32[1]{0:T(128)S(6)} %copy.17.offset_ref, bf16[512,768]{1,0:T(8,128)(2,1)S(1)} %copy-done.2, bf16[512,768]{1,0:T(8,128)(2,1)S(1)} %copy-done.1), custom_call_target="tpu_custom_call" | custom-call | flops 50000000 | bytes 1024 | tf_op jit(solution)/shard_map/pallas_call | solution.py:112
  12.1 1.9 %collective-permute-done.2 = bf16[128,768]{1,0:T(8,128)(2,1)S(1)} collective-permute-done((bf16[128,768]{1,0:T(8,128)(2,1)S(1)}, bf16[128,768]{1,0:T(8,128)(2,1)S(1)}, u32[]{:S(2)}, u32[]{:S(2)}) %collective-permute-start.2) | collective-permute-done | bytes 196640 | tf_op jit(solution)/shard_map/ppermute | solution.py:158
  14.0 0.9 %collective-permute-done.rest_0_ = bf16[256,768]{1,0:T(8,128)(2,1)S(1)} collective-permute-done((bf16[256,768]{1,0:T(8,128)(2,1)S(1)}, bf16[256,768]{1,0:T(8,128)(2,1)S(1)}, u32[]{:S(2)}, u32[]{:S(2)}) %collective-permute-start) | collective-permute-done | bytes 393248 | tf_op jit(solution)/shard_map/ppermute | solution.py:158
  14.9 2.1 %collective-permute-start.3 = (bf16[256,768]{1,0:T(8,128)(2,1)S(1)}, bf16[256,768]{1,0:T(8,128)(2,1)S(1)}, u32[]{:S(2)}, u32[]{:S(2)}) collective-permute-start(bf16[256,768]{1,0:T(8,128)(2,1)S(1)} %collective-permute-done.rest_0_), channel_id=1, source_target_pairs={{0,2},{1,31},{2,4},{3,1},{4,6},{5,3},{6,8},{7,5},{8,10},{9,7},{10,... | collective-permute-start | bytes 1179656 | tf_op jit(solution)/shard_map/ppermute | solution.py:158
  17.1 2.0 %collective-permute-start.5 = (bf16[208,768]{1,0:T(8,128)(2,1)S(1)}, bf16[208,768]{1,0:T(8,128)(2,1)S(1)}, u32[]{:S(2)}, u32[]{:S(2)}) collective-permute-start(bf16[208,768]{1,0:T(8,128)(2,1)S(1)} %slice.14), channel_id=1, source_target_pairs={{0,1},{1,0},{2,3},{3,2},{4,5},{5,4},{6,7},{7,6},{8,9},{9,8},{10,11... | collective-permute-start | bytes 958472 | tf_op jit(solution)/shard_map/ppermute | solution.py:158
  19.0 1.1 %shard_map.61.sum_in = f32[512,768]{1,0:T(8,128)S(1)} custom-call(f32[1]{0:T(128)S(6)} %copy.16.scale_ref, f32[1]{0:T(128)S(6)} %copy.17.offset_ref, bf16[512,768]{1,0:T(8,128)(2,1)S(1)} %get-tuple-element.15.low_ref, f32[512,768]{1,0:T(8,128)S(1)} %get-tuple-element.16.sum_in, ...), custom_call_target="tpu_custom_call", output_to_operand_aliasing={{}: (3, {})} | custom-call | flops 800000000 | bytes 1024 | tf_op jit(solution)/shard_map/pallas_call | solution.py:125
  20.2 3.2 %collective-permute-done.1.rest_0_ = bf16[256,768]{1,0:T(8,128)(2,1)S(1)} collective-permute-done((bf16[256,768]{1,0:T(8,128)(2,1)S(1)}, bf16[256,768]{1,0:T(8,128)(2,1)S(1)}, u32[]{:S(2)}, u32[]{:S(2)}) %collective-permute-start.1) | collective-permute-done | bytes 393248 | tf_op jit(solution)/shard_map/ppermute | solution.py:158
  23.4 2.1 %collective-permute-start.4 = (bf16[256,768]{1,0:T(8,128)(2,1)S(1)}, bf16[256,768]{1,0:T(8,128)(2,1)S(1)}, u32[]{:S(2)}, u32[]{:S(2)}) collective-permute-start(bf16[256,768]{1,0:T(8,128)(2,1)S(1)} %collective-permute-done.1.rest_0_), channel_id=1, source_target_pairs={{0,2},{1,31},{2,4},{3,1},{4,6},{5,3},{6,8},{7,5},{8,10},{9,7},{10,... | collective-permute-start | bytes 1179656 | tf_op jit(solution)/shard_map/ppermute | solution.py:158
  25.5 2.0 %collective-permute-start.6 = (bf16[176,768]{1,0:T(8,128)(2,1)S(1)}, bf16[176,768]{1,0:T(8,128)(2,1)S(1)}, u32[]{:S(2)}, u32[]{:S(2)}) collective-permute-start(bf16[176,768]{1,0:T(8,128)(2,1)S(1)} %slice.15), channel_id=1, source_target_pairs={{0,1},{1,0},{2,3},{3,2},{4,5},{5,4},{6,7},{7,6},{8,9},{9,8},{10,11... | collective-permute-start | bytes 811016 | tf_op jit(solution)/shard_map/ppermute | solution.py:158
  27.5 1.1 %shard_map.62.sum_ref = f32[512,768]{1,0:T(8,128)S(1)} custom-call(f32[1]{0:T(128)S(6)} %copy.16.scale_ref, f32[1]{0:T(128)S(6)} %copy.17.offset_ref, bf16[512,768]{1,0:T(8,128)(2,1)S(1)} %get-tuple-element.15.low_ref, f32[512,768]{1,0:T(8,128)S(1)} %shard_map.61.sum_in, ...), custom_call_target="tpu_custom_call", output_to_operand_aliasing={{}: (3, {})} | custom-call | flops 800000000 | bytes 1024 | tf_op jit(solution)/shard_map/pallas_call | solution.py:125
  28.6 0.8 %collective-permute-done.5.rest_0_ = bf16[208,768]{1,0:T(8,128)(2,1)S(1)} collective-permute-done((bf16[208,768]{1,0:T(8,128)(2,1)S(1)}, bf16[208,768]{1,0:T(8,128)(2,1)S(1)}, u32[]{:S(2)}, u32[]{:S(2)}) %collective-permute-start.5) | collective-permute-done | bytes 319520 | tf_op jit(solution)/shard_map/ppermute | solution.py:158
  29.4 0.0 collective-permute-done.3.rest_0_
  29.4 2.9 %collective-permute-start.7 = (bf16[208,768]{1,0:T(8,128)(2,1)S(1)}, bf16[208,768]{1,0:T(8,128)(2,1)S(1)}, u32[]{:S(2)}, u32[]{:S(2)}) collective-permute-start(bf16[208,768]{1,0:T(8,128)(2,1)S(1)} %collective-permute-done.5.rest_0_), channel_id=1, source_target_pairs={{0,2},{1,31},{2,4},{3,1},{4,6},{5,3},{6,8},{7,5},{8,10},{9,7},{10,... | collective-permute-start | bytes 958472 | tf_op jit(solution)/shard_map/ppermute | solution.py:158
  32.3 1.9 %collective-permute-start.8 = (bf16[128,768]{1,0:T(8,128)(2,1)S(1)}, bf16[128,768]{1,0:T(8,128)(2,1)S(1)}, u32[]{:S(2)}, u32[]{:S(2)}) collective-permute-start(bf16[128,768]{1,0:T(8,128)(2,1)S(1)} %slice.13), channel_id=1, source_target_pairs={{0,1},{1,0},{2,3},{3,2},{4,5},{5,4},{6,7},{7,6},{8,9},{9,8},{10,11... | collective-permute-start | bytes 589832 | tf_op jit(solution)/shard_map/ppermute | solution.py:158
  34.2 1.1 %shard_map.64.sum_in = f32[512,768]{1,0:T(8,128)S(1)} custom-call(f32[1]{0:T(128)S(6)} %copy.16.scale_ref, f32[1]{0:T(128)S(6)} %copy.17.offset_ref, bf16[512,768]{1,0:T(8,128)(2,1)S(1)} %get-tuple-element.19.low_ref, f32[512,768]{1,0:T(8,128)S(1)} %get-tuple-element.20.sum_in, ...), custom_call_target="tpu_custom_call", output_to_operand_aliasing={{}: (3, {})} | custom-call | flops 800000000 | bytes 1024 | tf_op jit(solution)/shard_map/pallas_call | solution.py:125
  35.3 0.0 collective-permute-done.6.rest_0_
  35.3 1.2 %collective-permute-done.4.rest_1_ = bf16[256,768]{1,0:T(8,128)(2,1)S(1)} collective-permute-done((bf16[256,768]{1,0:T(8,128)(2,1)S(1)}, bf16[256,768]{1,0:T(8,128)(2,1)S(1)}, u32[]{:S(2)}, u32[]{:S(2)}) %collective-permute-start.4) | collective-permute-done | bytes 393248 | tf_op jit(solution)/shard_map/ppermute | solution.py:158
  36.6 1.6 %collective-permute-start.9 = (bf16[176,768]{1,0:T(8,128)(2,1)S(1)}, bf16[176,768]{1,0:T(8,128)(2,1)S(1)}, u32[]{:S(2)}, u32[]{:S(2)}) collective-permute-start(bf16[176,768]{1,0:T(8,128)(2,1)S(1)} %collective-permute-done.6.rest_0_), channel_id=1, source_target_pairs={{0,2},{1,31},{2,4},{3,1},{4,6},{5,3},{6,8},{7,5},{8,10},{9,7},{10,... | collective-permute-start | bytes 811016 | tf_op jit(solution)/shard_map/ppermute | solution.py:158
  38.1 2.3 %collective-permute-start.10 = (bf16[128,768]{1,0:T(8,128)(2,1)S(1)}, bf16[128,768]{1,0:T(8,128)(2,1)S(1)}, u32[]{:S(2)}, u32[]{:S(2)}) collective-permute-start(bf16[128,768]{1,0:T(8,128)(2,1)S(1)} %collective-permute-done.2), channel_id=1, source_target_pairs={{0,1},{1,0},{2,3},{3,2},{4,5},{5,4},{6,7},{7,6},{8,9},{9,8},{10,11... | collective-permute-start | bytes 589832 | tf_op jit(solution)/shard_map/ppermute | solution.py:158
  40.4 2.4 %shard_map.63 = f32[512,768]{1,0:T(8,128)} custom-call(f32[1]{0:T(128)S(6)} %copy.16.scale_ref, f32[1]{0:T(128)S(6)} %copy.17.offset_ref, bf16[512,768]{1,0:T(8,128)(2,1)S(1)} %copy-done.2, bf16[512,768]{1,0:T(8,128)(2,1)S(1)} %get-tuple-element.15.low_ref, f32[512,768]{1,0:T(8,128)S(1)} %shard_map.62.sum_ref, ...), custom_call_target="tpu_custom_call" | custom-call | flops 50000000 | bytes 1024 | tf_op jit(solution)/shard_map/pallas_call | solution.py:141
  42.9 1.1 %shard_map.65.sum_in = f32[512,768]{1,0:T(8,128)S(1)} custom-call(f32[1]{0:T(128)S(6)} %copy.16.scale_ref, f32[1]{0:T(128)S(6)} %copy.17.offset_ref, bf16[512,768]{1,0:T(8,128)(2,1)S(1)} %get-tuple-element.19.low_ref, f32[512,768]{1,0:T(8,128)S(1)} %shard_map.64.sum_in, ...), custom_call_target="tpu_custom_call", output_to_operand_aliasing={{}: (3, {})} | custom-call | flops 300000000 | bytes 1024 | tf_op jit(solution)/shard_map/pallas_call | solution.py:125
  43.9 0.0 collective-permute-done.7.rest_0_
  43.9 0.0 collective-permute-done.8.rest_1_
  44.0 1.3 %shard_map.66.sum_ref = f32[512,768]{1,0:T(8,128)S(1)} custom-call(f32[1]{0:T(128)S(6)} %copy.16.scale_ref, f32[1]{0:T(128)S(6)} %copy.17.offset_ref, bf16[512,768]{1,0:T(8,128)(2,1)S(1)} %get-tuple-element.19.low_ref, f32[512,768]{1,0:T(8,128)S(1)} %shard_map.65.sum_in, ...), custom_call_target="tpu_custom_call", output_to_operand_aliasing={{}: (3, {})} | custom-call | flops 1000000000 | bytes 1024 | tf_op jit(solution)/shard_map/pallas_call | solution.py:125
  45.3 0.0 collective-permute-done.10.rest_1_
  45.3 3.9 %collective-permute-done.9.rest_0_ = bf16[176,768]{1,0:T(8,128)(2,1)S(1)} collective-permute-done((bf16[176,768]{1,0:T(8,128)(2,1)S(1)}, bf16[176,768]{1,0:T(8,128)(2,1)S(1)}, u32[]{:S(2)}, u32[]{:S(2)}) %collective-permute-start.9) | collective-permute-done | bytes 270368 | tf_op jit(solution)/shard_map/ppermute | solution.py:158
  49.2 2.4 %shard_map.67 = f32[512,768]{1,0:T(8,128)} custom-call(f32[1]{0:T(128)S(6)} %copy.16.scale_ref, f32[1]{0:T(128)S(6)} %copy.17.offset_ref, bf16[512,768]{1,0:T(8,128)(2,1)S(1)} %copy-done.1, bf16[512,768]{1,0:T(8,128)(2,1)S(1)} %get-tuple-element.19.low_ref, f32[512,768]{1,0:T(8,128)S(1)} %shard_map.66.sum_ref, ...), custom_call_target="tpu_custom_call" | custom-call | flops 50000000 | bytes 1024 | tf_op jit(solution)/shard_map/pallas_call | solution.py:141
  (9 shorter events, 0.1 us)
Async XLA Ops:
  0.6 1.1 %copy-start = (bf16[512,768]{1,0:T(8,128)(2,1)S(1)}, bf16[512,768]{1,0:T(8,128)(2,1)}, u32[]{:S(2)}) copy-start(bf16[512,768]{1,0:T(8,128)(2,1)} %raw_ref.3) | copy-start | bytes 2359300
  1.8 3.4 %copy-start.2 = (bf16[512,768]{1,0:T(8,128)(2,1)S(1)}, bf16[512,768]{1,0:T(8,128)(2,1)}, u32[]{:S(2)}) copy-start(bf16[512,768]{1,0:T(8,128)(2,1)} %raw_ref.2) | copy-start | bytes 2359300
  1.8 8.6 %copy-start.1 = (bf16[512,768]{1,0:T(8,128)(2,1)S(1)}, bf16[512,768]{1,0:T(8,128)(2,1)}, u32[]{:S(2)}) copy-start(bf16[512,768]{1,0:T(8,128)(2,1)} %raw_ref.3) | copy-start | bytes 2359300
  2.0 13.0 %collective-permute-start = (bf16[256,768]{1,0:T(8,128)(2,1)S(1)}, bf16[256,768]{1,0:T(8,128)(2,1)S(1)}, u32[]{:S(2)}, u32[]{:S(2)}) collective-permute-start(bf16[256,768]{1,0:T(8,128)(2,1)S(1)} %shard_map.60), channel_id=1, source_target_pairs={{0,1},{1,0},{2,3},{3,2},{4,5},{5,4},{6,7},{7,6},{8,9},{9,8},{10,11... | collective-permute-start | bytes 1179656 | tf_op jit(solution)/shard_map/ppermute | solution.py:158
  5.0 18.3 %collective-permute-start.1 = (bf16[256,768]{1,0:T(8,128)(2,1)S(1)}, bf16[256,768]{1,0:T(8,128)(2,1)S(1)}, u32[]{:S(2)}, u32[]{:S(2)}) collective-permute-start(bf16[256,768]{1,0:T(8,128)(2,1)S(1)} %slice.12), channel_id=1, source_target_pairs={{0,1},{1,0},{2,3},{3,2},{4,5},{5,4},{6,7},{7,6},{8,9},{9,8},{10,11... | collective-permute-start | bytes 1179656 | tf_op jit(solution)/shard_map/ppermute | solution.py:158
  5.1 8.9 %collective-permute-start.2 = (bf16[128,768]{1,0:T(8,128)(2,1)S(1)}, bf16[128,768]{1,0:T(8,128)(2,1)S(1)}, u32[]{:S(2)}, u32[]{:S(2)}) collective-permute-start(bf16[128,768]{1,0:T(8,128)(2,1)S(1)} %slice.13), channel_id=1, source_target_pairs={{0,30},{1,3},{2,0},{3,5},{4,2},{5,7},{6,4},{7,9},{8,6},{9,11},{10,... | collective-permute-start | bytes 589832 | tf_op jit(solution)/shard_map/ppermute | solution.py:158
  14.9 14.4 %collective-permute-start.3 = (bf16[256,768]{1,0:T(8,128)(2,1)S(1)}, bf16[256,768]{1,0:T(8,128)(2,1)S(1)}, u32[]{:S(2)}, u32[]{:S(2)}) collective-permute-start(bf16[256,768]{1,0:T(8,128)(2,1)S(1)} %collective-permute-done.rest_0_), channel_id=1, source_target_pairs={{0,2},{1,31},{2,4},{3,1},{4,6},{5,3},{6,8},{7,5},{8,10},{9,7},{10,... | collective-permute-start | bytes 1179656 | tf_op jit(solution)/shard_map/ppermute | solution.py:158
  17.1 12.3 %collective-permute-start.5 = (bf16[208,768]{1,0:T(8,128)(2,1)S(1)}, bf16[208,768]{1,0:T(8,128)(2,1)S(1)}, u32[]{:S(2)}, u32[]{:S(2)}) collective-permute-start(bf16[208,768]{1,0:T(8,128)(2,1)S(1)} %slice.14), channel_id=1, source_target_pairs={{0,1},{1,0},{2,3},{3,2},{4,5},{5,4},{6,7},{7,6},{8,9},{9,8},{10,11... | collective-permute-start | bytes 958472 | tf_op jit(solution)/shard_map/ppermute | solution.py:158
  23.4 13.2 %collective-permute-start.4 = (bf16[256,768]{1,0:T(8,128)(2,1)S(1)}, bf16[256,768]{1,0:T(8,128)(2,1)S(1)}, u32[]{:S(2)}, u32[]{:S(2)}) collective-permute-start(bf16[256,768]{1,0:T(8,128)(2,1)S(1)} %collective-permute-done.1.rest_0_), channel_id=1, source_target_pairs={{0,2},{1,31},{2,4},{3,1},{4,6},{5,3},{6,8},{7,5},{8,10},{9,7},{10,... | collective-permute-start | bytes 1179656 | tf_op jit(solution)/shard_map/ppermute | solution.py:158
  25.5 9.8 %collective-permute-start.6 = (bf16[176,768]{1,0:T(8,128)(2,1)S(1)}, bf16[176,768]{1,0:T(8,128)(2,1)S(1)}, u32[]{:S(2)}, u32[]{:S(2)}) collective-permute-start(bf16[176,768]{1,0:T(8,128)(2,1)S(1)} %slice.15), channel_id=1, source_target_pairs={{0,1},{1,0},{2,3},{3,2},{4,5},{5,4},{6,7},{7,6},{8,9},{9,8},{10,11... | collective-permute-start | bytes 811016 | tf_op jit(solution)/shard_map/ppermute | solution.py:158
  29.4 14.6 %collective-permute-start.7 = (bf16[208,768]{1,0:T(8,128)(2,1)S(1)}, bf16[208,768]{1,0:T(8,128)(2,1)S(1)}, u32[]{:S(2)}, u32[]{:S(2)}) collective-permute-start(bf16[208,768]{1,0:T(8,128)(2,1)S(1)} %collective-permute-done.5.rest_0_), channel_id=1, source_target_pairs={{0,2},{1,31},{2,4},{3,1},{4,6},{5,3},{6,8},{7,5},{8,10},{9,7},{10,... | collective-permute-start | bytes 958472 | tf_op jit(solution)/shard_map/ppermute | solution.py:158
  32.3 11.6 %collective-permute-start.8 = (bf16[128,768]{1,0:T(8,128)(2,1)S(1)}, bf16[128,768]{1,0:T(8,128)(2,1)S(1)}, u32[]{:S(2)}, u32[]{:S(2)}) collective-permute-start(bf16[128,768]{1,0:T(8,128)(2,1)S(1)} %slice.13), channel_id=1, source_target_pairs={{0,1},{1,0},{2,3},{3,2},{4,5},{5,4},{6,7},{7,6},{8,9},{9,8},{10,11... | collective-permute-start | bytes 589832 | tf_op jit(solution)/shard_map/ppermute | solution.py:158
  36.6 12.6 %collective-permute-start.9 = (bf16[176,768]{1,0:T(8,128)(2,1)S(1)}, bf16[176,768]{1,0:T(8,128)(2,1)S(1)}, u32[]{:S(2)}, u32[]{:S(2)}) collective-permute-start(bf16[176,768]{1,0:T(8,128)(2,1)S(1)} %collective-permute-done.6.rest_0_), channel_id=1, source_target_pairs={{0,2},{1,31},{2,4},{3,1},{4,6},{5,3},{6,8},{7,5},{8,10},{9,7},{10,... | collective-permute-start | bytes 811016 | tf_op jit(solution)/shard_map/ppermute | solution.py:158
  38.1 7.1 %collective-permute-start.10 = (bf16[128,768]{1,0:T(8,128)(2,1)S(1)}, bf16[128,768]{1,0:T(8,128)(2,1)S(1)}, u32[]{:S(2)}, u32[]{:S(2)}) collective-permute-start(bf16[128,768]{1,0:T(8,128)(2,1)S(1)} %collective-permute-done.2), channel_id=1, source_target_pairs={{0,1},{1,0},{2,3},{3,2},{4,5},{5,4},{6,7},{7,6},{8,9},{9,8},{10,11... | collective-permute-start | bytes 589832 | tf_op jit(solution)/shard_map/ppermute | solution.py:158

commit v3 on v2

--- a/solution.py
+++ b/solution.py
@@ -68,13 +68,18 @@
     others, (out_ref, other_low, held, sems) = rest[:count], rest[count:]
     scale, offset = scale_ref[0], offset_ref[0]
     lower_rows(others, other_low)
+    logits = scale * dot32(low_ref[...], other_low[...], LAST) + offset
+    weight = jax.nn.sigmoid(logits).astype(jnp.bfloat16)
     size = held.shape[0] // blocks
     copies = []
     for block in range(blocks):
-        at = pl.ds(block * size, size)
+        start = block * size
+        at = pl.ds(start, size)
         unit, recip = unit_rows(raw_ref[at, :])
-        total = sum_ref[at, :] + band_term(low_ref[at, :], other_low[...], scale, offset)
-        grad = scale * total
+        term = jnp.dot(
+            weight[start : start + size], other_low[...], preferred_element_type=jnp.float32
+        )
+        grad = scale * (sum_ref[at, :] + term)
         along = jnp.sum(unit * grad, axis=-1, keepdims=True)
         held[at, :] = (grad - unit * along) * recip
         copy = pltpu.make_async_copy(held.at[at, :], out_ref.at[at, :], sems.at[block])
@@ -101,7 +106,7 @@
         out_specs=VMEM,
         scratch_shapes=[pltpu.SemaphoreType.DMA],
         compiler_params=PARAMS,
-        cost_estimate=cost(0.05),
+        cost_estimate=cost(0.8),
     )(value)
 
 
@@ -115,7 +120,7 @@
         in_specs=[SMEM, SMEM, VMEM, VMEM],
         out_specs=(VMEM,) * 4,
         compiler_params=PARAMS,
-        cost_estimate=cost(0.05),
+        cost_estimate=cost(0.8),
     )(scale, offset, images, texts)
 
 
@@ -137,7 +142,7 @@
 def last_call(scale, offset, raw, low, total, others, micros):
     rows, width = raw.shape
     count = sum(other.shape[0] for other in others)
-    blocks = 2 if rows % 32 == 0 else 1
+    blocks = 4 if rows % 64 == 0 else 1
     return pl.pallas_call(
         functools.partial(last_kernel, len(others), blocks),
         out_shape=jax.ShapeDtypeStruct((rows, width), jnp.float32),
@@ -181,26 +186,28 @@
     def cut(value, start, stop):
         return value[rows * start // 32 : rows * stop // 32]
 
-    tail = cut(images, 24, 32)
-    near0 = exchange(take_call(texts, rows * 16 // 32), partner)
-    near1 = exchange(cut(texts, 16, 32), partner)
+    tail = cut(images, 21, 32)
+    lead = take_call(texts, rows * 16 // 32)
+    near0 = exchange(lead, partner)
+    near1 = exchange(tied(cut(texts, 16, 32), lead), partner)
     side = exchange(tail, backward)
     img_low, txt_low, sum_img, sum_txt = own_call(*args, images, texts)
-    far0 = exchange(tied(near0, img_low, side), onward)
-    near2 = exchange(tied(cut(images, 0, 13), near0), partner)
-    sum_img = add_call(*args, img_low, sum_img, (near0,), 0.8)
+    far0 = exchange(tied(near0, img_low), onward)
+    near2 = exchange(tied(cut(images, 0, 11), near0), partner)
+    sum_img = add_call(*args, img_low, tied(sum_img, side), (near0,), 0.8)
     far1 = exchange(tied(near1, sum_img), onward)
-    near3 = exchange(tied(cut(images, 13, 24), near1), partner)
+    near3 = exchange(tied(cut(images, 11, 21), near1), partner)
     sum_img = add_call(*args, img_low, sum_img, (near1,), 0.8)
     far2 = exchange(tied(near2, sum_img, far0), onward)
     near_tail = exchange(tied(tail, near2), partner)
+    far_tail = exchange(tied(side, near2), partner)
     sum_txt = add_call(*args, txt_low, sum_txt, (near2,), 0.8)
     far3 = exchange(tied(near3, sum_txt, far1), onward)
-    far_tail = exchange(tied(side, near3), partner)
-    sum_txt = add_call(*args, txt_low, sum_txt, (near3,), 0.3)
     grad_img = last_call(*args, images, img_low, sum_img, (far0, far1,), 0.05)
-    sum_txt = add_call(*args, txt_low, tied(sum_txt, far2, grad_img), (far2, near_tail,), 1.0)
-    grad_txt = last_call(*args, texts, txt_low, sum_txt, (far3, far_tail), 0.05)
+    sum_txt = add_call(*args, txt_low, tied(sum_txt, grad_img), (near3, far2,), 0.8)
+    sum_txt = add_call(*args, txt_low, sum_txt, (near_tail,), 1.0)
+    sum_txt = add_call(*args, txt_low, sum_txt, (far_tail,), 0.05)
+    grad_txt = last_call(*args, texts, txt_low, sum_txt, (far3,), 0.05)
     return grad_img, grad_txt
 
 

time: 51.8 us -> 50 us (0.965)
  starting transfers between devices: 23.9 us -> 20.1 us
  waiting for transfers between devices: 12 us -> 13.2 us
  Pallas kernels: 12.5 us -> 13.2 us
    ppermute x11, starting transfers between devices: 23.9 us -> 20.1 us  [exchange(): lax.ppermute(value, AXES, [(at, target(at) % count) for at in range(count)])]
    ppermute x11, waiting for transfers between devices: 12 us -> 13.2 us  [exchange(): lax.ppermute(value, AXES, [(at, target(at) % count) for at in range(count)])]
    pallas_call x5 -> x6, Pallas kernels: 5.67 us -> 6.74 us  [add_call(): pl.pallas_call(functools.partial(add_kernel, len(others)), out_shape=jax....]
    unnamed x6 -> x4, local copies, waits for them, and re-layouts: 1.13 us -> 1.2 us
  transfers between devices with their start and end apart: 11 -> 11, of which waited for: 6 -> 6; matrix products, arithmetic and copies ran while one was open for 0% -> 0% of each run, Pallas kernels for 19% -> 22%
where the time goes in v3:
time: 50 us; the launch traced here: 49.8 us
  starting transfers between devices  20.1 us (40%)
  Pallas kernels  13.2 us (26%)
  waiting for transfers between devices  13.2 us (26%)
  between operations  2.07 us (4%)
  local copies, waits for them, and re-layouts  1.28 us (3%)
    ppermute x11, starting transfers between devices, exchange(): lax.ppermute(value, AXES, [(at, target(at) % count) for at in range(count)])  20.1 us
    ppermute x11, waiting for transfers between devices, exchange(): lax.ppermute(value, AXES, [(at, target(at) % count) for at in range(count)])  13.2 us
    pallas_call x6, Pallas kernels, add_call(): pl.pallas_call(functools.partial(add_kernel, len(others)), out_shape=jax....  6.74 us
    pallas_call x2, Pallas kernels, last_call(): pl.pallas_call(functools.partial(last_kernel, len(others), blocks), out_s...  4.54 us
    pallas_call x1, Pallas kernels, own_call(): pl.pallas_call(own_kernel, out_shape=(low, low, total, total), in_specs=[...  1.74 us
    unnamed x4, local copies, waits for them, and re-layouts  1.2 us
  transfers between devices with their start and end apart: 11, of which 6 were waited for; matrix products, arithmetic and copies ran while one was open for 0% of the time, Pallas kernels for 22%

profile of v3, /device:TPU:0, one launch (start us, length us, event | category | flops | bytes accessed | tf_op | source)
XLA Modules:
  0.0 49.8 jit_solution(2323104587878901063)
XLA Ops:
  0.6 1.2 %copy-done.1 = bf16[512,768]{1,0:T(8,128)(2,1)S(1)} copy-done((bf16[512,768]{1,0:T(8,128)(2,1)S(1)}, bf16[512,768]{1,0:T(8,128)(2,1)}, u32[]{:S(2)}) %copy-start.1) | copy-done | bytes 786456
  1.8 0.2 shard_map.60
  2.0 3.0 %collective-permute-start.1 = (bf16[256,768]{1,0:T(8,128)(2,1)S(1)}, bf16[256,768]{1,0:T(8,128)(2,1)S(1)}, u32[]{:S(2)}, u32[]{:S(2)}) collective-permute-start(bf16[256,768]{1,0:T(8,128)(2,1)S(1)} %shard_map.60), channel_id=1, source_target_pairs={{0,1},{1,0},{2,3},{3,2},{4,5},{5,4},{6,7},{7,6},{8,9},{9,8},{10,11... | collective-permute-start | bytes 1179656 | tf_op jit(solution)/shard_map/ppermute | solution.py:163
  5.1 0.1 collective-permute-start.2
  5.2 3.9 %collective-permute-start = (bf16[176,768]{1,0:T(8,128)(2,1)S(1)}, bf16[176,768]{1,0:T(8,128)(2,1)S(1)}, u32[]{:S(2)}, u32[]{:S(2)}) collective-permute-start(bf16[176,768]{1,0:T(8,128)(2,1)S(1)} %get-tuple-element.29), channel_id=1, source_target_pairs={{0,30},{1,3},{2,0},{3,5},{4,2},{5,7},{6,4},{7,9},{8,6},{9,11},{10,... | collective-permute-start | bytes 811016 | tf_op jit(solution)/shard_map/ppermute | solution.py:163
  10.5 1.7 %shard_map.59 = (bf16[512,768]{1,0:T(8,128)(2,1)S(1)}, bf16[512,768]{1,0:T(8,128)(2,1)S(1)}, f32[512,768]{1,0:T(8,128)S(1)}, f32[512,768]{1,0:T(8,128)S(1)}) custom-call(f32[1]{0:T(128)S(6)} %copy.18.scale_ref, f32[1]{0:T(128)S(6)} %copy.19.offset_ref, bf16[512,768]{1,0:T(8,128)(2,1)S(1)} %copy-done, bf16[512,768]{1,0:T(8,128)(2,1)S(1)} %copy-done.1), custom_call_target="tpu_custom_call" | custom-call | flops 800000000 | bytes 1024 | tf_op jit(solution)/shard_map/pallas_call | solution.py:117
  12.2 2.8 %collective-permute-done.1.rest_0_ = bf16[256,768]{1,0:T(8,128)(2,1)S(1)} collective-permute-done((bf16[256,768]{1,0:T(8,128)(2,1)S(1)}, bf16[256,768]{1,0:T(8,128)(2,1)S(1)}, u32[]{:S(2)}, u32[]{:S(2)}) %collective-permute-start.1) | collective-permute-done | bytes 393248 | tf_op jit(solution)/shard_map/ppermute | solution.py:163
  15.0 2.1 %collective-permute-start.3 = (bf16[256,768]{1,0:T(8,128)(2,1)S(1)}, bf16[256,768]{1,0:T(8,128)(2,1)S(1)}, u32[]{:S(2)}, u32[]{:S(2)}) collective-permute-start(bf16[256,768]{1,0:T(8,128)(2,1)S(1)} %collective-permute-done.1.rest_0_), channel_id=1, source_target_pairs={{0,2},{1,31},{2,4},{3,1},{4,6},{5,3},{6,8},{7,5},{8,10},{9,7},{10,... | collective-permute-start | bytes 1179656 | tf_op jit(solution)/shard_map/ppermute | solution.py:163
  17.1 1.9 %collective-permute-start.5 = (bf16[176,768]{1,0:T(8,128)(2,1)S(1)}, bf16[176,768]{1,0:T(8,128)(2,1)S(1)}, u32[]{:S(2)}, u32[]{:S(2)}) collective-permute-start(bf16[176,768]{1,0:T(8,128)(2,1)S(1)} %get-tuple-element.25), channel_id=1, source_target_pairs={{0,1},{1,0},{2,3},{3,2},{4,5},{5,4},{6,7},{7,6},{8,9},{9,8},{10,11... | collective-permute-start | bytes 811016 | tf_op jit(solution)/shard_map/ppermute | solution.py:163
  19.0 0.0 collective-permute-done
  19.0 1.1 %shard_map.61.sum_in = f32[512,768]{1,0:T(8,128)S(1)} custom-call(f32[1]{0:T(128)S(6)} %copy.18.scale_ref, f32[1]{0:T(128)S(6)} %copy.19.offset_ref, bf16[512,768]{1,0:T(8,128)(2,1)S(1)} %get-tuple-element.17.low_ref, f32[512,768]{1,0:T(8,128)S(1)} %get-tuple-element.19.sum_in, ...), custom_call_target="tpu_custom_call", output_to_operand_aliasing={{}: (3, {})} | custom-call | flops 800000000 | bytes 1024 | tf_op jit(solution)/shard_map/pallas_call | solution.py:130
  20.1 3.3 %collective-permute-done.2.rest_0_ = bf16[256,768]{1,0:T(8,128)(2,1)S(1)} collective-permute-done((bf16[256,768]{1,0:T(8,128)(2,1)S(1)}, bf16[256,768]{1,0:T(8,128)(2,1)S(1)}, u32[]{:S(2)}, u32[]{:S(2)}) %collective-permute-start.2) | collective-permute-done | bytes 393248 | tf_op jit(solution)/shard_map/ppermute | solution.py:163
  23.4 2.1 %collective-permute-start.4 = (bf16[256,768]{1,0:T(8,128)(2,1)S(1)}, bf16[256,768]{1,0:T(8,128)(2,1)S(1)}, u32[]{:S(2)}, u32[]{:S(2)}) collective-permute-start(bf16[256,768]{1,0:T(8,128)(2,1)S(1)} %collective-permute-done.2.rest_0_), channel_id=1, source_target_pairs={{0,2},{1,31},{2,4},{3,1},{4,6},{5,3},{6,8},{7,5},{8,10},{9,7},{10,... | collective-permute-start | bytes 1179656 | tf_op jit(solution)/shard_map/ppermute | solution.py:163
  25.6 2.0 %collective-permute-start.6 = (bf16[160,768]{1,0:T(8,128)(2,1)S(1)}, bf16[160,768]{1,0:T(8,128)(2,1)S(1)}, u32[]{:S(2)}, u32[]{:S(2)}) collective-permute-start(bf16[160,768]{1,0:T(8,128)(2,1)S(1)} %slice.15), channel_id=1, source_target_pairs={{0,1},{1,0},{2,3},{3,2},{4,5},{5,4},{6,7},{7,6},{8,9},{9,8},{10,11... | collective-permute-start | bytes 737288 | tf_op jit(solution)/shard_map/ppermute | solution.py:163
  27.5 1.1 %shard_map.62.sum_ref = f32[512,768]{1,0:T(8,128)S(1)} custom-call(f32[1]{0:T(128)S(6)} %copy.18.scale_ref, f32[1]{0:T(128)S(6)} %copy.19.offset_ref, bf16[512,768]{1,0:T(8,128)(2,1)S(1)} %get-tuple-element.17.low_ref, f32[512,768]{1,0:T(8,128)S(1)} %shard_map.61.sum_in, ...), custom_call_target="tpu_custom_call", output_to_operand_aliasing={{}: (3, {})} | custom-call | flops 800000000 | bytes 1024 | tf_op jit(solution)/shard_map/pallas_call | solution.py:130
  28.7 0.0 collective-permute-done.3.rest_0_
  28.7 2.7 %collective-permute-start.7 = (bf16[176,768]{1,0:T(8,128)(2,1)S(1)}, bf16[176,768]{1,0:T(8,128)(2,1)S(1)}, u32[]{:S(2)}, u32[]{:S(2)}) collective-permute-start(bf16[176,768]{1,0:T(8,128)(2,1)S(1)} %collective-permute-done.5.rest_0_), channel_id=1, source_target_pairs={{0,2},{1,31},{2,4},{3,1},{4,6},{5,3},{6,8},{7,5},{8,10},{9,7},{10,... | collective-permute-start | bytes 811016 | tf_op jit(solution)/shard_map/ppermute | solution.py:163
  31.4 1.9 %collective-permute-start.8 = (bf16[176,768]{1,0:T(8,128)(2,1)S(1)}, bf16[176,768]{1,0:T(8,128)(2,1)S(1)}, u32[]{:S(2)}, u32[]{:S(2)}) collective-permute-start(bf16[176,768]{1,0:T(8,128)(2,1)S(1)} %get-tuple-element.29), channel_id=1, source_target_pairs={{0,1},{1,0},{2,3},{3,2},{4,5},{5,4},{6,7},{7,6},{8,9},{9,8},{10,11... | collective-permute-start | bytes 811016 | tf_op jit(solution)/shard_map/ppermute | solution.py:163
  33.3 0.1 collective-permute-start.9
  33.4 1.1 %shard_map.64.sum_in = f32[512,768]{1,0:T(8,128)S(1)} custom-call(f32[1]{0:T(128)S(6)} %copy.18.scale_ref, f32[1]{0:T(128)S(6)} %copy.19.offset_ref, bf16[512,768]{1,0:T(8,128)(2,1)S(1)} %get-tuple-element.23.low_ref, f32[512,768]{1,0:T(8,128)S(1)} %get-tuple-element.24.sum_in, ...), custom_call_target="tpu_custom_call", output_to_operand_aliasing={{}: (3, {})} | custom-call | flops 800000000 | bytes 1024 | tf_op jit(solution)/shard_map/pallas_call | solution.py:130
  34.5 0.0 collective-permute-done.6.rest_0_
  34.5 2.2 %collective-permute-done.4.rest_1_ = bf16[256,768]{1,0:T(8,128)(2,1)S(1)} collective-permute-done((bf16[256,768]{1,0:T(8,128)(2,1)S(1)}, bf16[256,768]{1,0:T(8,128)(2,1)S(1)}, u32[]{:S(2)}, u32[]{:S(2)}) %collective-permute-start.4) | collective-permute-done | bytes 393248 | tf_op jit(solution)/shard_map/ppermute | solution.py:163
  36.6 0.2 collective-permute-start.10
  36.9 2.4 %shard_map.63 = f32[512,768]{1,0:T(8,128)} custom-call(f32[1]{0:T(128)S(6)} %copy.18.scale_ref, f32[1]{0:T(128)S(6)} %copy.19.offset_ref, bf16[512,768]{1,0:T(8,128)(2,1)S(1)} %copy-done, bf16[512,768]{1,0:T(8,128)(2,1)S(1)} %get-tuple-element.17.low_ref, f32[512,768]{1,0:T(8,128)S(1)} %shard_map.62.sum_ref, ...), custom_call_target="tpu_custom_call" | custom-call | flops 50000000 | bytes 1024 | tf_op jit(solution)/shard_map/pallas_call | solution.py:146
  39.3 3.2 %collective-permute-done.7.rest_1_ = bf16[176,768]{1,0:T(8,128)(2,1)S(1)} collective-permute-done((bf16[176,768]{1,0:T(8,128)(2,1)S(1)}, bf16[176,768]{1,0:T(8,128)(2,1)S(1)}, u32[]{:S(2)}, u32[]{:S(2)}) %collective-permute-start.7) | collective-permute-done | bytes 270368 | tf_op jit(solution)/shard_map/ppermute | solution.py:163
  42.4 1.3 %shard_map.65.sum_in = f32[512,768]{1,0:T(8,128)S(1)} custom-call(f32[1]{0:T(128)S(6)} %copy.18.scale_ref, f32[1]{0:T(128)S(6)} %copy.19.offset_ref, bf16[512,768]{1,0:T(8,128)(2,1)S(1)} %get-tuple-element.23.low_ref, f32[512,768]{1,0:T(8,128)S(1)} %shard_map.64.sum_in, ...), custom_call_target="tpu_custom_call", output_to_operand_aliasing={{}: (3, {})} | custom-call | flops 800000000 | bytes 1024 | tf_op jit(solution)/shard_map/pallas_call | solution.py:130
  43.7 0.0 collective-permute-done.8.rest_0_
  43.7 1.1 %shard_map.66.sum_in = f32[512,768]{1,0:T(8,128)S(1)} custom-call(f32[1]{0:T(128)S(6)} %copy.18.scale_ref, f32[1]{0:T(128)S(6)} %copy.19.offset_ref, bf16[512,768]{1,0:T(8,128)(2,1)S(1)} %get-tuple-element.23.low_ref, f32[512,768]{1,0:T(8,128)S(1)} %shard_map.65.sum_in, ...), custom_call_target="tpu_custom_call", output_to_operand_aliasing={{}: (3, {})} | custom-call | flops 1000000000 | bytes 1024 | tf_op jit(solution)/shard_map/pallas_call | solution.py:130
  44.8 0.7 %collective-permute-done.9.rest_0_ = bf16[176,768]{1,0:T(8,128)(2,1)S(1)} collective-permute-done((bf16[176,768]{1,0:T(8,128)(2,1)S(1)}, bf16[176,768]{1,0:T(8,128)(2,1)S(1)}, u32[]{:S(2)}, u32[]{:S(2)}) %collective-permute-start.9) | collective-permute-done | bytes 270368 | tf_op jit(solution)/shard_map/ppermute | solution.py:163
  45.6 1.1 %shard_map.67.sum_ref = f32[512,768]{1,0:T(8,128)S(1)} custom-call(f32[1]{0:T(128)S(6)} %copy.18.scale_ref, f32[1]{0:T(128)S(6)} %copy.19.offset_ref, bf16[512,768]{1,0:T(8,128)(2,1)S(1)} %get-tuple-element.23.low_ref, f32[512,768]{1,0:T(8,128)S(1)} %shard_map.66.sum_in, ...), custom_call_target="tpu_custom_call", output_to_operand_aliasing={{}: (3, {})} | custom-call | flops 50000000 | bytes 1024 | tf_op jit(solution)/shard_map/pallas_call | solution.py:130
  46.7 1.0 %collective-permute-done.10.rest_0_ = bf16[160,768]{1,0:T(8,128)(2,1)S(1)} collective-permute-done((bf16[160,768]{1,0:T(8,128)(2,1)S(1)}, bf16[160,768]{1,0:T(8,128)(2,1)S(1)}, u32[]{:S(2)}, u32[]{:S(2)}) %collective-permute-start.10) | collective-permute-done | bytes 245792 | tf_op jit(solution)/shard_map/ppermute | solution.py:163
  47.7 2.1 %shard_map.68 = f32[512,768]{1,0:T(8,128)} custom-call(f32[1]{0:T(128)S(6)} %copy.18.scale_ref, f32[1]{0:T(128)S(6)} %copy.19.offset_ref, bf16[512,768]{1,0:T(8,128)(2,1)S(1)} %copy-done.1, bf16[512,768]{1,0:T(8,128)(2,1)S(1)} %get-tuple-element.23.low_ref, f32[512,768]{1,0:T(8,128)S(1)} %shard_map.67.sum_ref, ...), custom_call_target="tpu_custom_call" | custom-call | flops 50000000 | bytes 1024 | tf_op jit(solution)/shard_map/pallas_call | solution.py:146
  (7 shorter events, 0.1 us)
Async XLA Ops:
  0.6 4.6 %copy-start = (bf16[512,768]{1,0:T(8,128)(2,1)S(1)}, bf16[512,768]{1,0:T(8,128)(2,1)}, u32[]{:S(2)}) copy-start(bf16[512,768]{1,0:T(8,128)(2,1)} %raw_ref.2) | copy-start | bytes 2359300
  0.6 1.2 %copy-start.1 = (bf16[512,768]{1,0:T(8,128)(2,1)S(1)}, bf16[512,768]{1,0:T(8,128)(2,1)}, u32[]{:S(2)}) copy-start(bf16[512,768]{1,0:T(8,128)(2,1)} %raw_ref.3) | copy-start | bytes 2359300
  2.0 13.0 %collective-permute-start.1 = (bf16[256,768]{1,0:T(8,128)(2,1)S(1)}, bf16[256,768]{1,0:T(8,128)(2,1)S(1)}, u32[]{:S(2)}, u32[]{:S(2)}) collective-permute-start(bf16[256,768]{1,0:T(8,128)(2,1)S(1)} %shard_map.60), channel_id=1, source_target_pairs={{0,1},{1,0},{2,3},{3,2},{4,5},{5,4},{6,7},{7,6},{8,9},{9,8},{10,11... | collective-permute-start | bytes 1179656 | tf_op jit(solution)/shard_map/ppermute | solution.py:163
  5.1 18.3 %collective-permute-start.2 = (bf16[256,768]{1,0:T(8,128)(2,1)S(1)}, bf16[256,768]{1,0:T(8,128)(2,1)S(1)}, u32[]{:S(2)}, u32[]{:S(2)}) collective-permute-start(bf16[256,768]{1,0:T(8,128)(2,1)S(1)} %slice.13), channel_id=1, source_target_pairs={{0,1},{1,0},{2,3},{3,2},{4,5},{5,4},{6,7},{7,6},{8,9},{9,8},{10,11... | collective-permute-start | bytes 1179656 | tf_op jit(solution)/shard_map/ppermute | solution.py:163
  5.2 13.8 %collective-permute-start = (bf16[176,768]{1,0:T(8,128)(2,1)S(1)}, bf16[176,768]{1,0:T(8,128)(2,1)S(1)}, u32[]{:S(2)}, u32[]{:S(2)}) collective-permute-start(bf16[176,768]{1,0:T(8,128)(2,1)S(1)} %get-tuple-element.29), channel_id=1, source_target_pairs={{0,30},{1,3},{2,0},{3,5},{4,2},{5,7},{6,4},{7,9},{8,6},{9,11},{10,... | collective-permute-start | bytes 811016 | tf_op jit(solution)/shard_map/ppermute | solution.py:163
  15.0 13.6 %collective-permute-start.3 = (bf16[256,768]{1,0:T(8,128)(2,1)S(1)}, bf16[256,768]{1,0:T(8,128)(2,1)S(1)}, u32[]{:S(2)}, u32[]{:S(2)}) collective-permute-start(bf16[256,768]{1,0:T(8,128)(2,1)S(1)} %collective-permute-done.1.rest_0_), channel_id=1, source_target_pairs={{0,2},{1,31},{2,4},{3,1},{4,6},{5,3},{6,8},{7,5},{8,10},{9,7},{10,... | collective-permute-start | bytes 1179656 | tf_op jit(solution)/shard_map/ppermute | solution.py:163
  17.1 11.5 %collective-permute-start.5 = (bf16[176,768]{1,0:T(8,128)(2,1)S(1)}, bf16[176,768]{1,0:T(8,128)(2,1)S(1)}, u32[]{:S(2)}, u32[]{:S(2)}) collective-permute-start(bf16[176,768]{1,0:T(8,128)(2,1)S(1)} %get-tuple-element.25), channel_id=1, source_target_pairs={{0,1},{1,0},{2,3},{3,2},{4,5},{5,4},{6,7},{7,6},{8,9},{9,8},{10,11... | collective-permute-start | bytes 811016 | tf_op jit(solution)/shard_map/ppermute | solution.py:163
  23.4 13.2 %collective-permute-start.4 = (bf16[256,768]{1,0:T(8,128)(2,1)S(1)}, bf16[256,768]{1,0:T(8,128)(2,1)S(1)}, u32[]{:S(2)}, u32[]{:S(2)}) collective-permute-start(bf16[256,768]{1,0:T(8,128)(2,1)S(1)} %collective-permute-done.2.rest_0_), channel_id=1, source_target_pairs={{0,2},{1,31},{2,4},{3,1},{4,6},{5,3},{6,8},{7,5},{8,10},{9,7},{10,... | collective-permute-start | bytes 1179656 | tf_op jit(solution)/shard_map/ppermute | solution.py:163
  25.6 8.9 %collective-permute-start.6 = (bf16[160,768]{1,0:T(8,128)(2,1)S(1)}, bf16[160,768]{1,0:T(8,128)(2,1)S(1)}, u32[]{:S(2)}, u32[]{:S(2)}) collective-permute-start(bf16[160,768]{1,0:T(8,128)(2,1)S(1)} %slice.15), channel_id=1, source_target_pairs={{0,1},{1,0},{2,3},{3,2},{4,5},{5,4},{6,7},{7,6},{8,9},{9,8},{10,11... | collective-permute-start | bytes 737288 | tf_op jit(solution)/shard_map/ppermute | solution.py:163
  28.7 13.8 %collective-permute-start.7 = (bf16[176,768]{1,0:T(8,128)(2,1)S(1)}, bf16[176,768]{1,0:T(8,128)(2,1)S(1)}, u32[]{:S(2)}, u32[]{:S(2)}) collective-permute-start(bf16[176,768]{1,0:T(8,128)(2,1)S(1)} %collective-permute-done.5.rest_0_), channel_id=1, source_target_pairs={{0,2},{1,31},{2,4},{3,1},{4,6},{5,3},{6,8},{7,5},{8,10},{9,7},{10,... | collective-permute-start | bytes 811016 | tf_op jit(solution)/shard_map/ppermute | solution.py:163
  31.4 12.4 %collective-permute-start.8 = (bf16[176,768]{1,0:T(8,128)(2,1)S(1)}, bf16[176,768]{1,0:T(8,128)(2,1)S(1)}, u32[]{:S(2)}, u32[]{:S(2)}) collective-permute-start(bf16[176,768]{1,0:T(8,128)(2,1)S(1)} %get-tuple-element.29), channel_id=1, source_target_pairs={{0,1},{1,0},{2,3},{3,2},{4,5},{5,4},{6,7},{7,6},{8,9},{9,8},{10,11... | collective-permute-start | bytes 811016 | tf_op jit(solution)/shard_map/ppermute | solution.py:163
  33.3 12.3 %collective-permute-start.9 = (bf16[176,768]{1,0:T(8,128)(2,1)S(1)}, bf16[176,768]{1,0:T(8,128)(2,1)S(1)}, u32[]{:S(2)}, u32[]{:S(2)}) collective-permute-start(bf16[176,768]{1,0:T(8,128)(2,1)S(1)} %collective-permute-done), channel_id=1, source_target_pairs={{0,1},{1,0},{2,3},{3,2},{4,5},{5,4},{6,7},{7,6},{8,9},{9,8},{10,11... | collective-permute-start | bytes 811016 | tf_op jit(solution)/shard_map/ppermute | solution.py:163
  36.6 11.1 %collective-permute-start.10 = (bf16[160,768]{1,0:T(8,128)(2,1)S(1)}, bf16[160,768]{1,0:T(8,128)(2,1)S(1)}, u32[]{:S(2)}, u32[]{:S(2)}) collective-permute-start(bf16[160,768]{1,0:T(8,128)(2,1)S(1)} %collective-permute-done.6.rest_0_), channel_id=1, source_target_pairs={{0,2},{1,31},{2,4},{3,1},{4,6},{5,3},{6,8},{7,5},{8,10},{9,7},{10,... | collective-permute-start | bytes 737288 | tf_op jit(solution)/shard_map/ppermute | solution.py:163

commit v4 on v3

--- a/solution.py
+++ b/solution.py
@@ -186,28 +186,29 @@
     def cut(value, start, stop):
         return value[rows * start // 32 : rows * stop // 32]
 
-    tail = cut(images, 21, 32)
-    lead = take_call(texts, rows * 16 // 32)
+    tail = cut(images, 22, 32)
+    lead = take_call(texts, rows * 11 // 32)
     near0 = exchange(lead, partner)
-    near1 = exchange(tied(cut(texts, 16, 32), lead), partner)
+    near1 = exchange(tied(cut(texts, 11, 21), lead), partner)
+    near2 = exchange(tied(cut(texts, 21, 32), lead), partner)
+    near3 = exchange(tied(cut(images, 0, 11), lead), partner)
     side = exchange(tail, backward)
     img_low, txt_low, sum_img, sum_txt = own_call(*args, images, texts)
-    far0 = exchange(tied(near0, img_low), onward)
-    near2 = exchange(tied(cut(images, 0, 11), near0), partner)
-    sum_img = add_call(*args, img_low, tied(sum_img, side), (near0,), 0.8)
-    far1 = exchange(tied(near1, sum_img), onward)
-    near3 = exchange(tied(cut(images, 11, 21), near1), partner)
-    sum_img = add_call(*args, img_low, sum_img, (near1,), 0.8)
+    far0 = exchange(near0, onward)
+    near4 = exchange(tied(cut(images, 11, 22), near0), partner)
+    far1 = exchange(tied(near1, img_low), onward)
+    near_tail = exchange(tied(tail, near1), partner)
+    far_tail = exchange(tied(side, near1), partner)
+    sum_img = add_call(*args, img_low, tied(sum_img, side), (near1, near0,), 0.4)
     far2 = exchange(tied(near2, sum_img, far0), onward)
-    near_tail = exchange(tied(tail, near2), partner)
-    far_tail = exchange(tied(side, near2), partner)
-    sum_txt = add_call(*args, txt_low, sum_txt, (near2,), 0.8)
-    far3 = exchange(tied(near3, sum_txt, far1), onward)
-    grad_img = last_call(*args, images, img_low, sum_img, (far0, far1,), 0.05)
-    sum_txt = add_call(*args, txt_low, tied(sum_txt, grad_img), (near3, far2,), 0.8)
+    sum_img = add_call(*args, img_low, sum_img, (near2,), 0.4)
+    far3 = exchange(tied(near3, sum_img, far1), onward)
+    sum_txt = add_call(*args, txt_low, sum_txt, (near3,), 0.4)
+    far4 = exchange(tied(near4, sum_txt), onward)
+    grad_img = last_call(*args, images, img_low, sum_img, (far0, far1, far2,), 0.05)
+    sum_txt = add_call(*args, txt_low, tied(sum_txt, grad_img), (near4, far3,), 0.4)
     sum_txt = add_call(*args, txt_low, sum_txt, (near_tail,), 1.0)
-    sum_txt = add_call(*args, txt_low, sum_txt, (far_tail,), 0.05)
-    grad_txt = last_call(*args, texts, txt_low, sum_txt, (far3,), 0.05)
+    grad_txt = last_call(*args, texts, txt_low, sum_txt, (far4, far_tail), 0.05)
     return grad_img, grad_txt
 
 

time: 50 us -> 48 us (0.960)
  waiting for transfers between devices: 13.2 us -> 6.57 us
  starting transfers between devices: 20.1 us -> 25.6 us
  Pallas kernels: 13.2 us -> 12.3 us
    ppermute x11 -> x13, waiting for transfers between devices: 13.2 us -> 6.57 us  [exchange(): lax.ppermute(value, AXES, [(at, target(at) % count) for at in range(count)])]
    ppermute x11 -> x13, starting transfers between devices: 20.1 us -> 25.6 us  [exchange(): lax.ppermute(value, AXES, [(at, target(at) % count) for at in range(count)])]
    pallas_call x6 -> x5, Pallas kernels: 6.74 us -> 5.83 us  [add_call(): pl.pallas_call(functools.partial(add_kernel, len(others)), out_shape=jax....]
  transfers between devices with their start and end apart: 11 -> 13, of which waited for: 6 -> 5; matrix products, arithmetic and copies ran while one was open for 0% -> 0% of each run, Pallas kernels for 22% -> 21%
where the time goes in v4:
time: 48 us; the launch traced here: 47.8 us
  starting transfers between devices  25.6 us (53%)
  Pallas kernels  12.3 us (26%)
  waiting for transfers between devices  6.57 us (14%)
  between operations  2.07 us (4%)
  local copies, waits for them, and re-layouts  1.29 us (3%)
    ppermute x13, starting transfers between devices, exchange(): lax.ppermute(value, AXES, [(at, target(at) % count) for at in range(count)])  25.6 us
    ppermute x13, waiting for transfers between devices, exchange(): lax.ppermute(value, AXES, [(at, target(at) % count) for at in range(count)])  6.57 us
    pallas_call x5, Pallas kernels, add_call(): pl.pallas_call(functools.partial(add_kernel, len(others)), out_shape=jax....  5.83 us
    pallas_call x2, Pallas kernels, last_call(): pl.pallas_call(functools.partial(last_kernel, len(others), blocks), out_s...  4.69 us
    pallas_call x1, Pallas kernels, own_call(): pl.pallas_call(own_kernel, out_shape=(low, low, total, total), in_specs=[...  1.74 us
    unnamed x4, local copies, waits for them, and re-layouts  1.2 us
  transfers between devices with their start and end apart: 13, of which 5 were waited for; matrix products, arithmetic and copies ran while one was open for 0% of the time, Pallas kernels for 21%

profile of v4, /device:TPU:0, one launch (start us, length us, event | category | flops | bytes accessed | tf_op | source)
XLA Modules:
  0.0 47.8 jit_solution(2149650842839420948)
XLA Ops:
  0.6 1.2 %copy-done.1 = bf16[512,768]{1,0:T(8,128)(2,1)S(1)} copy-done((bf16[512,768]{1,0:T(8,128)(2,1)S(1)}, bf16[512,768]{1,0:T(8,128)(2,1)}, u32[]{:S(2)}) %copy-start.1) | copy-done | bytes 786456
  1.9 3.0 %collective-permute-start.2 = (bf16[176,768]{1,0:T(8,128)(2,1)S(1)}, bf16[176,768]{1,0:T(8,128)(2,1)S(1)}, u32[]{:S(2)}, u32[]{:S(2)}) collective-permute-start(bf16[176,768]{1,0:T(8,128)(2,1)S(1)} %shard_map.60), channel_id=1, source_target_pairs={{0,1},{1,0},{2,3},{3,2},{4,5},{5,4},{6,7},{7,6},{8,9},{9,8},{10,11... | collective-permute-start | bytes 811016 | tf_op jit(solution)/shard_map/ppermute | solution.py:163
  4.9 3.7 %collective-permute-start = (bf16[160,768]{1,0:T(8,128)(2,1)S(1)}, bf16[160,768]{1,0:T(8,128)(2,1)S(1)}, u32[]{:S(2)}, u32[]{:S(2)}) collective-permute-start(bf16[160,768]{1,0:T(8,128)(2,1)S(1)} %slice.15), channel_id=1, source_target_pairs={{0,30},{1,3},{2,0},{3,5},{4,2},{5,7},{6,4},{7,9},{8,6},{9,11},{10,... | collective-permute-start | bytes 737288 | tf_op jit(solution)/shard_map/ppermute | solution.py:163
  8.7 0.1 collective-permute-start.1
  8.8 2.1 %collective-permute-start.3 = (bf16[176,768]{1,0:T(8,128)(2,1)S(1)}, bf16[176,768]{1,0:T(8,128)(2,1)S(1)}, u32[]{:S(2)}, u32[]{:S(2)}) collective-permute-start(bf16[176,768]{1,0:T(8,128)(2,1)S(1)} %slice.17), channel_id=1, source_target_pairs={{0,1},{1,0},{2,3},{3,2},{4,5},{5,4},{6,7},{7,6},{8,9},{9,8},{10,11... | collective-permute-start | bytes 811016 | tf_op jit(solution)/shard_map/ppermute | solution.py:163
  10.9 0.1 collective-permute-start.7
  12.3 0.0 collective-permute-done.2.rest_1_
  12.3 2.0 %collective-permute-start.4 = (bf16[176,768]{1,0:T(8,128)(2,1)S(1)}, bf16[176,768]{1,0:T(8,128)(2,1)S(1)}, u32[]{:S(2)}, u32[]{:S(2)}) collective-permute-start(bf16[176,768]{1,0:T(8,128)(2,1)S(1)} %collective-permute-done.2.rest_1_), channel_id=1, source_target_pairs={{0,2},{1,31},{2,4},{3,1},{4,6},{5,3},{6,8},{7,5},{8,10},{9,7},{10,... | collective-permute-start | bytes 811016 | tf_op jit(solution)/shard_map/ppermute | solution.py:163
  14.3 1.7 %shard_map.59 = (bf16[512,768]{1,0:T(8,128)(2,1)S(1)}, bf16[512,768]{1,0:T(8,128)(2,1)S(1)}, f32[512,768]{1,0:T(8,128)S(1)}, f32[512,768]{1,0:T(8,128)S(1)}) custom-call(f32[1]{0:T(128)S(6)} %copy.16.scale_ref, f32[1]{0:T(128)S(6)} %copy.17.offset_ref, bf16[512,768]{1,0:T(8,128)(2,1)S(1)} %copy-done, bf16[512,768]{1,0:T(8,128)(2,1)S(1)} %copy-done.1), custom_call_target="tpu_custom_call" | custom-call | flops 800000000 | bytes 1024 | tf_op jit(solution)/shard_map/pallas_call | solution.py:117
  16.1 1.5 %collective-permute-done.1.rest_0_ = bf16[160,768]{1,0:T(8,128)(2,1)S(1)} collective-permute-done((bf16[160,768]{1,0:T(8,128)(2,1)S(1)}, bf16[160,768]{1,0:T(8,128)(2,1)S(1)}, u32[]{:S(2)}, u32[]{:S(2)}) %collective-permute-start.1) | collective-permute-done | bytes 245792 | tf_op jit(solution)/shard_map/ppermute | solution.py:163
  17.6 2.0 %collective-permute-start.5 = (bf16[160,768]{1,0:T(8,128)(2,1)S(1)}, bf16[160,768]{1,0:T(8,128)(2,1)S(1)}, u32[]{:S(2)}, u32[]{:S(2)}) collective-permute-start(bf16[160,768]{1,0:T(8,128)(2,1)S(1)} %collective-permute-done.1.rest_0_), channel_id=1, source_target_pairs={{0,2},{1,31},{2,4},{3,1},{4,6},{5,3},{6,8},{7,5},{8,10},{9,7},{10,... | collective-permute-start | bytes 737288 | tf_op jit(solution)/shard_map/ppermute | solution.py:163
  19.6 1.9 %collective-permute-start.8 = (bf16[176,768]{1,0:T(8,128)(2,1)S(1)}, bf16[176,768]{1,0:T(8,128)(2,1)S(1)}, u32[]{:S(2)}, u32[]{:S(2)}) collective-permute-start(bf16[176,768]{1,0:T(8,128)(2,1)S(1)} %get-tuple-element.29), channel_id=1, source_target_pairs={{0,1},{1,0},{2,3},{3,2},{4,5},{5,4},{6,7},{7,6},{8,9},{9,8},{10,11... | collective-permute-start | bytes 811016 | tf_op jit(solution)/shard_map/ppermute | solution.py:163
  21.5 1.3 %shard_map.61.sum_in = f32[512,768]{1,0:T(8,128)S(1)} custom-call(f32[1]{0:T(128)S(6)} %copy.16.scale_ref, f32[1]{0:T(128)S(6)} %copy.17.offset_ref, bf16[512,768]{1,0:T(8,128)(2,1)S(1)} %get-tuple-element.18.low_ref, f32[512,768]{1,0:T(8,128)S(1)} %get-tuple-element.20.sum_in, ...), custom_call_target="tpu_custom_call", output_to_operand_aliasing={{}: (3, {})} | custom-call | flops 400000000 | bytes 1024 | tf_op jit(solution)/shard_map/pallas_call | solution.py:130
  22.8 0.6 %collective-permute-done.3.rest_0_ = bf16[176,768]{1,0:T(8,128)(2,1)S(1)} collective-permute-done((bf16[176,768]{1,0:T(8,128)(2,1)S(1)}, bf16[176,768]{1,0:T(8,128)(2,1)S(1)}, u32[]{:S(2)}, u32[]{:S(2)}) %collective-permute-start.3) | collective-permute-done | bytes 270368 | tf_op jit(solution)/shard_map/ppermute | solution.py:163
  23.4 0.0 collective-permute-done.4.rest_0_
  23.4 2.0 %collective-permute-start.6 = (bf16[176,768]{1,0:T(8,128)(2,1)S(1)}, bf16[176,768]{1,0:T(8,128)(2,1)S(1)}, u32[]{:S(2)}, u32[]{:S(2)}) collective-permute-start(bf16[176,768]{1,0:T(8,128)(2,1)S(1)} %collective-permute-done.3.rest_0_), channel_id=1, source_target_pairs={{0,2},{1,31},{2,4},{3,1},{4,6},{5,3},{6,8},{7,5},{8,10},{9,7},{10,... | collective-permute-start | bytes 811016 | tf_op jit(solution)/shard_map/ppermute | solution.py:163
  25.4 1.1 %shard_map.62.sum_ref = f32[512,768]{1,0:T(8,128)S(1)} custom-call(f32[1]{0:T(128)S(6)} %copy.16.scale_ref, f32[1]{0:T(128)S(6)} %copy.17.offset_ref, bf16[512,768]{1,0:T(8,128)(2,1)S(1)} %get-tuple-element.18.low_ref, f32[512,768]{1,0:T(8,128)S(1)} %shard_map.61.sum_in, ...), custom_call_target="tpu_custom_call", output_to_operand_aliasing={{}: (3, {})} | custom-call | flops 400000000 | bytes 1024 | tf_op jit(solution)/shard_map/pallas_call | solution.py:130
  26.5 2.7 %collective-permute-done.7.rest_0_ = bf16[176,768]{1,0:T(8,128)(2,1)S(1)} collective-permute-done((bf16[176,768]{1,0:T(8,128)(2,1)S(1)}, bf16[176,768]{1,0:T(8,128)(2,1)S(1)}, u32[]{:S(2)}, u32[]{:S(2)}) %collective-permute-start.7) | collective-permute-done | bytes 270368 | tf_op jit(solution)/shard_map/ppermute | solution.py:163
  29.2 0.0 collective-permute-done.5.rest_1_
  29.2 2.0 %collective-permute-start.9 = (bf16[176,768]{1,0:T(8,128)(2,1)S(1)}, bf16[176,768]{1,0:T(8,128)(2,1)S(1)}, u32[]{:S(2)}, u32[]{:S(2)}) collective-permute-start(bf16[176,768]{1,0:T(8,128)(2,1)S(1)} %collective-permute-done.7.rest_0_), channel_id=1, source_target_pairs={{0,2},{1,31},{2,4},{3,1},{4,6},{5,3},{6,8},{7,5},{8,10},{9,7},{10,... | collective-permute-start | bytes 811016 | tf_op jit(solution)/shard_map/ppermute | solution.py:163
  31.2 1.9 %collective-permute-start.10 = (bf16[160,768]{1,0:T(8,128)(2,1)S(1)}, bf16[160,768]{1,0:T(8,128)(2,1)S(1)}, u32[]{:S(2)}, u32[]{:S(2)}) collective-permute-start(bf16[160,768]{1,0:T(8,128)(2,1)S(1)} %slice.15), channel_id=1, source_target_pairs={{0,1},{1,0},{2,3},{3,2},{4,5},{5,4},{6,7},{7,6},{8,9},{9,8},{10,11... | collective-permute-start | bytes 737288 | tf_op jit(solution)/shard_map/ppermute | solution.py:163
  33.1 1.1 %shard_map.64.sum_in = f32[512,768]{1,0:T(8,128)S(1)} custom-call(f32[1]{0:T(128)S(6)} %copy.16.scale_ref, f32[1]{0:T(128)S(6)} %copy.17.offset_ref, bf16[512,768]{1,0:T(8,128)(2,1)S(1)} %get-tuple-element.25.low_ref, f32[512,768]{1,0:T(8,128)S(1)} %get-tuple-element.26.sum_in, ...), custom_call_target="tpu_custom_call", output_to_operand_aliasing={{}: (3, {})} | custom-call | flops 400000000 | bytes 1024 | tf_op jit(solution)/shard_map/pallas_call | solution.py:130
  34.2 0.0 collective-permute-done.8.rest_0_
  34.2 2.8 %collective-permute-start.11 = (bf16[176,768]{1,0:T(8,128)(2,1)S(1)}, bf16[176,768]{1,0:T(8,128)(2,1)S(1)}, u32[]{:S(2)}, u32[]{:S(2)}) collective-permute-start(bf16[176,768]{1,0:T(8,128)(2,1)S(1)} %collective-permute-done.8.rest_0_), channel_id=1, source_target_pairs={{0,2},{1,31},{2,4},{3,1},{4,6},{5,3},{6,8},{7,5},{8,10},{9,7},{10,... | collective-permute-start | bytes 811016 | tf_op jit(solution)/shard_map/ppermute | solution.py:163
  37.0 1.9 %collective-permute-start.12 = (bf16[160,768]{1,0:T(8,128)(2,1)S(1)}, bf16[160,768]{1,0:T(8,128)(2,1)S(1)}, u32[]{:S(2)}, u32[]{:S(2)}) collective-permute-start(bf16[160,768]{1,0:T(8,128)(2,1)S(1)} %collective-permute-done), channel_id=1, source_target_pairs={{0,1},{1,0},{2,3},{3,2},{4,5},{5,4},{6,7},{7,6},{8,9},{9,8},{10,11... | collective-permute-start | bytes 737288 | tf_op jit(solution)/shard_map/ppermute | solution.py:163
  38.9 0.0 collective-permute-done.6.rest_2_
  38.9 2.4 %shard_map.63 = f32[512,768]{1,0:T(8,128)} custom-call(f32[1]{0:T(128)S(6)} %copy.16.scale_ref, f32[1]{0:T(128)S(6)} %copy.17.offset_ref, bf16[512,768]{1,0:T(8,128)(2,1)S(1)} %copy-done, bf16[512,768]{1,0:T(8,128)(2,1)S(1)} %get-tuple-element.18.low_ref, f32[512,768]{1,0:T(8,128)S(1)} %shard_map.62.sum_ref, ...), custom_call_target="tpu_custom_call" | custom-call | flops 50000000 | bytes 1024 | tf_op jit(solution)/shard_map/pallas_call | solution.py:146
  41.3 1.3 %shard_map.65.sum_in = f32[512,768]{1,0:T(8,128)S(1)} custom-call(f32[1]{0:T(128)S(6)} %copy.16.scale_ref, f32[1]{0:T(128)S(6)} %copy.17.offset_ref, bf16[512,768]{1,0:T(8,128)(2,1)S(1)} %get-tuple-element.25.low_ref, f32[512,768]{1,0:T(8,128)S(1)} %shard_map.64.sum_in, ...), custom_call_target="tpu_custom_call", output_to_operand_aliasing={{}: (3, {})} | custom-call | flops 400000000 | bytes 1024 | tf_op jit(solution)/shard_map/pallas_call | solution.py:130
  42.6 1.1 %shard_map.66.sum_ref = f32[512,768]{1,0:T(8,128)S(1)} custom-call(f32[1]{0:T(128)S(6)} %copy.16.scale_ref, f32[1]{0:T(128)S(6)} %copy.17.offset_ref, bf16[512,768]{1,0:T(8,128)(2,1)S(1)} %get-tuple-element.25.low_ref, f32[512,768]{1,0:T(8,128)S(1)} %shard_map.65.sum_in, ...), custom_call_target="tpu_custom_call", output_to_operand_aliasing={{}: (3, {})} | custom-call | flops 1000000000 | bytes 1024 | tf_op jit(solution)/shard_map/pallas_call | solution.py:130
  43.7 1.2 %collective-permute-done.12.rest_1_ = bf16[160,768]{1,0:T(8,128)(2,1)S(1)} collective-permute-done((bf16[160,768]{1,0:T(8,128)(2,1)S(1)}, bf16[160,768]{1,0:T(8,128)(2,1)S(1)}, u32[]{:S(2)}, u32[]{:S(2)}) %collective-permute-start.12) | collective-permute-done | bytes 245792 | tf_op jit(solution)/shard_map/ppermute | solution.py:163
  44.9 0.6 %collective-permute-done.11.rest_0_ = bf16[176,768]{1,0:T(8,128)(2,1)S(1)} collective-permute-done((bf16[176,768]{1,0:T(8,128)(2,1)S(1)}, bf16[176,768]{1,0:T(8,128)(2,1)S(1)}, u32[]{:S(2)}, u32[]{:S(2)}) %collective-permute-start.11) | collective-permute-done | bytes 270368 | tf_op jit(solution)/shard_map/ppermute | solution.py:163
  45.5 2.3 %shard_map.67 = f32[512,768]{1,0:T(8,128)} custom-call(f32[1]{0:T(128)S(6)} %copy.16.scale_ref, f32[1]{0:T(128)S(6)} %copy.17.offset_ref, bf16[512,768]{1,0:T(8,128)(2,1)S(1)} %copy-done.1, bf16[512,768]{1,0:T(8,128)(2,1)S(1)} %get-tuple-element.25.low_ref, f32[512,768]{1,0:T(8,128)S(1)} %shard_map.66.sum_ref, ...), custom_call_target="tpu_custom_call" | custom-call | flops 50000000 | bytes 1024 | tf_op jit(solution)/shard_map/pallas_call | solution.py:146
  (11 shorter events, 0.1 us)
Async XLA Ops:
  0.6 4.3 %copy-start = (bf16[512,768]{1,0:T(8,128)(2,1)S(1)}, bf16[512,768]{1,0:T(8,128)(2,1)}, u32[]{:S(2)}) copy-start(bf16[512,768]{1,0:T(8,128)(2,1)} %raw_ref.2) | copy-start | bytes 2359300
  0.6 1.2 %copy-start.1 = (bf16[512,768]{1,0:T(8,128)(2,1)S(1)}, bf16[512,768]{1,0:T(8,128)(2,1)}, u32[]{:S(2)}) copy-start(bf16[512,768]{1,0:T(8,128)(2,1)} %raw_ref.3) | copy-start | bytes 2359300
  1.9 10.4 %collective-permute-start.2 = (bf16[176,768]{1,0:T(8,128)(2,1)S(1)}, bf16[176,768]{1,0:T(8,128)(2,1)S(1)}, u32[]{:S(2)}, u32[]{:S(2)}) collective-permute-start(bf16[176,768]{1,0:T(8,128)(2,1)S(1)} %shard_map.60), channel_id=1, source_target_pairs={{0,1},{1,0},{2,3},{3,2},{4,5},{5,4},{6,7},{7,6},{8,9},{9,8},{10,11... | collective-permute-start | bytes 811016 | tf_op jit(solution)/shard_map/ppermute | solution.py:163
  4.9 14.7 %collective-permute-start = (bf16[160,768]{1,0:T(8,128)(2,1)S(1)}, bf16[160,768]{1,0:T(8,128)(2,1)S(1)}, u32[]{:S(2)}, u32[]{:S(2)}) collective-permute-start(bf16[160,768]{1,0:T(8,128)(2,1)S(1)} %slice.15), channel_id=1, source_target_pairs={{0,30},{1,3},{2,0},{3,5},{4,2},{5,7},{6,4},{7,9},{8,6},{9,11},{10,... | collective-permute-start | bytes 737288 | tf_op jit(solution)/shard_map/ppermute | solution.py:163
  8.7 8.9 %collective-permute-start.1 = (bf16[160,768]{1,0:T(8,128)(2,1)S(1)}, bf16[160,768]{1,0:T(8,128)(2,1)S(1)}, u32[]{:S(2)}, u32[]{:S(2)}) collective-permute-start(bf16[160,768]{1,0:T(8,128)(2,1)S(1)} %slice.16), channel_id=1, source_target_pairs={{0,1},{1,0},{2,3},{3,2},{4,5},{5,4},{6,7},{7,6},{8,9},{9,8},{10,11... | collective-permute-start | bytes 737288 | tf_op jit(solution)/shard_map/ppermute | solution.py:163
  8.8 14.6 %collective-permute-start.3 = (bf16[176,768]{1,0:T(8,128)(2,1)S(1)}, bf16[176,768]{1,0:T(8,128)(2,1)S(1)}, u32[]{:S(2)}, u32[]{:S(2)}) collective-permute-start(bf16[176,768]{1,0:T(8,128)(2,1)S(1)} %slice.17), channel_id=1, source_target_pairs={{0,1},{1,0},{2,3},{3,2},{4,5},{5,4},{6,7},{7,6},{8,9},{9,8},{10,11... | collective-permute-start | bytes 811016 | tf_op jit(solution)/shard_map/ppermute | solution.py:163
  10.9 18.2 %collective-permute-start.7 = (bf16[176,768]{1,0:T(8,128)(2,1)S(1)}, bf16[176,768]{1,0:T(8,128)(2,1)S(1)}, u32[]{:S(2)}, u32[]{:S(2)}) collective-permute-start(bf16[176,768]{1,0:T(8,128)(2,1)S(1)} %get-tuple-element.27), channel_id=1, source_target_pairs={{0,1},{1,0},{2,3},{3,2},{4,5},{5,4},{6,7},{7,6},{8,9},{9,8},{10,11... | collective-permute-start | bytes 811016 | tf_op jit(solution)/shard_map/ppermute | solution.py:163
  12.3 11.1 %collective-permute-start.4 = (bf16[176,768]{1,0:T(8,128)(2,1)S(1)}, bf16[176,768]{1,0:T(8,128)(2,1)S(1)}, u32[]{:S(2)}, u32[]{:S(2)}) collective-permute-start(bf16[176,768]{1,0:T(8,128)(2,1)S(1)} %collective-permute-done.2.rest_1_), channel_id=1, source_target_pairs={{0,2},{1,31},{2,4},{3,1},{4,6},{5,3},{6,8},{7,5},{8,10},{9,7},{10,... | collective-permute-start | bytes 811016 | tf_op jit(solution)/shard_map/ppermute | solution.py:163
  17.6 11.6 %collective-permute-start.5 = (bf16[160,768]{1,0:T(8,128)(2,1)S(1)}, bf16[160,768]{1,0:T(8,128)(2,1)S(1)}, u32[]{:S(2)}, u32[]{:S(2)}) collective-permute-start(bf16[160,768]{1,0:T(8,128)(2,1)S(1)} %collective-permute-done.1.rest_0_), channel_id=1, source_target_pairs={{0,2},{1,31},{2,4},{3,1},{4,6},{5,3},{6,8},{7,5},{8,10},{9,7},{10,... | collective-permute-start | bytes 737288 | tf_op jit(solution)/shard_map/ppermute | solution.py:163
  19.6 14.6 %collective-permute-start.8 = (bf16[176,768]{1,0:T(8,128)(2,1)S(1)}, bf16[176,768]{1,0:T(8,128)(2,1)S(1)}, u32[]{:S(2)}, u32[]{:S(2)}) collective-permute-start(bf16[176,768]{1,0:T(8,128)(2,1)S(1)} %get-tuple-element.29), channel_id=1, source_target_pairs={{0,1},{1,0},{2,3},{3,2},{4,5},{5,4},{6,7},{7,6},{8,9},{9,8},{10,11... | collective-permute-start | bytes 811016 | tf_op jit(solution)/shard_map/ppermute | solution.py:163
  23.4 15.5 %collective-permute-start.6 = (bf16[176,768]{1,0:T(8,128)(2,1)S(1)}, bf16[176,768]{1,0:T(8,128)(2,1)S(1)}, u32[]{:S(2)}, u32[]{:S(2)}) collective-permute-start(bf16[176,768]{1,0:T(8,128)(2,1)S(1)} %collective-permute-done.3.rest_0_), channel_id=1, source_target_pairs={{0,2},{1,31},{2,4},{3,1},{4,6},{5,3},{6,8},{7,5},{8,10},{9,7},{10,... | collective-permute-start | bytes 811016 | tf_op jit(solution)/shard_map/ppermute | solution.py:163
  29.2 12.1 %collective-permute-start.9 = (bf16[176,768]{1,0:T(8,128)(2,1)S(1)}, bf16[176,768]{1,0:T(8,128)(2,1)S(1)}, u32[]{:S(2)}, u32[]{:S(2)}) collective-permute-start(bf16[176,768]{1,0:T(8,128)(2,1)S(1)} %collective-permute-done.7.rest_0_), channel_id=1, source_target_pairs={{0,2},{1,31},{2,4},{3,1},{4,6},{5,3},{6,8},{7,5},{8,10},{9,7},{10,... | collective-permute-start | bytes 811016 | tf_op jit(solution)/shard_map/ppermute | solution.py:163
  31.2 11.4 %collective-permute-start.10 = (bf16[160,768]{1,0:T(8,128)(2,1)S(1)}, bf16[160,768]{1,0:T(8,128)(2,1)S(1)}, u32[]{:S(2)}, u32[]{:S(2)}) collective-permute-start(bf16[160,768]{1,0:T(8,128)(2,1)S(1)} %slice.15), channel_id=1, source_target_pairs={{0,1},{1,0},{2,3},{3,2},{4,5},{5,4},{6,7},{7,6},{8,9},{9,8},{10,11... | collective-permute-start | bytes 737288 | tf_op jit(solution)/shard_map/ppermute | solution.py:163
  34.2 11.3 %collective-permute-start.11 = (bf16[176,768]{1,0:T(8,128)(2,1)S(1)}, bf16[176,768]{1,0:T(8,128)(2,1)S(1)}, u32[]{:S(2)}, u32[]{:S(2)}) collective-permute-start(bf16[176,768]{1,0:T(8,128)(2,1)S(1)} %collective-permute-done.8.rest_0_), channel_id=1, source_target_pairs={{0,2},{1,31},{2,4},{3,1},{4,6},{5,3},{6,8},{7,5},{8,10},{9,7},{10,... | collective-permute-start | bytes 811016 | tf_op jit(solution)/shard_map/ppermute | solution.py:163
  37.0 7.9 %collective-permute-start.12 = (bf16[160,768]{1,0:T(8,128)(2,1)S(1)}, bf16[160,768]{1,0:T(8,128)(2,1)S(1)}, u32[]{:S(2)}, u32[]{:S(2)}) collective-permute-start(bf16[160,768]{1,0:T(8,128)(2,1)S(1)} %collective-permute-done), channel_id=1, source_target_pairs={{0,1},{1,0},{2,3},{3,2},{4,5},{5,4},{6,7},{7,6},{8,9},{9,8},{10,11... | collective-permute-start | bytes 737288 | tf_op jit(solution)/shard_map/ppermute | solution.py:163

commit v5 on v4

--- a/solution.py
+++ b/solution.py
@@ -64,10 +64,21 @@
     sum_out[...] = sum_in[...] + band_term(low_ref[...], other_low[...], scale, offset)
 
 
-def last_kernel(count, blocks, scale_ref, offset_ref, raw_ref, low_ref, sum_ref, *rest):
+def unit_kernel(value_ref, unit_ref, recip_ref):
+    unit_ref[...], recip_ref[...] = unit_rows(value_ref[...])
+
+
+def low_kernel(value_ref, low_ref):
+    low_ref[...] = unit_rows(value_ref[...])[0].astype(jnp.bfloat16)
+
+
+def last_kernel(count, raw_count, blocks, scale_ref, offset_ref, unit_ref, recip_ref, low_ref, sum_ref, *rest):
     others, (out_ref, other_low, held, sems) = rest[:count], rest[count:]
     scale, offset = scale_ref[0], offset_ref[0]
-    lower_rows(others, other_low)
+    lower_rows(others[:raw_count], other_low)
+    if count > raw_count:
+        at = sum(other.shape[0] for other in others[:raw_count])
+        other_low[at:, :] = others[-1][...]
     logits = scale * dot32(low_ref[...], other_low[...], LAST) + offset
     weight = jax.nn.sigmoid(logits).astype(jnp.bfloat16)
     size = held.shape[0] // blocks
@@ -75,13 +86,13 @@
     for block in range(blocks):
         start = block * size
         at = pl.ds(start, size)
-        unit, recip = unit_rows(raw_ref[at, :])
+        unit = unit_ref[at, :]
         term = jnp.dot(
             weight[start : start + size], other_low[...], preferred_element_type=jnp.float32
         )
         grad = scale * (sum_ref[at, :] + term)
         along = jnp.sum(unit * grad, axis=-1, keepdims=True)
-        held[at, :] = (grad - unit * along) * recip
+        held[at, :] = (grad - unit * along) * recip_ref[at, :]
         copy = pltpu.make_async_copy(held.at[at, :], out_ref.at[at, :], sems.at[block])
         copy.start()
         copies.append(copy)
@@ -139,14 +150,14 @@
     )(scale, offset, low, total, *others)
 
 
-def last_call(scale, offset, raw, low, total, others, micros):
-    rows, width = raw.shape
+def last_call(scale, offset, unit, recip, low, total, others, raw_count, micros):
+    rows, width = unit.shape
     count = sum(other.shape[0] for other in others)
     blocks = 4 if rows % 64 == 0 else 1
     return pl.pallas_call(
-        functools.partial(last_kernel, len(others), blocks),
+        functools.partial(last_kernel, len(others), raw_count, blocks),
         out_shape=jax.ShapeDtypeStruct((rows, width), jnp.float32),
-        in_specs=[SMEM, SMEM] + [VMEM] * (3 + len(others)),
+        in_specs=[SMEM, SMEM] + [VMEM] * (4 + len(others)),
         out_specs=pl.BlockSpec(memory_space=pl.ANY),
         scratch_shapes=[
             pltpu.VMEM((count, width), jnp.bfloat16),
@@ -155,7 +166,33 @@
         ],
         compiler_params=PARAMS,
         cost_estimate=cost(micros),
-    )(scale, offset, raw, low, total, *others)
+    )(scale, offset, unit, recip, low, total, *others)
+
+
+def unit_call(value):
+    rows, width = value.shape
+    return pl.pallas_call(
+        unit_kernel,
+        out_shape=(
+            jax.ShapeDtypeStruct((rows, width), jnp.float32),
+            jax.ShapeDtypeStruct((rows, 1), jnp.float32),
+        ),
+        in_specs=[VMEM],
+        out_specs=(VMEM, VMEM),
+        compiler_params=PARAMS,
+        cost_estimate=cost(0.05),
+    )(value)
+
+
+def low_call(value):
+    return pl.pallas_call(
+        low_kernel,
+        out_shape=jax.ShapeDtypeStruct(value.shape, jnp.bfloat16),
+        in_specs=[VMEM],
+        out_specs=VMEM,
+        compiler_params=PARAMS,
+        cost_estimate=cost(0.3),
+    )(value)
 
 
 def exchange(value, target):
@@ -202,13 +239,15 @@
     sum_img = add_call(*args, img_low, tied(sum_img, side), (near1, near0,), 0.4)
     far2 = exchange(tied(near2, sum_img, far0), onward)
     sum_img = add_call(*args, img_low, sum_img, (near2,), 0.4)
-    far3 = exchange(tied(near3, sum_img, far1), onward)
+    unit_img, recip_img = unit_call(tied(images, sum_img))
+    unit_txt, recip_txt = unit_call(tied(texts, unit_img))
+    far3 = exchange(tied(near3, unit_txt, unit_img, sum_img, far1), onward)
     sum_txt = add_call(*args, txt_low, sum_txt, (near3,), 0.4)
     far4 = exchange(tied(near4, sum_txt), onward)
-    grad_img = last_call(*args, images, img_low, sum_img, (far0, far1, far2,), 0.05)
+    grad_img = last_call(*args, unit_img, recip_img, img_low, sum_img, (far0, far1, far2), 3, 0.05)
     sum_txt = add_call(*args, txt_low, tied(sum_txt, grad_img), (near4, far3,), 0.4)
     sum_txt = add_call(*args, txt_low, sum_txt, (near_tail,), 1.0)
-    grad_txt = last_call(*args, texts, txt_low, sum_txt, (far4, far_tail), 0.05)
+    grad_txt = last_call(*args, unit_txt, recip_txt, txt_low, sum_txt, (far4, low_call(tied(far_tail, sum_txt))), 1, 0.05)
     return grad_img, grad_txt
 
 

time: 48 us -> 47.8 us (level)
  starting transfers between devices: 25.6 us -> 23.7 us
  waiting for transfers between devices: 6.57 us -> 7.87 us
    ppermute x13, starting transfers between devices: 25.6 us -> 23.7 us  [exchange(): lax.ppermute(value, AXES, [(at, target(at) % count) for at in range(count)])]
    ppermute x13, waiting for transfers between devices: 6.57 us -> 7.87 us  [exchange(): lax.ppermute(value, AXES, [(at, target(at) % count) for at in range(count)])]
    pallas_call x2 -> x5, Pallas kernels: 4.69 us -> 5.1 us  [the longest x2 4.43 us: last_call(): pl.pallas_call(functools.partial(last_kernel, len(others), raw_count, blo...]
  transfers between devices with their start and end apart: 13 -> 13, of which waited for: 5 -> 6; matrix products, arithmetic and copies ran while one was open for 0% -> 0% of each run, Pallas kernels for 21% -> 22%
where the time goes in v5:
time: 47.8 us; the launch traced here: 47.6 us
  starting transfers between devices  23.7 us (50%)
  Pallas kernels  12.7 us (27%)
  waiting for transfers between devices  7.87 us (16%)
  between operations  2.09 us (4%)
  local copies, waits for them, and re-layouts  1.29 us (3%)
    ppermute x13, starting transfers between devices, exchange(): lax.ppermute(value, AXES, [(at, target(at) % count) for at in range(count)])  23.7 us
    ppermute x13, waiting for transfers between devices, exchange(): lax.ppermute(value, AXES, [(at, target(at) % count) for at in range(count)])  7.87 us
    pallas_call x5, Pallas kernels, add_call(): pl.pallas_call(functools.partial(add_kernel, len(others)), out_shape=jax....  5.83 us
    pallas_call x2, Pallas kernels, last_call(): pl.pallas_call(functools.partial(last_kernel, len(others), raw_count, blo...  4.43 us
    pallas_call x1, Pallas kernels, own_call(): pl.pallas_call(own_kernel, out_shape=(low, low, total, total), in_specs=[...  1.76 us
    unnamed x4, local copies, waits for them, and re-layouts  1.2 us
  transfers between devices with their start and end apart: 13, of which 6 were waited for; matrix products, arithmetic and copies ran while one was open for 0% of the time, Pallas kernels for 22%

profile of v5, /device:TPU:0, one launch (start us, length us, event | category | flops | bytes accessed | tf_op | source)
XLA Modules:
  0.0 47.6 jit_solution(12134674592042473339)
XLA Ops:
  0.6 1.2 %copy-done.1 = bf16[512,768]{1,0:T(8,128)(2,1)S(1)} copy-done((bf16[512,768]{1,0:T(8,128)(2,1)S(1)}, bf16[512,768]{1,0:T(8,128)(2,1)}, u32[]{:S(2)}) %copy-start.1) | copy-done | bytes 786456
  1.9 3.0 %collective-permute-start.2 = (bf16[176,768]{1,0:T(8,128)(2,1)S(1)}, bf16[176,768]{1,0:T(8,128)(2,1)S(1)}, u32[]{:S(2)}, u32[]{:S(2)}) collective-permute-start(bf16[176,768]{1,0:T(8,128)(2,1)S(1)} %shard_map.60), channel_id=1, source_target_pairs={{0,1},{1,0},{2,3},{3,2},{4,5},{5,4},{6,7},{7,6},{8,9},{9,8},{10,11... | collective-permute-start | bytes 811016 | tf_op jit(solution)/shard_map/ppermute | solution.py:200
  4.9 3.7 %collective-permute-start = (bf16[160,768]{1,0:T(8,128)(2,1)S(1)}, bf16[160,768]{1,0:T(8,128)(2,1)S(1)}, u32[]{:S(2)}, u32[]{:S(2)}) collective-permute-start(bf16[160,768]{1,0:T(8,128)(2,1)S(1)} %slice.15), channel_id=1, source_target_pairs={{0,30},{1,3},{2,0},{3,5},{4,2},{5,7},{6,4},{7,9},{8,6},{9,11},{10,... | collective-permute-start | bytes 737288 | tf_op jit(solution)/shard_map/ppermute | solution.py:200
  8.7 0.1 collective-permute-start.1
  8.8 2.1 %collective-permute-start.3 = (bf16[176,768]{1,0:T(8,128)(2,1)S(1)}, bf16[176,768]{1,0:T(8,128)(2,1)S(1)}, u32[]{:S(2)}, u32[]{:S(2)}) collective-permute-start(bf16[176,768]{1,0:T(8,128)(2,1)S(1)} %slice.17), channel_id=1, source_target_pairs={{0,1},{1,0},{2,3},{3,2},{4,5},{5,4},{6,7},{7,6},{8,9},{9,8},{10,11... | collective-permute-start | bytes 811016 | tf_op jit(solution)/shard_map/ppermute | solution.py:200
  10.9 0.1 collective-permute-start.7
  12.3 2.0 %collective-permute-start.4 = (bf16[176,768]{1,0:T(8,128)(2,1)S(1)}, bf16[176,768]{1,0:T(8,128)(2,1)S(1)}, u32[]{:S(2)}, u32[]{:S(2)}) collective-permute-start(bf16[176,768]{1,0:T(8,128)(2,1)S(1)} %collective-permute-done.2.rest_1_), channel_id=1, source_target_pairs={{0,2},{1,31},{2,4},{3,1},{4,6},{5,3},{6,8},{7,5},{8,10},{9,7},{10,... | collective-permute-start | bytes 811016 | tf_op jit(solution)/shard_map/ppermute | solution.py:200
  14.3 1.8 %shard_map.59 = (bf16[512,768]{1,0:T(8,128)(2,1)S(1)}, bf16[512,768]{1,0:T(8,128)(2,1)S(1)}, f32[512,768]{1,0:T(8,128)S(1)}, f32[512,768]{1,0:T(8,128)S(1)}) custom-call(f32[1]{0:T(128)S(6)} %copy.16.scale_ref, f32[1]{0:T(128)S(6)} %copy.17.offset_ref, bf16[512,768]{1,0:T(8,128)(2,1)S(1)} %copy-done, bf16[512,768]{1,0:T(8,128)(2,1)S(1)} %copy-done.1), custom_call_target="tpu_custom_call" | custom-call | flops 800000000 | bytes 1024 | tf_op jit(solution)/shard_map/pallas_call | solution.py:128
  16.1 1.5 %collective-permute-done.1.rest_0_ = bf16[160,768]{1,0:T(8,128)(2,1)S(1)} collective-permute-done((bf16[160,768]{1,0:T(8,128)(2,1)S(1)}, bf16[160,768]{1,0:T(8,128)(2,1)S(1)}, u32[]{:S(2)}, u32[]{:S(2)}) %collective-permute-start.1) | collective-permute-done | bytes 245792 | tf_op jit(solution)/shard_map/ppermute | solution.py:200
  17.6 2.0 %collective-permute-start.5 = (bf16[160,768]{1,0:T(8,128)(2,1)S(1)}, bf16[160,768]{1,0:T(8,128)(2,1)S(1)}, u32[]{:S(2)}, u32[]{:S(2)}) collective-permute-start(bf16[160,768]{1,0:T(8,128)(2,1)S(1)} %collective-permute-done.1.rest_0_), channel_id=1, source_target_pairs={{0,2},{1,31},{2,4},{3,1},{4,6},{5,3},{6,8},{7,5},{8,10},{9,7},{10,... | collective-permute-start | bytes 737288 | tf_op jit(solution)/shard_map/ppermute | solution.py:200
  19.6 0.0 collective-permute-done
  19.6 1.9 %collective-permute-start.8 = (bf16[176,768]{1,0:T(8,128)(2,1)S(1)}, bf16[176,768]{1,0:T(8,128)(2,1)S(1)}, u32[]{:S(2)}, u32[]{:S(2)}) collective-permute-start(bf16[176,768]{1,0:T(8,128)(2,1)S(1)} %get-tuple-element.42), channel_id=1, source_target_pairs={{0,1},{1,0},{2,3},{3,2},{4,5},{5,4},{6,7},{7,6},{8,9},{9,8},{10,11... | collective-permute-start | bytes 811016 | tf_op jit(solution)/shard_map/ppermute | solution.py:200
  21.5 1.3 %shard_map.61.sum_in = f32[512,768]{1,0:T(8,128)S(1)} custom-call(f32[1]{0:T(128)S(6)} %copy.16.scale_ref, f32[1]{0:T(128)S(6)} %copy.17.offset_ref, bf16[512,768]{1,0:T(8,128)(2,1)S(1)} %get-tuple-element.25.low_ref, f32[512,768]{1,0:T(8,128)S(1)} %get-tuple-element.27.sum_in, ...), custom_call_target="tpu_custom_call", output_to_operand_aliasing={{}: (3, {})} | custom-call | flops 400000000 | bytes 1024 | tf_op jit(solution)/shard_map/pallas_call | solution.py:141
  22.8 0.6 %collective-permute-done.3.rest_0_ = bf16[176,768]{1,0:T(8,128)(2,1)S(1)} collective-permute-done((bf16[176,768]{1,0:T(8,128)(2,1)S(1)}, bf16[176,768]{1,0:T(8,128)(2,1)S(1)}, u32[]{:S(2)}, u32[]{:S(2)}) %collective-permute-start.3) | collective-permute-done | bytes 270368 | tf_op jit(solution)/shard_map/ppermute | solution.py:200
  23.4 2.0 %collective-permute-start.6 = (bf16[176,768]{1,0:T(8,128)(2,1)S(1)}, bf16[176,768]{1,0:T(8,128)(2,1)S(1)}, u32[]{:S(2)}, u32[]{:S(2)}) collective-permute-start(bf16[176,768]{1,0:T(8,128)(2,1)S(1)} %collective-permute-done.3.rest_0_), channel_id=1, source_target_pairs={{0,2},{1,31},{2,4},{3,1},{4,6},{5,3},{6,8},{7,5},{8,10},{9,7},{10,... | collective-permute-start | bytes 811016 | tf_op jit(solution)/shard_map/ppermute | solution.py:200
  25.4 1.1 %shard_map.62.sum_ref = f32[512,768]{1,0:T(8,128)S(1)} custom-call(f32[1]{0:T(128)S(6)} %copy.16.scale_ref, f32[1]{0:T(128)S(6)} %copy.17.offset_ref, bf16[512,768]{1,0:T(8,128)(2,1)S(1)} %get-tuple-element.25.low_ref, f32[512,768]{1,0:T(8,128)S(1)} %shard_map.61.sum_in, ...), custom_call_target="tpu_custom_call", output_to_operand_aliasing={{}: (3, {})} | custom-call | flops 400000000 | bytes 1024 | tf_op jit(solution)/shard_map/pallas_call | solution.py:141
  26.5 0.3 shard_map.63
  26.8 0.3 shard_map.65
  27.1 2.1 %collective-permute-done.7.rest_0_ = bf16[176,768]{1,0:T(8,128)(2,1)S(1)} collective-permute-done((bf16[176,768]{1,0:T(8,128)(2,1)S(1)}, bf16[176,768]{1,0:T(8,128)(2,1)S(1)}, u32[]{:S(2)}, u32[]{:S(2)}) %collective-permute-start.7) | collective-permute-done | bytes 270368 | tf_op jit(solution)/shard_map/ppermute | solution.py:200
  29.2 2.0 %collective-permute-start.9 = (bf16[176,768]{1,0:T(8,128)(2,1)S(1)}, bf16[176,768]{1,0:T(8,128)(2,1)S(1)}, u32[]{:S(2)}, u32[]{:S(2)}) collective-permute-start(bf16[176,768]{1,0:T(8,128)(2,1)S(1)} %collective-permute-done.7.rest_0_), channel_id=1, source_target_pairs={{0,2},{1,31},{2,4},{3,1},{4,6},{5,3},{6,8},{7,5},{8,10},{9,7},{10,... | collective-permute-start | bytes 811016 | tf_op jit(solution)/shard_map/ppermute | solution.py:200
  31.2 1.9 %collective-permute-start.10 = (bf16[160,768]{1,0:T(8,128)(2,1)S(1)}, bf16[160,768]{1,0:T(8,128)(2,1)S(1)}, u32[]{:S(2)}, u32[]{:S(2)}) collective-permute-start(bf16[160,768]{1,0:T(8,128)(2,1)S(1)} %slice.15), channel_id=1, source_target_pairs={{0,1},{1,0},{2,3},{3,2},{4,5},{5,4},{6,7},{7,6},{8,9},{9,8},{10,11... | collective-permute-start | bytes 737288 | tf_op jit(solution)/shard_map/ppermute | solution.py:200
  33.1 0.1 collective-permute-start.12
  33.2 1.1 %shard_map.66.sum_in = f32[512,768]{1,0:T(8,128)S(1)} custom-call(f32[1]{0:T(128)S(6)} %copy.16.scale_ref, f32[1]{0:T(128)S(6)} %copy.17.offset_ref, bf16[512,768]{1,0:T(8,128)(2,1)S(1)} %get-tuple-element.38.low_ref, f32[512,768]{1,0:T(8,128)S(1)} %get-tuple-element.39.sum_in, ...), custom_call_target="tpu_custom_call", output_to_operand_aliasing={{}: (3, {})} | custom-call | flops 400000000 | bytes 1024 | tf_op jit(solution)/shard_map/pallas_call | solution.py:141
  34.3 2.7 %collective-permute-start.11 = (bf16[176,768]{1,0:T(8,128)(2,1)S(1)}, bf16[176,768]{1,0:T(8,128)(2,1)S(1)}, u32[]{:S(2)}, u32[]{:S(2)}) collective-permute-start(bf16[176,768]{1,0:T(8,128)(2,1)S(1)} %collective-permute-done.8.rest_0_), channel_id=1, source_target_pairs={{0,2},{1,31},{2,4},{3,1},{4,6},{5,3},{6,8},{7,5},{8,10},{9,7},{10,... | collective-permute-start | bytes 811016 | tf_op jit(solution)/shard_map/ppermute | solution.py:200
  37.0 2.3 %shard_map.64 = f32[512,768]{1,0:T(8,128)} custom-call(f32[1]{0:T(128)S(6)} %copy.16.scale_ref, f32[1]{0:T(128)S(6)} %copy.17.offset_ref, f32[512,768]{1,0:T(8,128)S(1)} %get-tuple-element.31.unit_ref, f32[512,1]{1,0:T(8,128)S(1)} %get-tuple-element.32.recip_ref, bf16[512,768]{1,0:T(8,128)(2,1)S(1)} %get-tuple-element.25.low_ref, ...), custom_call_target="tpu_custom_call" | custom-call | flops 50000000 | bytes 1024 | tf_op jit(solution)/shard_map/pallas_call | solution.py:157
  39.3 0.7 %collective-permute-done.9.rest_1_ = bf16[176,768]{1,0:T(8,128)(2,1)S(1)} collective-permute-done((bf16[176,768]{1,0:T(8,128)(2,1)S(1)}, bf16[176,768]{1,0:T(8,128)(2,1)S(1)}, u32[]{:S(2)}, u32[]{:S(2)}) %collective-permute-start.9) | collective-permute-done | bytes 270368 | tf_op jit(solution)/shard_map/ppermute | solution.py:200
  40.0 1.3 %shard_map.67.sum_in = f32[512,768]{1,0:T(8,128)S(1)} custom-call(f32[1]{0:T(128)S(6)} %copy.16.scale_ref, f32[1]{0:T(128)S(6)} %copy.17.offset_ref, bf16[512,768]{1,0:T(8,128)(2,1)S(1)} %get-tuple-element.38.low_ref, f32[512,768]{1,0:T(8,128)S(1)} %shard_map.66.sum_in, ...), custom_call_target="tpu_custom_call", output_to_operand_aliasing={{}: (3, {})} | custom-call | flops 400000000 | bytes 1024 | tf_op jit(solution)/shard_map/pallas_call | solution.py:141
  41.3 1.1 %shard_map.68.sum_ref = f32[512,768]{1,0:T(8,128)S(1)} custom-call(f32[1]{0:T(128)S(6)} %copy.16.scale_ref, f32[1]{0:T(128)S(6)} %copy.17.offset_ref, bf16[512,768]{1,0:T(8,128)(2,1)S(1)} %get-tuple-element.38.low_ref, f32[512,768]{1,0:T(8,128)S(1)} %shard_map.67.sum_in, ...), custom_call_target="tpu_custom_call", output_to_operand_aliasing={{}: (3, {})} | custom-call | flops 1000000000 | bytes 1024 | tf_op jit(solution)/shard_map/pallas_call | solution.py:141
  42.4 2.0 %collective-permute-done.12.value_ref = bf16[160,768]{1,0:T(8,128)(2,1)S(1)} collective-permute-done((bf16[160,768]{1,0:T(8,128)(2,1)S(1)}, bf16[160,768]{1,0:T(8,128)(2,1)S(1)}, u32[]{:S(2)}, u32[]{:S(2)}) %collective-permute-start.12) | collective-permute-done | bytes 245792 | tf_op jit(solution)/shard_map/ppermute | solution.py:200
  44.4 0.1 shard_map.69.rest_1_
  44.5 1.0 %collective-permute-done.11.rest_0_ = bf16[176,768]{1,0:T(8,128)(2,1)S(1)} collective-permute-done((bf16[176,768]{1,0:T(8,128)(2,1)S(1)}, bf16[176,768]{1,0:T(8,128)(2,1)S(1)}, u32[]{:S(2)}, u32[]{:S(2)}) %collective-permute-start.11) | collective-permute-done | bytes 270368 | tf_op jit(solution)/shard_map/ppermute | solution.py:200
  45.5 2.2 %shard_map.70 = f32[512,768]{1,0:T(8,128)} custom-call(f32[1]{0:T(128)S(6)} %copy.16.scale_ref, f32[1]{0:T(128)S(6)} %copy.17.offset_ref, f32[512,768]{1,0:T(8,128)S(1)} %get-tuple-element.36.unit_ref, f32[512,1]{1,0:T(8,128)S(1)} %get-tuple-element.37.recip_ref, bf16[512,768]{1,0:T(8,128)(2,1)S(1)} %get-tuple-element.38.low_ref, ...), custom_call_target="tpu_custom_call" | custom-call | flops 50000000 | bytes 1024 | tf_op jit(solution)/shard_map/pallas_call | solution.py:157
  (14 shorter events, 0.1 us)
Async XLA Ops:
  0.6 4.3 %copy-start = (bf16[512,768]{1,0:T(8,128)(2,1)S(1)}, bf16[512,768]{1,0:T(8,128)(2,1)}, u32[]{:S(2)}) copy-start(bf16[512,768]{1,0:T(8,128)(2,1)} %value_ref.2) | copy-start | bytes 2359300
  0.6 1.2 %copy-start.1 = (bf16[512,768]{1,0:T(8,128)(2,1)S(1)}, bf16[512,768]{1,0:T(8,128)(2,1)}, u32[]{:S(2)}) copy-start(bf16[512,768]{1,0:T(8,128)(2,1)} %value_ref.3) | copy-start | bytes 2359300
  1.9 10.4 %collective-permute-start.2 = (bf16[176,768]{1,0:T(8,128)(2,1)S(1)}, bf16[176,768]{1,0:T(8,128)(2,1)S(1)}, u32[]{:S(2)}, u32[]{:S(2)}) collective-permute-start(bf16[176,768]{1,0:T(8,128)(2,1)S(1)} %shard_map.60), channel_id=1, source_target_pairs={{0,1},{1,0},{2,3},{3,2},{4,5},{5,4},{6,7},{7,6},{8,9},{9,8},{10,11... | collective-permute-start | bytes 811016 | tf_op jit(solution)/shard_map/ppermute | solution.py:200
  4.9 14.7 %collective-permute-start = (bf16[160,768]{1,0:T(8,128)(2,1)S(1)}, bf16[160,768]{1,0:T(8,128)(2,1)S(1)}, u32[]{:S(2)}, u32[]{:S(2)}) collective-permute-start(bf16[160,768]{1,0:T(8,128)(2,1)S(1)} %slice.15), channel_id=1, source_target_pairs={{0,30},{1,3},{2,0},{3,5},{4,2},{5,7},{6,4},{7,9},{8,6},{9,11},{10,... | collective-permute-start | bytes 737288 | tf_op jit(solution)/shard_map/ppermute | solution.py:200
  8.7 8.9 %collective-permute-start.1 = (bf16[160,768]{1,0:T(8,128)(2,1)S(1)}, bf16[160,768]{1,0:T(8,128)(2,1)S(1)}, u32[]{:S(2)}, u32[]{:S(2)}) collective-permute-start(bf16[160,768]{1,0:T(8,128)(2,1)S(1)} %slice.16), channel_id=1, source_target_pairs={{0,1},{1,0},{2,3},{3,2},{4,5},{5,4},{6,7},{7,6},{8,9},{9,8},{10,11... | collective-permute-start | bytes 737288 | tf_op jit(solution)/shard_map/ppermute | solution.py:200
  8.8 14.6 %collective-permute-start.3 = (bf16[176,768]{1,0:T(8,128)(2,1)S(1)}, bf16[176,768]{1,0:T(8,128)(2,1)S(1)}, u32[]{:S(2)}, u32[]{:S(2)}) collective-permute-start(bf16[176,768]{1,0:T(8,128)(2,1)S(1)} %slice.17), channel_id=1, source_target_pairs={{0,1},{1,0},{2,3},{3,2},{4,5},{5,4},{6,7},{7,6},{8,9},{9,8},{10,11... | collective-permute-start | bytes 811016 | tf_op jit(solution)/shard_map/ppermute | solution.py:200
  10.9 18.2 %collective-permute-start.7 = (bf16[176,768]{1,0:T(8,128)(2,1)S(1)}, bf16[176,768]{1,0:T(8,128)(2,1)S(1)}, u32[]{:S(2)}, u32[]{:S(2)}) collective-permute-start(bf16[176,768]{1,0:T(8,128)(2,1)S(1)} %get-tuple-element.40), channel_id=1, source_target_pairs={{0,1},{1,0},{2,3},{3,2},{4,5},{5,4},{6,7},{7,6},{8,9},{9,8},{10,11... | collective-permute-start | bytes 811016 | tf_op jit(solution)/shard_map/ppermute | solution.py:200
  12.3 11.1 %collective-permute-start.4 = (bf16[176,768]{1,0:T(8,128)(2,1)S(1)}, bf16[176,768]{1,0:T(8,128)(2,1)S(1)}, u32[]{:S(2)}, u32[]{:S(2)}) collective-permute-start(bf16[176,768]{1,0:T(8,128)(2,1)S(1)} %collective-permute-done.2.rest_1_), channel_id=1, source_target_pairs={{0,2},{1,31},{2,4},{3,1},{4,6},{5,3},{6,8},{7,5},{8,10},{9,7},{10,... | collective-permute-start | bytes 811016 | tf_op jit(solution)/shard_map/ppermute | solution.py:200
  17.6 11.6 %collective-permute-start.5 = (bf16[160,768]{1,0:T(8,128)(2,1)S(1)}, bf16[160,768]{1,0:T(8,128)(2,1)S(1)}, u32[]{:S(2)}, u32[]{:S(2)}) collective-permute-start(bf16[160,768]{1,0:T(8,128)(2,1)S(1)} %collective-permute-done.1.rest_0_), channel_id=1, source_target_pairs={{0,2},{1,31},{2,4},{3,1},{4,6},{5,3},{6,8},{7,5},{8,10},{9,7},{10,... | collective-permute-start | bytes 737288 | tf_op jit(solution)/shard_map/ppermute | solution.py:200
  19.6 14.7 %collective-permute-start.8 = (bf16[176,768]{1,0:T(8,128)(2,1)S(1)}, bf16[176,768]{1,0:T(8,128)(2,1)S(1)}, u32[]{:S(2)}, u32[]{:S(2)}) collective-permute-start(bf16[176,768]{1,0:T(8,128)(2,1)S(1)} %get-tuple-element.42), channel_id=1, source_target_pairs={{0,1},{1,0},{2,3},{3,2},{4,5},{5,4},{6,7},{7,6},{8,9},{9,8},{10,11... | collective-permute-start | bytes 811016 | tf_op jit(solution)/shard_map/ppermute | solution.py:200
  23.4 13.6 %collective-permute-start.6 = (bf16[176,768]{1,0:T(8,128)(2,1)S(1)}, bf16[176,768]{1,0:T(8,128)(2,1)S(1)}, u32[]{:S(2)}, u32[]{:S(2)}) collective-permute-start(bf16[176,768]{1,0:T(8,128)(2,1)S(1)} %collective-permute-done.3.rest_0_), channel_id=1, source_target_pairs={{0,2},{1,31},{2,4},{3,1},{4,6},{5,3},{6,8},{7,5},{8,10},{9,7},{10,... | collective-permute-start | bytes 811016 | tf_op jit(solution)/shard_map/ppermute | solution.py:200
  29.2 10.8 %collective-permute-start.9 = (bf16[176,768]{1,0:T(8,128)(2,1)S(1)}, bf16[176,768]{1,0:T(8,128)(2,1)S(1)}, u32[]{:S(2)}, u32[]{:S(2)}) collective-permute-start(bf16[176,768]{1,0:T(8,128)(2,1)S(1)} %collective-permute-done.7.rest_0_), channel_id=1, source_target_pairs={{0,2},{1,31},{2,4},{3,1},{4,6},{5,3},{6,8},{7,5},{8,10},{9,7},{10,... | collective-permute-start | bytes 811016 | tf_op jit(solution)/shard_map/ppermute | solution.py:200
  31.2 10.1 %collective-permute-start.10 = (bf16[160,768]{1,0:T(8,128)(2,1)S(1)}, bf16[160,768]{1,0:T(8,128)(2,1)S(1)}, u32[]{:S(2)}, u32[]{:S(2)}) collective-permute-start(bf16[160,768]{1,0:T(8,128)(2,1)S(1)} %slice.15), channel_id=1, source_target_pairs={{0,1},{1,0},{2,3},{3,2},{4,5},{5,4},{6,7},{7,6},{8,9},{9,8},{10,11... | collective-permute-start | bytes 737288 | tf_op jit(solution)/shard_map/ppermute | solution.py:200
  33.1 11.3 %collective-permute-start.12 = (bf16[160,768]{1,0:T(8,128)(2,1)S(1)}, bf16[160,768]{1,0:T(8,128)(2,1)S(1)}, u32[]{:S(2)}, u32[]{:S(2)}) collective-permute-start(bf16[160,768]{1,0:T(8,128)(2,1)S(1)} %collective-permute-done), channel_id=1, source_target_pairs={{0,1},{1,0},{2,3},{3,2},{4,5},{5,4},{6,7},{7,6},{8,9},{9,8},{10,11... | collective-permute-start | bytes 737288 | tf_op jit(solution)/shard_map/ppermute | solution.py:200
  34.3 11.2 %collective-permute-start.11 = (bf16[176,768]{1,0:T(8,128)(2,1)S(1)}, bf16[176,768]{1,0:T(8,128)(2,1)S(1)}, u32[]{:S(2)}, u32[]{:S(2)}) collective-permute-start(bf16[176,768]{1,0:T(8,128)(2,1)S(1)} %collective-permute-done.8.rest_0_), channel_id=1, source_target_pairs={{0,2},{1,31},{2,4},{3,1},{4,6},{5,3},{6,8},{7,5},{8,10},{9,7},{10,... | collective-permute-start | bytes 811016 | tf_op jit(solution)/shard_map/ppermute | solution.py:200

commit v6 on v5

--- a/solution.py
+++ b/solution.py
@@ -236,17 +236,17 @@
     far1 = exchange(tied(near1, img_low), onward)
     near_tail = exchange(tied(tail, near1), partner)
     far_tail = exchange(tied(side, near1), partner)
-    sum_img = add_call(*args, img_low, tied(sum_img, side), (near1, near0,), 0.4)
+    sum_img = add_call(*args, img_low, tied(sum_img, side), (near1, near0,), 0.2)
     far2 = exchange(tied(near2, sum_img, far0), onward)
-    sum_img = add_call(*args, img_low, sum_img, (near2,), 0.4)
+    sum_img = add_call(*args, img_low, sum_img, (near2,), 0.2)
     unit_img, recip_img = unit_call(tied(images, sum_img))
     unit_txt, recip_txt = unit_call(tied(texts, unit_img))
     far3 = exchange(tied(near3, unit_txt, unit_img, sum_img, far1), onward)
-    sum_txt = add_call(*args, txt_low, sum_txt, (near3,), 0.4)
+    sum_txt = add_call(*args, txt_low, sum_txt, (near3,), 0.2)
     far4 = exchange(tied(near4, sum_txt), onward)
     grad_img = last_call(*args, unit_img, recip_img, img_low, sum_img, (far0, far1, far2), 3, 0.05)
-    sum_txt = add_call(*args, txt_low, tied(sum_txt, grad_img), (near4, far3,), 0.4)
-    sum_txt = add_call(*args, txt_low, sum_txt, (near_tail,), 1.0)
+    sum_txt = add_call(*args, txt_low, tied(sum_txt, grad_img), (near_tail,), 0.3)
+    sum_txt = add_call(*args, txt_low, sum_txt, (near4, far3,), 0.2)
     grad_txt = last_call(*args, unit_txt, recip_txt, txt_low, sum_txt, (far4, low_call(tied(far_tail, sum_txt))), 1, 0.05)
     return grad_img, grad_txt
 

time: 47.8 us -> 47.9 us (level)
  starting transfers between devices: 23.7 us -> 24.8 us
  waiting for transfers between devices: 7.87 us -> 6.86 us
    ppermute x13, starting transfers between devices: 23.7 us -> 24.8 us  [exchange(): lax.ppermute(value, AXES, [(at, target(at) % count) for at in range(count)])]
    ppermute x13, waiting for transfers between devices: 7.87 us -> 6.86 us  [exchange(): lax.ppermute(value, AXES, [(at, target(at) % count) for at in range(count)])]
  transfers between devices with their start and end apart: 13 -> 13, of which waited for: 6 -> 7; matrix products, arithmetic and copies ran while one was open for 0% -> 0% of each run, Pallas kernels for 22% -> 22%
where the time goes in v6:
time: 47.9 us; the launch traced here: 47.8 us
  starting transfers between devices  24.8 us (52%)
  Pallas kernels  12.7 us (27%)
  waiting for transfers between devices  6.86 us (14%)
  between operations  2.08 us (4%)
  local copies, waits for them, and re-layouts  1.29 us (3%)
    ppermute x13, starting transfers between devices, exchange(): lax.ppermute(value, AXES, [(at, target(at) % count) for at in range(count)])  24.8 us
    ppermute x13, waiting for transfers between devices, exchange(): lax.ppermute(value, AXES, [(at, target(at) % count) for at in range(count)])  6.86 us
    pallas_call x5, Pallas kernels, add_call(): pl.pallas_call(functools.partial(add_kernel, len(others)), out_shape=jax....  5.83 us
    pallas_call x2, Pallas kernels, last_call(): pl.pallas_call(functools.partial(last_kernel, len(others), raw_count, blo...  4.43 us
    pallas_call x1, Pallas kernels, own_call(): pl.pallas_call(own_kernel, out_shape=(low, low, total, total), in_specs=[...  1.76 us
    unnamed x4, local copies, waits for them, and re-layouts  1.2 us
  transfers between devices with their start and end apart: 13, of which 7 were waited for; matrix products, arithmetic and copies ran while one was open for 0% of the time, Pallas kernels for 22%

profile of v6, /device:TPU:0, one launch (start us, length us, event | category | flops | bytes accessed | tf_op | source)
XLA Modules:
  0.0 47.8 jit_solution(5237722596728056348)
XLA Ops:
  0.6 1.2 %copy-done.1 = bf16[512,768]{1,0:T(8,128)(2,1)S(1)} copy-done((bf16[512,768]{1,0:T(8,128)(2,1)S(1)}, bf16[512,768]{1,0:T(8,128)(2,1)}, u32[]{:S(2)}) %copy-start.1) | copy-done | bytes 786456
  1.9 3.0 %collective-permute-start.2 = (bf16[176,768]{1,0:T(8,128)(2,1)S(1)}, bf16[176,768]{1,0:T(8,128)(2,1)S(1)}, u32[]{:S(2)}, u32[]{:S(2)}) collective-permute-start(bf16[176,768]{1,0:T(8,128)(2,1)S(1)} %shard_map.60), channel_id=1, source_target_pairs={{0,1},{1,0},{2,3},{3,2},{4,5},{5,4},{6,7},{7,6},{8,9},{9,8},{10,11... | collective-permute-start | bytes 811016 | tf_op jit(solution)/shard_map/ppermute | solution.py:200
  4.9 3.7 %collective-permute-start = (bf16[160,768]{1,0:T(8,128)(2,1)S(1)}, bf16[160,768]{1,0:T(8,128)(2,1)S(1)}, u32[]{:S(2)}, u32[]{:S(2)}) collective-permute-start(bf16[160,768]{1,0:T(8,128)(2,1)S(1)} %slice.15), channel_id=1, source_target_pairs={{0,30},{1,3},{2,0},{3,5},{4,2},{5,7},{6,4},{7,9},{8,6},{9,11},{10,... | collective-permute-start | bytes 737288 | tf_op jit(solution)/shard_map/ppermute | solution.py:200
  8.7 0.1 collective-permute-start.1
  8.8 2.1 %collective-permute-start.3 = (bf16[176,768]{1,0:T(8,128)(2,1)S(1)}, bf16[176,768]{1,0:T(8,128)(2,1)S(1)}, u32[]{:S(2)}, u32[]{:S(2)}) collective-permute-start(bf16[176,768]{1,0:T(8,128)(2,1)S(1)} %slice.17), channel_id=1, source_target_pairs={{0,1},{1,0},{2,3},{3,2},{4,5},{5,4},{6,7},{7,6},{8,9},{9,8},{10,11... | collective-permute-start | bytes 811016 | tf_op jit(solution)/shard_map/ppermute | solution.py:200
  10.9 0.1 collective-permute-start.7
  12.3 2.0 %collective-permute-start.4 = (bf16[176,768]{1,0:T(8,128)(2,1)S(1)}, bf16[176,768]{1,0:T(8,128)(2,1)S(1)}, u32[]{:S(2)}, u32[]{:S(2)}) collective-permute-start(bf16[176,768]{1,0:T(8,128)(2,1)S(1)} %collective-permute-done.2.rest_1_), channel_id=1, source_target_pairs={{0,2},{1,31},{2,4},{3,1},{4,6},{5,3},{6,8},{7,5},{8,10},{9,7},{10,... | collective-permute-start | bytes 811016 | tf_op jit(solution)/shard_map/ppermute | solution.py:200
  14.3 1.8 %shard_map.59 = (bf16[512,768]{1,0:T(8,128)(2,1)S(1)}, bf16[512,768]{1,0:T(8,128)(2,1)S(1)}, f32[512,768]{1,0:T(8,128)S(1)}, f32[512,768]{1,0:T(8,128)S(1)}) custom-call(f32[1]{0:T(128)S(6)} %copy.16.scale_ref, f32[1]{0:T(128)S(6)} %copy.17.offset_ref, bf16[512,768]{1,0:T(8,128)(2,1)S(1)} %copy-done, bf16[512,768]{1,0:T(8,128)(2,1)S(1)} %copy-done.1), custom_call_target="tpu_custom_call" | custom-call | flops 800000000 | bytes 1024 | tf_op jit(solution)/shard_map/pallas_call | solution.py:128
  16.1 1.5 %collective-permute-done.1.rest_0_ = bf16[160,768]{1,0:T(8,128)(2,1)S(1)} collective-permute-done((bf16[160,768]{1,0:T(8,128)(2,1)S(1)}, bf16[160,768]{1,0:T(8,128)(2,1)S(1)}, u32[]{:S(2)}, u32[]{:S(2)}) %collective-permute-start.1) | collective-permute-done | bytes 245792 | tf_op jit(solution)/shard_map/ppermute | solution.py:200
  17.6 2.0 %collective-permute-start.5 = (bf16[160,768]{1,0:T(8,128)(2,1)S(1)}, bf16[160,768]{1,0:T(8,128)(2,1)S(1)}, u32[]{:S(2)}, u32[]{:S(2)}) collective-permute-start(bf16[160,768]{1,0:T(8,128)(2,1)S(1)} %collective-permute-done.1.rest_0_), channel_id=1, source_target_pairs={{0,2},{1,31},{2,4},{3,1},{4,6},{5,3},{6,8},{7,5},{8,10},{9,7},{10,... | collective-permute-start | bytes 737288 | tf_op jit(solution)/shard_map/ppermute | solution.py:200
  19.6 1.9 %collective-permute-start.9 = (bf16[176,768]{1,0:T(8,128)(2,1)S(1)}, bf16[176,768]{1,0:T(8,128)(2,1)S(1)}, u32[]{:S(2)}, u32[]{:S(2)}) collective-permute-start(bf16[176,768]{1,0:T(8,128)(2,1)S(1)} %get-tuple-element.43), channel_id=1, source_target_pairs={{0,1},{1,0},{2,3},{3,2},{4,5},{5,4},{6,7},{7,6},{8,9},{9,8},{10,11... | collective-permute-start | bytes 811016 | tf_op jit(solution)/shard_map/ppermute | solution.py:200
  21.5 1.3 %shard_map.61.sum_in = f32[512,768]{1,0:T(8,128)S(1)} custom-call(f32[1]{0:T(128)S(6)} %copy.16.scale_ref, f32[1]{0:T(128)S(6)} %copy.17.offset_ref, bf16[512,768]{1,0:T(8,128)(2,1)S(1)} %get-tuple-element.25.low_ref, f32[512,768]{1,0:T(8,128)S(1)} %get-tuple-element.27.sum_in, ...), custom_call_target="tpu_custom_call", output_to_operand_aliasing={{}: (3, {})} | custom-call | flops 200000000 | bytes 1024 | tf_op jit(solution)/shard_map/pallas_call | solution.py:141
  22.8 0.6 %collective-permute-done.3.rest_0_ = bf16[176,768]{1,0:T(8,128)(2,1)S(1)} collective-permute-done((bf16[176,768]{1,0:T(8,128)(2,1)S(1)}, bf16[176,768]{1,0:T(8,128)(2,1)S(1)}, u32[]{:S(2)}, u32[]{:S(2)}) %collective-permute-start.3) | collective-permute-done | bytes 270368 | tf_op jit(solution)/shard_map/ppermute | solution.py:200
  23.4 2.0 %collective-permute-start.6 = (bf16[176,768]{1,0:T(8,128)(2,1)S(1)}, bf16[176,768]{1,0:T(8,128)(2,1)S(1)}, u32[]{:S(2)}, u32[]{:S(2)}) collective-permute-start(bf16[176,768]{1,0:T(8,128)(2,1)S(1)} %collective-permute-done.3.rest_0_), channel_id=1, source_target_pairs={{0,2},{1,31},{2,4},{3,1},{4,6},{5,3},{6,8},{7,5},{8,10},{9,7},{10,... | collective-permute-start | bytes 811016 | tf_op jit(solution)/shard_map/ppermute | solution.py:200
  25.4 1.9 %collective-permute-start.8 = (bf16[160,768]{1,0:T(8,128)(2,1)S(1)}, bf16[160,768]{1,0:T(8,128)(2,1)S(1)}, u32[]{:S(2)}, u32[]{:S(2)}) collective-permute-start(bf16[160,768]{1,0:T(8,128)(2,1)S(1)} %slice.15), channel_id=1, source_target_pairs={{0,1},{1,0},{2,3},{3,2},{4,5},{5,4},{6,7},{7,6},{8,9},{9,8},{10,11... | collective-permute-start | bytes 737288 | tf_op jit(solution)/shard_map/ppermute | solution.py:200
  27.3 1.1 %shard_map.62.sum_ref = f32[512,768]{1,0:T(8,128)S(1)} custom-call(f32[1]{0:T(128)S(6)} %copy.16.scale_ref, f32[1]{0:T(128)S(6)} %copy.17.offset_ref, bf16[512,768]{1,0:T(8,128)(2,1)S(1)} %get-tuple-element.25.low_ref, f32[512,768]{1,0:T(8,128)S(1)} %shard_map.61.sum_in, ...), custom_call_target="tpu_custom_call", output_to_operand_aliasing={{}: (3, {})} | custom-call | flops 200000000 | bytes 1024 | tf_op jit(solution)/shard_map/pallas_call | solution.py:141
  28.4 0.3 shard_map.63
  28.7 0.3 shard_map.65
  28.9 0.2 collective-permute-done.7.rest_0_
  29.2 2.0 %collective-permute-start.10 = (bf16[176,768]{1,0:T(8,128)(2,1)S(1)}, bf16[176,768]{1,0:T(8,128)(2,1)S(1)}, u32[]{:S(2)}, u32[]{:S(2)}) collective-permute-start(bf16[176,768]{1,0:T(8,128)(2,1)S(1)} %collective-permute-done.7.rest_0_), channel_id=1, source_target_pairs={{0,2},{1,31},{2,4},{3,1},{4,6},{5,3},{6,8},{7,5},{8,10},{9,7},{10,... | collective-permute-start | bytes 811016 | tf_op jit(solution)/shard_map/ppermute | solution.py:200
  31.2 1.9 %collective-permute-start.12 = (bf16[160,768]{1,0:T(8,128)(2,1)S(1)}, bf16[160,768]{1,0:T(8,128)(2,1)S(1)}, u32[]{:S(2)}, u32[]{:S(2)}) collective-permute-start(bf16[160,768]{1,0:T(8,128)(2,1)S(1)} %collective-permute-done), channel_id=1, source_target_pairs={{0,1},{1,0},{2,3},{3,2},{4,5},{5,4},{6,7},{7,6},{8,9},{9,8},{10,11... | collective-permute-start | bytes 737288 | tf_op jit(solution)/shard_map/ppermute | solution.py:200
  33.1 1.1 %shard_map.66.sum_in = f32[512,768]{1,0:T(8,128)S(1)} custom-call(f32[1]{0:T(128)S(6)} %copy.16.scale_ref, f32[1]{0:T(128)S(6)} %copy.17.offset_ref, bf16[512,768]{1,0:T(8,128)(2,1)S(1)} %get-tuple-element.38.low_ref, f32[512,768]{1,0:T(8,128)S(1)} %get-tuple-element.39.sum_in, ...), custom_call_target="tpu_custom_call", output_to_operand_aliasing={{}: (3, {})} | custom-call | flops 200000000 | bytes 1024 | tf_op jit(solution)/shard_map/pallas_call | solution.py:141
  34.2 0.8 %collective-permute-done.9.rest_0_ = bf16[176,768]{1,0:T(8,128)(2,1)S(1)} collective-permute-done((bf16[176,768]{1,0:T(8,128)(2,1)S(1)}, bf16[176,768]{1,0:T(8,128)(2,1)S(1)}, u32[]{:S(2)}, u32[]{:S(2)}) %collective-permute-start.9) | collective-permute-done | bytes 270368 | tf_op jit(solution)/shard_map/ppermute | solution.py:200
  35.0 2.0 %collective-permute-start.11 = (bf16[176,768]{1,0:T(8,128)(2,1)S(1)}, bf16[176,768]{1,0:T(8,128)(2,1)S(1)}, u32[]{:S(2)}, u32[]{:S(2)}) collective-permute-start(bf16[176,768]{1,0:T(8,128)(2,1)S(1)} %collective-permute-done.9.rest_0_), channel_id=1, source_target_pairs={{0,2},{1,31},{2,4},{3,1},{4,6},{5,3},{6,8},{7,5},{8,10},{9,7},{10,... | collective-permute-start | bytes 811016 | tf_op jit(solution)/shard_map/ppermute | solution.py:200
  37.0 2.3 %shard_map.64 = f32[512,768]{1,0:T(8,128)} custom-call(f32[1]{0:T(128)S(6)} %copy.16.scale_ref, f32[1]{0:T(128)S(6)} %copy.17.offset_ref, f32[512,768]{1,0:T(8,128)S(1)} %get-tuple-element.31.unit_ref, f32[512,1]{1,0:T(8,128)S(1)} %get-tuple-element.32.recip_ref, bf16[512,768]{1,0:T(8,128)(2,1)S(1)} %get-tuple-element.25.low_ref, ...), custom_call_target="tpu_custom_call" | custom-call | flops 50000000 | bytes 1024 | tf_op jit(solution)/shard_map/pallas_call | solution.py:157
  39.3 1.0 %collective-permute-done.8.rest_0_ = bf16[160,768]{1,0:T(8,128)(2,1)S(1)} collective-permute-done((bf16[160,768]{1,0:T(8,128)(2,1)S(1)}, bf16[160,768]{1,0:T(8,128)(2,1)S(1)}, u32[]{:S(2)}, u32[]{:S(2)}) %collective-permute-start.8) | collective-permute-done | bytes 245792 | tf_op jit(solution)/shard_map/ppermute | solution.py:200
  40.2 1.1 %shard_map.67.sum_in = f32[512,768]{1,0:T(8,128)S(1)} custom-call(f32[1]{0:T(128)S(6)} %copy.16.scale_ref, f32[1]{0:T(128)S(6)} %copy.17.offset_ref, bf16[512,768]{1,0:T(8,128)(2,1)S(1)} %get-tuple-element.38.low_ref, f32[512,768]{1,0:T(8,128)S(1)} %shard_map.66.sum_in, ...), custom_call_target="tpu_custom_call", output_to_operand_aliasing={{}: (3, {})} | custom-call | flops 300000000 | bytes 1024 | tf_op jit(solution)/shard_map/pallas_call | solution.py:141
  41.3 1.3 %shard_map.68.sum_ref = f32[512,768]{1,0:T(8,128)S(1)} custom-call(f32[1]{0:T(128)S(6)} %copy.16.scale_ref, f32[1]{0:T(128)S(6)} %copy.17.offset_ref, bf16[512,768]{1,0:T(8,128)(2,1)S(1)} %get-tuple-element.38.low_ref, f32[512,768]{1,0:T(8,128)S(1)} %shard_map.67.sum_in, ...), custom_call_target="tpu_custom_call", output_to_operand_aliasing={{}: (3, {})} | custom-call | flops 200000000 | bytes 1024 | tf_op jit(solution)/shard_map/pallas_call | solution.py:141
  42.6 1.9 %collective-permute-done.12.value_ref = bf16[160,768]{1,0:T(8,128)(2,1)S(1)} collective-permute-done((bf16[160,768]{1,0:T(8,128)(2,1)S(1)}, bf16[160,768]{1,0:T(8,128)(2,1)S(1)}, u32[]{:S(2)}, u32[]{:S(2)}) %collective-permute-start.12) | collective-permute-done | bytes 245792 | tf_op jit(solution)/shard_map/ppermute | solution.py:200
  44.6 0.1 shard_map.69.rest_1_
  44.7 0.9 %collective-permute-done.11.rest_0_ = bf16[176,768]{1,0:T(8,128)(2,1)S(1)} collective-permute-done((bf16[176,768]{1,0:T(8,128)(2,1)S(1)}, bf16[176,768]{1,0:T(8,128)(2,1)S(1)}, u32[]{:S(2)}, u32[]{:S(2)}) %collective-permute-start.11) | collective-permute-done | bytes 270368 | tf_op jit(solution)/shard_map/ppermute | solution.py:200
  45.6 2.2 %shard_map.70 = f32[512,768]{1,0:T(8,128)} custom-call(f32[1]{0:T(128)S(6)} %copy.16.scale_ref, f32[1]{0:T(128)S(6)} %copy.17.offset_ref, f32[512,768]{1,0:T(8,128)S(1)} %get-tuple-element.36.unit_ref, f32[512,1]{1,0:T(8,128)S(1)} %get-tuple-element.37.recip_ref, bf16[512,768]{1,0:T(8,128)(2,1)S(1)} %get-tuple-element.38.low_ref, ...), custom_call_target="tpu_custom_call" | custom-call | flops 50000000 | bytes 1024 | tf_op jit(solution)/shard_map/pallas_call | solution.py:157
  (14 shorter events, 0.1 us)
Async XLA Ops:
  0.6 4.3 %copy-start = (bf16[512,768]{1,0:T(8,128)(2,1)S(1)}, bf16[512,768]{1,0:T(8,128)(2,1)}, u32[]{:S(2)}) copy-start(bf16[512,768]{1,0:T(8,128)(2,1)} %value_ref.2) | copy-start | bytes 2359300
  0.6 1.2 %copy-start.1 = (bf16[512,768]{1,0:T(8,128)(2,1)S(1)}, bf16[512,768]{1,0:T(8,128)(2,1)}, u32[]{:S(2)}) copy-start(bf16[512,768]{1,0:T(8,128)(2,1)} %value_ref.3) | copy-start | bytes 2359300
  1.9 10.4 %collective-permute-start.2 = (bf16[176,768]{1,0:T(8,128)(2,1)S(1)}, bf16[176,768]{1,0:T(8,128)(2,1)S(1)}, u32[]{:S(2)}, u32[]{:S(2)}) collective-permute-start(bf16[176,768]{1,0:T(8,128)(2,1)S(1)} %shard_map.60), channel_id=1, source_target_pairs={{0,1},{1,0},{2,3},{3,2},{4,5},{5,4},{6,7},{7,6},{8,9},{9,8},{10,11... | collective-permute-start | bytes 811016 | tf_op jit(solution)/shard_map/ppermute | solution.py:200
  4.9 14.7 %collective-permute-start = (bf16[160,768]{1,0:T(8,128)(2,1)S(1)}, bf16[160,768]{1,0:T(8,128)(2,1)S(1)}, u32[]{:S(2)}, u32[]{:S(2)}) collective-permute-start(bf16[160,768]{1,0:T(8,128)(2,1)S(1)} %slice.15), channel_id=1, source_target_pairs={{0,30},{1,3},{2,0},{3,5},{4,2},{5,7},{6,4},{7,9},{8,6},{9,11},{10,... | collective-permute-start | bytes 737288 | tf_op jit(solution)/shard_map/ppermute | solution.py:200
  8.7 8.9 %collective-permute-start.1 = (bf16[160,768]{1,0:T(8,128)(2,1)S(1)}, bf16[160,768]{1,0:T(8,128)(2,1)S(1)}, u32[]{:S(2)}, u32[]{:S(2)}) collective-permute-start(bf16[160,768]{1,0:T(8,128)(2,1)S(1)} %slice.16), channel_id=1, source_target_pairs={{0,1},{1,0},{2,3},{3,2},{4,5},{5,4},{6,7},{7,6},{8,9},{9,8},{10,11... | collective-permute-start | bytes 737288 | tf_op jit(solution)/shard_map/ppermute | solution.py:200
  8.8 14.6 %collective-permute-start.3 = (bf16[176,768]{1,0:T(8,128)(2,1)S(1)}, bf16[176,768]{1,0:T(8,128)(2,1)S(1)}, u32[]{:S(2)}, u32[]{:S(2)}) collective-permute-start(bf16[176,768]{1,0:T(8,128)(2,1)S(1)} %slice.17), channel_id=1, source_target_pairs={{0,1},{1,0},{2,3},{3,2},{4,5},{5,4},{6,7},{7,6},{8,9},{9,8},{10,11... | collective-permute-start | bytes 811016 | tf_op jit(solution)/shard_map/ppermute | solution.py:200
  10.9 18.2 %collective-permute-start.7 = (bf16[176,768]{1,0:T(8,128)(2,1)S(1)}, bf16[176,768]{1,0:T(8,128)(2,1)S(1)}, u32[]{:S(2)}, u32[]{:S(2)}) collective-permute-start(bf16[176,768]{1,0:T(8,128)(2,1)S(1)} %get-tuple-element.40), channel_id=1, source_target_pairs={{0,1},{1,0},{2,3},{3,2},{4,5},{5,4},{6,7},{7,6},{8,9},{9,8},{10,11... | collective-permute-start | bytes 811016 | tf_op jit(solution)/shard_map/ppermute | solution.py:200
  12.3 11.1 %collective-permute-start.4 = (bf16[176,768]{1,0:T(8,128)(2,1)S(1)}, bf16[176,768]{1,0:T(8,128)(2,1)S(1)}, u32[]{:S(2)}, u32[]{:S(2)}) collective-permute-start(bf16[176,768]{1,0:T(8,128)(2,1)S(1)} %collective-permute-done.2.rest_1_), channel_id=1, source_target_pairs={{0,2},{1,31},{2,4},{3,1},{4,6},{5,3},{6,8},{7,5},{8,10},{9,7},{10,... | collective-permute-start | bytes 811016 | tf_op jit(solution)/shard_map/ppermute | solution.py:200
  17.6 11.6 %collective-permute-start.5 = (bf16[160,768]{1,0:T(8,128)(2,1)S(1)}, bf16[160,768]{1,0:T(8,128)(2,1)S(1)}, u32[]{:S(2)}, u32[]{:S(2)}) collective-permute-start(bf16[160,768]{1,0:T(8,128)(2,1)S(1)} %collective-permute-done.1.rest_0_), channel_id=1, source_target_pairs={{0,2},{1,31},{2,4},{3,1},{4,6},{5,3},{6,8},{7,5},{8,10},{9,7},{10,... | collective-permute-start | bytes 737288 | tf_op jit(solution)/shard_map/ppermute | solution.py:200
  19.6 15.4 %collective-permute-start.9 = (bf16[176,768]{1,0:T(8,128)(2,1)S(1)}, bf16[176,768]{1,0:T(8,128)(2,1)S(1)}, u32[]{:S(2)}, u32[]{:S(2)}) collective-permute-start(bf16[176,768]{1,0:T(8,128)(2,1)S(1)} %get-tuple-element.43), channel_id=1, source_target_pairs={{0,1},{1,0},{2,3},{3,2},{4,5},{5,4},{6,7},{7,6},{8,9},{9,8},{10,11... | collective-permute-start | bytes 811016 | tf_op jit(solution)/shard_map/ppermute | solution.py:200
  23.4 13.6 %collective-permute-start.6 = (bf16[176,768]{1,0:T(8,128)(2,1)S(1)}, bf16[176,768]{1,0:T(8,128)(2,1)S(1)}, u32[]{:S(2)}, u32[]{:S(2)}) collective-permute-start(bf16[176,768]{1,0:T(8,128)(2,1)S(1)} %collective-permute-done.3.rest_0_), channel_id=1, source_target_pairs={{0,2},{1,31},{2,4},{3,1},{4,6},{5,3},{6,8},{7,5},{8,10},{9,7},{10,... | collective-permute-start | bytes 811016 | tf_op jit(solution)/shard_map/ppermute | solution.py:200
  25.4 14.8 %collective-permute-start.8 = (bf16[160,768]{1,0:T(8,128)(2,1)S(1)}, bf16[160,768]{1,0:T(8,128)(2,1)S(1)}, u32[]{:S(2)}, u32[]{:S(2)}) collective-permute-start(bf16[160,768]{1,0:T(8,128)(2,1)S(1)} %slice.15), channel_id=1, source_target_pairs={{0,1},{1,0},{2,3},{3,2},{4,5},{5,4},{6,7},{7,6},{8,9},{9,8},{10,11... | collective-permute-start | bytes 737288 | tf_op jit(solution)/shard_map/ppermute | solution.py:200
  29.2 12.1 %collective-permute-start.10 = (bf16[176,768]{1,0:T(8,128)(2,1)S(1)}, bf16[176,768]{1,0:T(8,128)(2,1)S(1)}, u32[]{:S(2)}, u32[]{:S(2)}) collective-permute-start(bf16[176,768]{1,0:T(8,128)(2,1)S(1)} %collective-permute-done.7.rest_0_), channel_id=1, source_target_pairs={{0,2},{1,31},{2,4},{3,1},{4,6},{5,3},{6,8},{7,5},{8,10},{9,7},{10,... | collective-permute-start | bytes 811016 | tf_op jit(solution)/shard_map/ppermute | solution.py:200
  31.2 13.4 %collective-permute-start.12 = (bf16[160,768]{1,0:T(8,128)(2,1)S(1)}, bf16[160,768]{1,0:T(8,128)(2,1)S(1)}, u32[]{:S(2)}, u32[]{:S(2)}) collective-permute-start(bf16[160,768]{1,0:T(8,128)(2,1)S(1)} %collective-permute-done), channel_id=1, source_target_pairs={{0,1},{1,0},{2,3},{3,2},{4,5},{5,4},{6,7},{7,6},{8,9},{9,8},{10,11... | collective-permute-start | bytes 737288 | tf_op jit(solution)/shard_map/ppermute | solution.py:200
  35.0 10.6 %collective-permute-start.11 = (bf16[176,768]{1,0:T(8,128)(2,1)S(1)}, bf16[176,768]{1,0:T(8,128)(2,1)S(1)}, u32[]{:S(2)}, u32[]{:S(2)}) collective-permute-start(bf16[176,768]{1,0:T(8,128)(2,1)S(1)} %collective-permute-done.9.rest_0_), channel_id=1, source_target_pairs={{0,2},{1,31},{2,4},{3,1},{4,6},{5,3},{6,8},{7,5},{8,10},{9,7},{10,... | collective-permute-start | bytes 811016 | tf_op jit(solution)/shard_map/ppermute | solution.py:200

commit v7 on v5

--- a/solution.py
+++ b/solution.py
@@ -68,17 +68,10 @@
     unit_ref[...], recip_ref[...] = unit_rows(value_ref[...])
 
 
-def low_kernel(value_ref, low_ref):
-    low_ref[...] = unit_rows(value_ref[...])[0].astype(jnp.bfloat16)
-
-
-def last_kernel(count, raw_count, blocks, scale_ref, offset_ref, unit_ref, recip_ref, low_ref, sum_ref, *rest):
+def last_kernel(count, blocks, scale_ref, offset_ref, unit_ref, recip_ref, low_ref, sum_ref, *rest):
     others, (out_ref, other_low, held, sems) = rest[:count], rest[count:]
     scale, offset = scale_ref[0], offset_ref[0]
-    lower_rows(others[:raw_count], other_low)
-    if count > raw_count:
-        at = sum(other.shape[0] for other in others[:raw_count])
-        other_low[at:, :] = others[-1][...]
+    lower_rows(others, other_low)
     logits = scale * dot32(low_ref[...], other_low[...], LAST) + offset
     weight = jax.nn.sigmoid(logits).astype(jnp.bfloat16)
     size = held.shape[0] // blocks
@@ -150,12 +143,12 @@
     )(scale, offset, low, total, *others)
 
 
-def last_call(scale, offset, unit, recip, low, total, others, raw_count, micros):
+def last_call(scale, offset, unit, recip, low, total, others, micros):
     rows, width = unit.shape
     count = sum(other.shape[0] for other in others)
     blocks = 4 if rows % 64 == 0 else 1
     return pl.pallas_call(
-        functools.partial(last_kernel, len(others), raw_count, blocks),
+        functools.partial(last_kernel, len(others), blocks),
         out_shape=jax.ShapeDtypeStruct((rows, width), jnp.float32),
         in_specs=[SMEM, SMEM] + [VMEM] * (4 + len(others)),
         out_specs=pl.BlockSpec(memory_space=pl.ANY),
@@ -181,17 +174,6 @@
         out_specs=(VMEM, VMEM),
         compiler_params=PARAMS,
         cost_estimate=cost(0.05),
-    )(value)
-
-
-def low_call(value):
-    return pl.pallas_call(
-        low_kernel,
-        out_shape=jax.ShapeDtypeStruct(value.shape, jnp.bfloat16),
-        in_specs=[VMEM],
-        out_specs=VMEM,
-        compiler_params=PARAMS,
-        cost_estimate=cost(0.3),
     )(value)
 
 
@@ -244,10 +226,10 @@
     far3 = exchange(tied(near3, unit_txt, unit_img, sum_img, far1), onward)
     sum_txt = add_call(*args, txt_low, sum_txt, (near3,), 0.4)
     far4 = exchange(tied(near4, sum_txt), onward)
-    grad_img = last_call(*args, unit_img, recip_img, img_low, sum_img, (far0, far1, far2), 3, 0.05)
+    grad_img = last_call(*args, unit_img, recip_img, img_low, sum_img, (far0, far1, far2,), 0.05)
     sum_txt = add_call(*args, txt_low, tied(sum_txt, grad_img), (near4, far3,), 0.4)
     sum_txt = add_call(*args, txt_low, sum_txt, (near_tail,), 1.0)
-    grad_txt = last_call(*args, unit_txt, recip_txt, txt_low, sum_txt, (far4, low_call(tied(far_tail, sum_txt))), 1, 0.05)
+    grad_txt = last_call(*args, unit_txt, recip_txt, txt_low, sum_txt, (far4, far_tail), 0.05)
     return grad_img, grad_txt
 
 

time: 47.8 us -> 47.8 us (level)
  starting transfers between devices: 23.7 us -> 25.6 us
  waiting for transfers between devices: 7.87 us -> 6.14 us
    ppermute x13, starting transfers between devices: 23.7 us -> 25.6 us  [exchange(): lax.ppermute(value, AXES, [(at, target(at) % count) for at in range(count)])]
    ppermute x13, waiting for transfers between devices: 7.87 us -> 6.14 us  [exchange(): lax.ppermute(value, AXES, [(at, target(at) % count) for at in range(count)])]
    pallas_call x3 -> x2, Pallas kernels: 4.56 us -> 4.4 us  [last_call(): pl.pallas_call(functools.partial(last_kernel, len(others), blocks), out_s...]
  transfers between devices with their start and end apart: 13 -> 13, of which waited for: 6 -> 5; matrix products, arithmetic and copies ran while one was open for 0% -> 0% of each run, Pallas kernels for 22% -> 22%
where the time goes in v7:
time: 47.8 us; the launch traced here: 47.7 us
  starting transfers between devices  25.6 us (54%)
  Pallas kernels  12.6 us (26%)
  waiting for transfers between devices  6.14 us (13%)
  between operations  2.09 us (4%)
  local copies, waits for them, and re-layouts  1.29 us (3%)
    ppermute x13, starting transfers between devices, exchange(): lax.ppermute(value, AXES, [(at, target(at) % count) for at in range(count)])  25.6 us
    ppermute x13, waiting for transfers between devices, exchange(): lax.ppermute(value, AXES, [(at, target(at) % count) for at in range(count)])  6.14 us
    pallas_call x5, Pallas kernels, add_call(): pl.pallas_call(functools.partial(add_kernel, len(others)), out_shape=jax....  5.83 us
    pallas_call x2, Pallas kernels, last_call(): pl.pallas_call(functools.partial(last_kernel, len(others), blocks), out_s...  4.4 us
    pallas_call x1, Pallas kernels, own_call(): pl.pallas_call(own_kernel, out_shape=(low, low, total, total), in_specs=[...  1.76 us
    unnamed x4, local copies, waits for them, and re-layouts  1.2 us
  transfers between devices with their start and end apart: 13, of which 5 were waited for; matrix products, arithmetic and copies ran while one was open for 0% of the time, Pallas kernels for 22%

profile of v7, /device:TPU:0, one launch (start us, length us, event | category | flops | bytes accessed | tf_op | source)
XLA Modules:
  0.0 47.7 jit_solution(16442664120494126078)
XLA Ops:
  0.6 1.2 %copy-done.1 = bf16[512,768]{1,0:T(8,128)(2,1)S(1)} copy-done((bf16[512,768]{1,0:T(8,128)(2,1)S(1)}, bf16[512,768]{1,0:T(8,128)(2,1)}, u32[]{:S(2)}) %copy-start.1) | copy-done | bytes 786456
  1.9 3.0 %collective-permute-start.2 = (bf16[176,768]{1,0:T(8,128)(2,1)S(1)}, bf16[176,768]{1,0:T(8,128)(2,1)S(1)}, u32[]{:S(2)}, u32[]{:S(2)}) collective-permute-start(bf16[176,768]{1,0:T(8,128)(2,1)S(1)} %shard_map.60), channel_id=1, source_target_pairs={{0,1},{1,0},{2,3},{3,2},{4,5},{5,4},{6,7},{7,6},{8,9},{9,8},{10,11... | collective-permute-start | bytes 811016 | tf_op jit(solution)/shard_map/ppermute | solution.py:182
  4.9 3.7 %collective-permute-start = (bf16[160,768]{1,0:T(8,128)(2,1)S(1)}, bf16[160,768]{1,0:T(8,128)(2,1)S(1)}, u32[]{:S(2)}, u32[]{:S(2)}) collective-permute-start(bf16[160,768]{1,0:T(8,128)(2,1)S(1)} %slice.15), channel_id=1, source_target_pairs={{0,30},{1,3},{2,0},{3,5},{4,2},{5,7},{6,4},{7,9},{8,6},{9,11},{10,... | collective-permute-start | bytes 737288 | tf_op jit(solution)/shard_map/ppermute | solution.py:182
  8.7 0.1 collective-permute-start.1
  8.8 2.1 %collective-permute-start.3 = (bf16[176,768]{1,0:T(8,128)(2,1)S(1)}, bf16[176,768]{1,0:T(8,128)(2,1)S(1)}, u32[]{:S(2)}, u32[]{:S(2)}) collective-permute-start(bf16[176,768]{1,0:T(8,128)(2,1)S(1)} %slice.17), channel_id=1, source_target_pairs={{0,1},{1,0},{2,3},{3,2},{4,5},{5,4},{6,7},{7,6},{8,9},{9,8},{10,11... | collective-permute-start | bytes 811016 | tf_op jit(solution)/shard_map/ppermute | solution.py:182
  10.9 0.1 collective-permute-start.7
  12.3 2.0 %collective-permute-start.4 = (bf16[176,768]{1,0:T(8,128)(2,1)S(1)}, bf16[176,768]{1,0:T(8,128)(2,1)S(1)}, u32[]{:S(2)}, u32[]{:S(2)}) collective-permute-start(bf16[176,768]{1,0:T(8,128)(2,1)S(1)} %collective-permute-done.2.rest_1_), channel_id=1, source_target_pairs={{0,2},{1,31},{2,4},{3,1},{4,6},{5,3},{6,8},{7,5},{8,10},{9,7},{10,... | collective-permute-start | bytes 811016 | tf_op jit(solution)/shard_map/ppermute | solution.py:182
  14.3 1.8 %shard_map.59 = (bf16[512,768]{1,0:T(8,128)(2,1)S(1)}, bf16[512,768]{1,0:T(8,128)(2,1)S(1)}, f32[512,768]{1,0:T(8,128)S(1)}, f32[512,768]{1,0:T(8,128)S(1)}) custom-call(f32[1]{0:T(128)S(6)} %copy.16.scale_ref, f32[1]{0:T(128)S(6)} %copy.17.offset_ref, bf16[512,768]{1,0:T(8,128)(2,1)S(1)} %copy-done, bf16[512,768]{1,0:T(8,128)(2,1)S(1)} %copy-done.1), custom_call_target="tpu_custom_call" | custom-call | flops 800000000 | bytes 1024 | tf_op jit(solution)/shard_map/pallas_call | solution.py:121
  16.1 1.5 %collective-permute-done.1.rest_0_ = bf16[160,768]{1,0:T(8,128)(2,1)S(1)} collective-permute-done((bf16[160,768]{1,0:T(8,128)(2,1)S(1)}, bf16[160,768]{1,0:T(8,128)(2,1)S(1)}, u32[]{:S(2)}, u32[]{:S(2)}) %collective-permute-start.1) | collective-permute-done | bytes 245792 | tf_op jit(solution)/shard_map/ppermute | solution.py:182
  17.6 2.0 %collective-permute-start.5 = (bf16[160,768]{1,0:T(8,128)(2,1)S(1)}, bf16[160,768]{1,0:T(8,128)(2,1)S(1)}, u32[]{:S(2)}, u32[]{:S(2)}) collective-permute-start(bf16[160,768]{1,0:T(8,128)(2,1)S(1)} %collective-permute-done.1.rest_0_), channel_id=1, source_target_pairs={{0,2},{1,31},{2,4},{3,1},{4,6},{5,3},{6,8},{7,5},{8,10},{9,7},{10,... | collective-permute-start | bytes 737288 | tf_op jit(solution)/shard_map/ppermute | solution.py:182
  19.6 0.0 collective-permute-done
  19.6 1.9 %collective-permute-start.8 = (bf16[176,768]{1,0:T(8,128)(2,1)S(1)}, bf16[176,768]{1,0:T(8,128)(2,1)S(1)}, u32[]{:S(2)}, u32[]{:S(2)}) collective-permute-start(bf16[176,768]{1,0:T(8,128)(2,1)S(1)} %get-tuple-element.41), channel_id=1, source_target_pairs={{0,1},{1,0},{2,3},{3,2},{4,5},{5,4},{6,7},{7,6},{8,9},{9,8},{10,11... | collective-permute-start | bytes 811016 | tf_op jit(solution)/shard_map/ppermute | solution.py:182
  21.5 1.3 %shard_map.61.sum_in = f32[512,768]{1,0:T(8,128)S(1)} custom-call(f32[1]{0:T(128)S(6)} %copy.16.scale_ref, f32[1]{0:T(128)S(6)} %copy.17.offset_ref, bf16[512,768]{1,0:T(8,128)(2,1)S(1)} %get-tuple-element.24.low_ref, f32[512,768]{1,0:T(8,128)S(1)} %get-tuple-element.26.sum_in, ...), custom_call_target="tpu_custom_call", output_to_operand_aliasing={{}: (3, {})} | custom-call | flops 400000000 | bytes 1024 | tf_op jit(solution)/shard_map/pallas_call | solution.py:134
  22.8 0.6 %collective-permute-done.3.rest_0_ = bf16[176,768]{1,0:T(8,128)(2,1)S(1)} collective-permute-done((bf16[176,768]{1,0:T(8,128)(2,1)S(1)}, bf16[176,768]{1,0:T(8,128)(2,1)S(1)}, u32[]{:S(2)}, u32[]{:S(2)}) %collective-permute-start.3) | collective-permute-done | bytes 270368 | tf_op jit(solution)/shard_map/ppermute | solution.py:182
  23.4 2.0 %collective-permute-start.6 = (bf16[176,768]{1,0:T(8,128)(2,1)S(1)}, bf16[176,768]{1,0:T(8,128)(2,1)S(1)}, u32[]{:S(2)}, u32[]{:S(2)}) collective-permute-start(bf16[176,768]{1,0:T(8,128)(2,1)S(1)} %collective-permute-done.3.rest_0_), channel_id=1, source_target_pairs={{0,2},{1,31},{2,4},{3,1},{4,6},{5,3},{6,8},{7,5},{8,10},{9,7},{10,... | collective-permute-start | bytes 811016 | tf_op jit(solution)/shard_map/ppermute | solution.py:182
  25.4 1.1 %shard_map.62.sum_ref = f32[512,768]{1,0:T(8,128)S(1)} custom-call(f32[1]{0:T(128)S(6)} %copy.16.scale_ref, f32[1]{0:T(128)S(6)} %copy.17.offset_ref, bf16[512,768]{1,0:T(8,128)(2,1)S(1)} %get-tuple-element.24.low_ref, f32[512,768]{1,0:T(8,128)S(1)} %shard_map.61.sum_in, ...), custom_call_target="tpu_custom_call", output_to_operand_aliasing={{}: (3, {})} | custom-call | flops 400000000 | bytes 1024 | tf_op jit(solution)/shard_map/pallas_call | solution.py:134
  26.5 0.3 shard_map.63
  26.8 0.3 shard_map.65
  27.1 2.1 %collective-permute-done.7.rest_0_ = bf16[176,768]{1,0:T(8,128)(2,1)S(1)} collective-permute-done((bf16[176,768]{1,0:T(8,128)(2,1)S(1)}, bf16[176,768]{1,0:T(8,128)(2,1)S(1)}, u32[]{:S(2)}, u32[]{:S(2)}) %collective-permute-start.7) | collective-permute-done | bytes 270368 | tf_op jit(solution)/shard_map/ppermute | solution.py:182
  29.2 0.0 collective-permute-done.5.rest_1_
  29.2 2.0 %collective-permute-start.9 = (bf16[176,768]{1,0:T(8,128)(2,1)S(1)}, bf16[176,768]{1,0:T(8,128)(2,1)S(1)}, u32[]{:S(2)}, u32[]{:S(2)}) collective-permute-start(bf16[176,768]{1,0:T(8,128)(2,1)S(1)} %collective-permute-done.7.rest_0_), channel_id=1, source_target_pairs={{0,2},{1,31},{2,4},{3,1},{4,6},{5,3},{6,8},{7,5},{8,10},{9,7},{10,... | collective-permute-start | bytes 811016 | tf_op jit(solution)/shard_map/ppermute | solution.py:182
  31.2 1.9 %collective-permute-start.10 = (bf16[160,768]{1,0:T(8,128)(2,1)S(1)}, bf16[160,768]{1,0:T(8,128)(2,1)S(1)}, u32[]{:S(2)}, u32[]{:S(2)}) collective-permute-start(bf16[160,768]{1,0:T(8,128)(2,1)S(1)} %slice.15), channel_id=1, source_target_pairs={{0,1},{1,0},{2,3},{3,2},{4,5},{5,4},{6,7},{7,6},{8,9},{9,8},{10,11... | collective-permute-start | bytes 737288 | tf_op jit(solution)/shard_map/ppermute | solution.py:182
  33.1 1.1 %shard_map.66.sum_in = f32[512,768]{1,0:T(8,128)S(1)} custom-call(f32[1]{0:T(128)S(6)} %copy.16.scale_ref, f32[1]{0:T(128)S(6)} %copy.17.offset_ref, bf16[512,768]{1,0:T(8,128)(2,1)S(1)} %get-tuple-element.37.low_ref, f32[512,768]{1,0:T(8,128)S(1)} %get-tuple-element.38.sum_in, ...), custom_call_target="tpu_custom_call", output_to_operand_aliasing={{}: (3, {})} | custom-call | flops 400000000 | bytes 1024 | tf_op jit(solution)/shard_map/pallas_call | solution.py:134
  34.2 2.8 %collective-permute-start.11 = (bf16[176,768]{1,0:T(8,128)(2,1)S(1)}, bf16[176,768]{1,0:T(8,128)(2,1)S(1)}, u32[]{:S(2)}, u32[]{:S(2)}) collective-permute-start(bf16[176,768]{1,0:T(8,128)(2,1)S(1)} %collective-permute-done.8.rest_0_), channel_id=1, source_target_pairs={{0,2},{1,31},{2,4},{3,1},{4,6},{5,3},{6,8},{7,5},{8,10},{9,7},{10,... | collective-permute-start | bytes 811016 | tf_op jit(solution)/shard_map/ppermute | solution.py:182
  37.0 1.9 %collective-permute-start.12 = (bf16[160,768]{1,0:T(8,128)(2,1)S(1)}, bf16[160,768]{1,0:T(8,128)(2,1)S(1)}, u32[]{:S(2)}, u32[]{:S(2)}) collective-permute-start(bf16[160,768]{1,0:T(8,128)(2,1)S(1)} %collective-permute-done), channel_id=1, source_target_pairs={{0,1},{1,0},{2,3},{3,2},{4,5},{5,4},{6,7},{7,6},{8,9},{9,8},{10,11... | collective-permute-start | bytes 737288 | tf_op jit(solution)/shard_map/ppermute | solution.py:182
  38.9 2.3 %shard_map.64 = f32[512,768]{1,0:T(8,128)} custom-call(f32[1]{0:T(128)S(6)} %copy.16.scale_ref, f32[1]{0:T(128)S(6)} %copy.17.offset_ref, f32[512,768]{1,0:T(8,128)S(1)} %get-tuple-element.30.unit_ref, f32[512,1]{1,0:T(8,128)S(1)} %get-tuple-element.31.recip_ref, bf16[512,768]{1,0:T(8,128)(2,1)S(1)} %get-tuple-element.24.low_ref, ...), custom_call_target="tpu_custom_call" | custom-call | flops 50000000 | bytes 1024 | tf_op jit(solution)/shard_map/pallas_call | solution.py:150
  41.2 0.0 collective-permute-done.9.rest_1_
  41.2 1.3 %shard_map.67.sum_in = f32[512,768]{1,0:T(8,128)S(1)} custom-call(f32[1]{0:T(128)S(6)} %copy.16.scale_ref, f32[1]{0:T(128)S(6)} %copy.17.offset_ref, bf16[512,768]{1,0:T(8,128)(2,1)S(1)} %get-tuple-element.37.low_ref, f32[512,768]{1,0:T(8,128)S(1)} %shard_map.66.sum_in, ...), custom_call_target="tpu_custom_call", output_to_operand_aliasing={{}: (3, {})} | custom-call | flops 400000000 | bytes 1024 | tf_op jit(solution)/shard_map/pallas_call | solution.py:134
  42.5 1.1 %shard_map.68.sum_ref = f32[512,768]{1,0:T(8,128)S(1)} custom-call(f32[1]{0:T(128)S(6)} %copy.16.scale_ref, f32[1]{0:T(128)S(6)} %copy.17.offset_ref, bf16[512,768]{1,0:T(8,128)(2,1)S(1)} %get-tuple-element.37.low_ref, f32[512,768]{1,0:T(8,128)S(1)} %shard_map.67.sum_in, ...), custom_call_target="tpu_custom_call", output_to_operand_aliasing={{}: (3, {})} | custom-call | flops 1000000000 | bytes 1024 | tf_op jit(solution)/shard_map/pallas_call | solution.py:134
  43.6 1.3 %collective-permute-done.12.rest_1_ = bf16[160,768]{1,0:T(8,128)(2,1)S(1)} collective-permute-done((bf16[160,768]{1,0:T(8,128)(2,1)S(1)}, bf16[160,768]{1,0:T(8,128)(2,1)S(1)}, u32[]{:S(2)}, u32[]{:S(2)}) %collective-permute-start.12) | collective-permute-done | bytes 245792 | tf_op jit(solution)/shard_map/ppermute | solution.py:182
  44.9 0.6 %collective-permute-done.11.rest_0_ = bf16[176,768]{1,0:T(8,128)(2,1)S(1)} collective-permute-done((bf16[176,768]{1,0:T(8,128)(2,1)S(1)}, bf16[176,768]{1,0:T(8,128)(2,1)S(1)}, u32[]{:S(2)}, u32[]{:S(2)}) %collective-permute-start.11) | collective-permute-done | bytes 270368 | tf_op jit(solution)/shard_map/ppermute | solution.py:182
  45.5 2.1 %shard_map.69 = f32[512,768]{1,0:T(8,128)} custom-call(f32[1]{0:T(128)S(6)} %copy.16.scale_ref, f32[1]{0:T(128)S(6)} %copy.17.offset_ref, f32[512,768]{1,0:T(8,128)S(1)} %get-tuple-element.35.unit_ref, f32[512,1]{1,0:T(8,128)S(1)} %get-tuple-element.36.recip_ref, bf16[512,768]{1,0:T(8,128)(2,1)S(1)} %get-tuple-element.37.low_ref, ...), custom_call_target="tpu_custom_call" | custom-call | flops 50000000 | bytes 1024 | tf_op jit(solution)/shard_map/pallas_call | solution.py:150
  (13 shorter events, 0.1 us)
Async XLA Ops:
  0.6 4.3 %copy-start = (bf16[512,768]{1,0:T(8,128)(2,1)S(1)}, bf16[512,768]{1,0:T(8,128)(2,1)}, u32[]{:S(2)}) copy-start(bf16[512,768]{1,0:T(8,128)(2,1)} %value_ref.2) | copy-start | bytes 2359300
  0.6 1.2 %copy-start.1 = (bf16[512,768]{1,0:T(8,128)(2,1)S(1)}, bf16[512,768]{1,0:T(8,128)(2,1)}, u32[]{:S(2)}) copy-start(bf16[512,768]{1,0:T(8,128)(2,1)} %value_ref.3) | copy-start | bytes 2359300
  1.9 10.4 %collective-permute-start.2 = (bf16[176,768]{1,0:T(8,128)(2,1)S(1)}, bf16[176,768]{1,0:T(8,128)(2,1)S(1)}, u32[]{:S(2)}, u32[]{:S(2)}) collective-permute-start(bf16[176,768]{1,0:T(8,128)(2,1)S(1)} %shard_map.60), channel_id=1, source_target_pairs={{0,1},{1,0},{2,3},{3,2},{4,5},{5,4},{6,7},{7,6},{8,9},{9,8},{10,11... | collective-permute-start | bytes 811016 | tf_op jit(solution)/shard_map/ppermute | solution.py:182
  4.9 14.7 %collective-permute-start = (bf16[160,768]{1,0:T(8,128)(2,1)S(1)}, bf16[160,768]{1,0:T(8,128)(2,1)S(1)}, u32[]{:S(2)}, u32[]{:S(2)}) collective-permute-start(bf16[160,768]{1,0:T(8,128)(2,1)S(1)} %slice.15), channel_id=1, source_target_pairs={{0,30},{1,3},{2,0},{3,5},{4,2},{5,7},{6,4},{7,9},{8,6},{9,11},{10,... | collective-permute-start | bytes 737288 | tf_op jit(solution)/shard_map/ppermute | solution.py:182
  8.7 8.9 %collective-permute-start.1 = (bf16[160,768]{1,0:T(8,128)(2,1)S(1)}, bf16[160,768]{1,0:T(8,128)(2,1)S(1)}, u32[]{:S(2)}, u32[]{:S(2)}) collective-permute-start(bf16[160,768]{1,0:T(8,128)(2,1)S(1)} %slice.16), channel_id=1, source_target_pairs={{0,1},{1,0},{2,3},{3,2},{4,5},{5,4},{6,7},{7,6},{8,9},{9,8},{10,11... | collective-permute-start | bytes 737288 | tf_op jit(solution)/shard_map/ppermute | solution.py:182
  8.8 14.6 %collective-permute-start.3 = (bf16[176,768]{1,0:T(8,128)(2,1)S(1)}, bf16[176,768]{1,0:T(8,128)(2,1)S(1)}, u32[]{:S(2)}, u32[]{:S(2)}) collective-permute-start(bf16[176,768]{1,0:T(8,128)(2,1)S(1)} %slice.17), channel_id=1, source_target_pairs={{0,1},{1,0},{2,3},{3,2},{4,5},{5,4},{6,7},{7,6},{8,9},{9,8},{10,11... | collective-permute-start | bytes 811016 | tf_op jit(solution)/shard_map/ppermute | solution.py:182
  10.9 18.2 %collective-permute-start.7 = (bf16[176,768]{1,0:T(8,128)(2,1)S(1)}, bf16[176,768]{1,0:T(8,128)(2,1)S(1)}, u32[]{:S(2)}, u32[]{:S(2)}) collective-permute-start(bf16[176,768]{1,0:T(8,128)(2,1)S(1)} %get-tuple-element.39), channel_id=1, source_target_pairs={{0,1},{1,0},{2,3},{3,2},{4,5},{5,4},{6,7},{7,6},{8,9},{9,8},{10,11... | collective-permute-start | bytes 811016 | tf_op jit(solution)/shard_map/ppermute | solution.py:182
  12.3 11.1 %collective-permute-start.4 = (bf16[176,768]{1,0:T(8,128)(2,1)S(1)}, bf16[176,768]{1,0:T(8,128)(2,1)S(1)}, u32[]{:S(2)}, u32[]{:S(2)}) collective-permute-start(bf16[176,768]{1,0:T(8,128)(2,1)S(1)} %collective-permute-done.2.rest_1_), channel_id=1, source_target_pairs={{0,2},{1,31},{2,4},{3,1},{4,6},{5,3},{6,8},{7,5},{8,10},{9,7},{10,... | collective-permute-start | bytes 811016 | tf_op jit(solution)/shard_map/ppermute | solution.py:182
  17.6 11.6 %collective-permute-start.5 = (bf16[160,768]{1,0:T(8,128)(2,1)S(1)}, bf16[160,768]{1,0:T(8,128)(2,1)S(1)}, u32[]{:S(2)}, u32[]{:S(2)}) collective-permute-start(bf16[160,768]{1,0:T(8,128)(2,1)S(1)} %collective-permute-done.1.rest_0_), channel_id=1, source_target_pairs={{0,2},{1,31},{2,4},{3,1},{4,6},{5,3},{6,8},{7,5},{8,10},{9,7},{10,... | collective-permute-start | bytes 737288 | tf_op jit(solution)/shard_map/ppermute | solution.py:182
  19.6 14.6 %collective-permute-start.8 = (bf16[176,768]{1,0:T(8,128)(2,1)S(1)}, bf16[176,768]{1,0:T(8,128)(2,1)S(1)}, u32[]{:S(2)}, u32[]{:S(2)}) collective-permute-start(bf16[176,768]{1,0:T(8,128)(2,1)S(1)} %get-tuple-element.41), channel_id=1, source_target_pairs={{0,1},{1,0},{2,3},{3,2},{4,5},{5,4},{6,7},{7,6},{8,9},{9,8},{10,11... | collective-permute-start | bytes 811016 | tf_op jit(solution)/shard_map/ppermute | solution.py:182
  23.4 15.5 %collective-permute-start.6 = (bf16[176,768]{1,0:T(8,128)(2,1)S(1)}, bf16[176,768]{1,0:T(8,128)(2,1)S(1)}, u32[]{:S(2)}, u32[]{:S(2)}) collective-permute-start(bf16[176,768]{1,0:T(8,128)(2,1)S(1)} %collective-permute-done.3.rest_0_), channel_id=1, source_target_pairs={{0,2},{1,31},{2,4},{3,1},{4,6},{5,3},{6,8},{7,5},{8,10},{9,7},{10,... | collective-permute-start | bytes 811016 | tf_op jit(solution)/shard_map/ppermute | solution.py:182
  29.2 12.0 %collective-permute-start.9 = (bf16[176,768]{1,0:T(8,128)(2,1)S(1)}, bf16[176,768]{1,0:T(8,128)(2,1)S(1)}, u32[]{:S(2)}, u32[]{:S(2)}) collective-permute-start(bf16[176,768]{1,0:T(8,128)(2,1)S(1)} %collective-permute-done.7.rest_0_), channel_id=1, source_target_pairs={{0,2},{1,31},{2,4},{3,1},{4,6},{5,3},{6,8},{7,5},{8,10},{9,7},{10,... | collective-permute-start | bytes 811016 | tf_op jit(solution)/shard_map/ppermute | solution.py:182
  31.2 11.3 %collective-permute-start.10 = (bf16[160,768]{1,0:T(8,128)(2,1)S(1)}, bf16[160,768]{1,0:T(8,128)(2,1)S(1)}, u32[]{:S(2)}, u32[]{:S(2)}) collective-permute-start(bf16[160,768]{1,0:T(8,128)(2,1)S(1)} %slice.15), channel_id=1, source_target_pairs={{0,1},{1,0},{2,3},{3,2},{4,5},{5,4},{6,7},{7,6},{8,9},{9,8},{10,11... | collective-permute-start | bytes 737288 | tf_op jit(solution)/shard_map/ppermute | solution.py:182
  34.2 11.3 %collective-permute-start.11 = (bf16[176,768]{1,0:T(8,128)(2,1)S(1)}, bf16[176,768]{1,0:T(8,128)(2,1)S(1)}, u32[]{:S(2)}, u32[]{:S(2)}) collective-permute-start(bf16[176,768]{1,0:T(8,128)(2,1)S(1)} %collective-permute-done.8.rest_0_), channel_id=1, source_target_pairs={{0,2},{1,31},{2,4},{3,1},{4,6},{5,3},{6,8},{7,5},{8,10},{9,7},{10,... | collective-permute-start | bytes 811016 | tf_op jit(solution)/shard_map/ppermute | solution.py:182
  37.0 7.9 %collective-permute-start.12 = (bf16[160,768]{1,0:T(8,128)(2,1)S(1)}, bf16[160,768]{1,0:T(8,128)(2,1)S(1)}, u32[]{:S(2)}, u32[]{:S(2)}) collective-permute-start(bf16[160,768]{1,0:T(8,128)(2,1)S(1)} %collective-permute-done), channel_id=1, source_target_pairs={{0,1},{1,0},{2,3},{3,2},{4,5},{5,4},{6,7},{7,6},{8,9},{9,8},{10,11... | collective-permute-start | bytes 737288 | tf_op jit(solution)/shard_map/ppermute | solution.py:182

commit v8 on v7

--- a/solution.py
+++ b/solution.py
@@ -72,8 +72,8 @@
     others, (out_ref, other_low, held, sems) = rest[:count], rest[count:]
     scale, offset = scale_ref[0], offset_ref[0]
     lower_rows(others, other_low)
-    logits = scale * dot32(low_ref[...], other_low[...], LAST) + offset
-    weight = jax.nn.sigmoid(logits).astype(jnp.bfloat16)
+    half = (0.5 * scale) * dot32(low_ref[...], other_low[...], LAST) + 0.5 * offset
+    weight = (0.5 * jnp.tanh(half) + 0.5).astype(jnp.bfloat16)
     size = held.shape[0] // blocks
     copies = []
     for block in range(blocks):

time: 47.8 us -> 47.8 us (level)
  no operation moved by 1% of the time
where the time goes in v8:
time: 47.8 us; the launch traced here: 47.7 us
  starting transfers between devices  25.6 us (54%)
  Pallas kernels  12.6 us (26%)
  waiting for transfers between devices  6.13 us (13%)
  between operations  2.09 us (4%)
  local copies, waits for them, and re-layouts  1.29 us (3%)
    ppermute x13, starting transfers between devices, exchange(): lax.ppermute(value, AXES, [(at, target(at) % count) for at in range(count)])  25.6 us
    ppermute x13, waiting for transfers between devices, exchange(): lax.ppermute(value, AXES, [(at, target(at) % count) for at in range(count)])  6.13 us
    pallas_call x5, Pallas kernels, add_call(): pl.pallas_call(functools.partial(add_kernel, len(others)), out_shape=jax....  5.83 us
    pallas_call x2, Pallas kernels, last_call(): pl.pallas_call(functools.partial(last_kernel, len(others), blocks), out_s...  4.42 us
    pallas_call x1, Pallas kernels, own_call(): pl.pallas_call(own_kernel, out_shape=(low, low, total, total), in_specs=[...  1.76 us
    unnamed x4, local copies, waits for them, and re-layouts  1.2 us
  transfers between devices with their start and end apart: 13, of which 5 were waited for; matrix products, arithmetic and copies ran while one was open for 0% of the time, Pallas kernels for 22%

profile of v8, /device:TPU:0, one launch (start us, length us, event | category | flops | bytes accessed | tf_op | source)
XLA Modules:
  0.0 47.7 jit_solution(9283269283178477742)
XLA Ops:
  0.6 1.2 %copy-done.1 = bf16[512,768]{1,0:T(8,128)(2,1)S(1)} copy-done((bf16[512,768]{1,0:T(8,128)(2,1)S(1)}, bf16[512,768]{1,0:T(8,128)(2,1)}, u32[]{:S(2)}) %copy-start.1) | copy-done | bytes 786456
  1.9 3.0 %collective-permute-start.2 = (bf16[176,768]{1,0:T(8,128)(2,1)S(1)}, bf16[176,768]{1,0:T(8,128)(2,1)S(1)}, u32[]{:S(2)}, u32[]{:S(2)}) collective-permute-start(bf16[176,768]{1,0:T(8,128)(2,1)S(1)} %shard_map.60), channel_id=1, source_target_pairs={{0,1},{1,0},{2,3},{3,2},{4,5},{5,4},{6,7},{7,6},{8,9},{9,8},{10,11... | collective-permute-start | bytes 811016 | tf_op jit(solution)/shard_map/ppermute | solution.py:182
  4.9 3.7 %collective-permute-start = (bf16[160,768]{1,0:T(8,128)(2,1)S(1)}, bf16[160,768]{1,0:T(8,128)(2,1)S(1)}, u32[]{:S(2)}, u32[]{:S(2)}) collective-permute-start(bf16[160,768]{1,0:T(8,128)(2,1)S(1)} %slice.15), channel_id=1, source_target_pairs={{0,30},{1,3},{2,0},{3,5},{4,2},{5,7},{6,4},{7,9},{8,6},{9,11},{10,... | collective-permute-start | bytes 737288 | tf_op jit(solution)/shard_map/ppermute | solution.py:182
  8.7 0.1 collective-permute-start.1
  8.8 2.1 %collective-permute-start.3 = (bf16[176,768]{1,0:T(8,128)(2,1)S(1)}, bf16[176,768]{1,0:T(8,128)(2,1)S(1)}, u32[]{:S(2)}, u32[]{:S(2)}) collective-permute-start(bf16[176,768]{1,0:T(8,128)(2,1)S(1)} %slice.17), channel_id=1, source_target_pairs={{0,1},{1,0},{2,3},{3,2},{4,5},{5,4},{6,7},{7,6},{8,9},{9,8},{10,11... | collective-permute-start | bytes 811016 | tf_op jit(solution)/shard_map/ppermute | solution.py:182
  10.9 0.1 collective-permute-start.7
  12.3 2.0 %collective-permute-start.4 = (bf16[176,768]{1,0:T(8,128)(2,1)S(1)}, bf16[176,768]{1,0:T(8,128)(2,1)S(1)}, u32[]{:S(2)}, u32[]{:S(2)}) collective-permute-start(bf16[176,768]{1,0:T(8,128)(2,1)S(1)} %collective-permute-done.2.rest_1_), channel_id=1, source_target_pairs={{0,2},{1,31},{2,4},{3,1},{4,6},{5,3},{6,8},{7,5},{8,10},{9,7},{10,... | collective-permute-start | bytes 811016 | tf_op jit(solution)/shard_map/ppermute | solution.py:182
  14.3 1.8 %shard_map.59 = (bf16[512,768]{1,0:T(8,128)(2,1)S(1)}, bf16[512,768]{1,0:T(8,128)(2,1)S(1)}, f32[512,768]{1,0:T(8,128)S(1)}, f32[512,768]{1,0:T(8,128)S(1)}) custom-call(f32[1]{0:T(128)S(6)} %copy.16.scale_ref, f32[1]{0:T(128)S(6)} %copy.17.offset_ref, bf16[512,768]{1,0:T(8,128)(2,1)S(1)} %copy-done, bf16[512,768]{1,0:T(8,128)(2,1)S(1)} %copy-done.1), custom_call_target="tpu_custom_call" | custom-call | flops 800000000 | bytes 1024 | tf_op jit(solution)/shard_map/pallas_call | solution.py:121
  16.1 1.5 %collective-permute-done.1.rest_0_ = bf16[160,768]{1,0:T(8,128)(2,1)S(1)} collective-permute-done((bf16[160,768]{1,0:T(8,128)(2,1)S(1)}, bf16[160,768]{1,0:T(8,128)(2,1)S(1)}, u32[]{:S(2)}, u32[]{:S(2)}) %collective-permute-start.1) | collective-permute-done | bytes 245792 | tf_op jit(solution)/shard_map/ppermute | solution.py:182
  17.6 2.0 %collective-permute-start.5 = (bf16[160,768]{1,0:T(8,128)(2,1)S(1)}, bf16[160,768]{1,0:T(8,128)(2,1)S(1)}, u32[]{:S(2)}, u32[]{:S(2)}) collective-permute-start(bf16[160,768]{1,0:T(8,128)(2,1)S(1)} %collective-permute-done.1.rest_0_), channel_id=1, source_target_pairs={{0,2},{1,31},{2,4},{3,1},{4,6},{5,3},{6,8},{7,5},{8,10},{9,7},{10,... | collective-permute-start | bytes 737288 | tf_op jit(solution)/shard_map/ppermute | solution.py:182
  19.6 0.0 collective-permute-done
  19.6 1.9 %collective-permute-start.8 = (bf16[176,768]{1,0:T(8,128)(2,1)S(1)}, bf16[176,768]{1,0:T(8,128)(2,1)S(1)}, u32[]{:S(2)}, u32[]{:S(2)}) collective-permute-start(bf16[176,768]{1,0:T(8,128)(2,1)S(1)} %get-tuple-element.41), channel_id=1, source_target_pairs={{0,1},{1,0},{2,3},{3,2},{4,5},{5,4},{6,7},{7,6},{8,9},{9,8},{10,11... | collective-permute-start | bytes 811016 | tf_op jit(solution)/shard_map/ppermute | solution.py:182
  21.5 1.3 %shard_map.61.sum_in = f32[512,768]{1,0:T(8,128)S(1)} custom-call(f32[1]{0:T(128)S(6)} %copy.16.scale_ref, f32[1]{0:T(128)S(6)} %copy.17.offset_ref, bf16[512,768]{1,0:T(8,128)(2,1)S(1)} %get-tuple-element.24.low_ref, f32[512,768]{1,0:T(8,128)S(1)} %get-tuple-element.26.sum_in, ...), custom_call_target="tpu_custom_call", output_to_operand_aliasing={{}: (3, {})} | custom-call | flops 400000000 | bytes 1024 | tf_op jit(solution)/shard_map/pallas_call | solution.py:134
  22.8 0.6 %collective-permute-done.3.rest_0_ = bf16[176,768]{1,0:T(8,128)(2,1)S(1)} collective-permute-done((bf16[176,768]{1,0:T(8,128)(2,1)S(1)}, bf16[176,768]{1,0:T(8,128)(2,1)S(1)}, u32[]{:S(2)}, u32[]{:S(2)}) %collective-permute-start.3) | collective-permute-done | bytes 270368 | tf_op jit(solution)/shard_map/ppermute | solution.py:182
  23.4 2.0 %collective-permute-start.6 = (bf16[176,768]{1,0:T(8,128)(2,1)S(1)}, bf16[176,768]{1,0:T(8,128)(2,1)S(1)}, u32[]{:S(2)}, u32[]{:S(2)}) collective-permute-start(bf16[176,768]{1,0:T(8,128)(2,1)S(1)} %collective-permute-done.3.rest_0_), channel_id=1, source_target_pairs={{0,2},{1,31},{2,4},{3,1},{4,6},{5,3},{6,8},{7,5},{8,10},{9,7},{10,... | collective-permute-start | bytes 811016 | tf_op jit(solution)/shard_map/ppermute | solution.py:182
  25.4 1.1 %shard_map.62.sum_ref = f32[512,768]{1,0:T(8,128)S(1)} custom-call(f32[1]{0:T(128)S(6)} %copy.16.scale_ref, f32[1]{0:T(128)S(6)} %copy.17.offset_ref, bf16[512,768]{1,0:T(8,128)(2,1)S(1)} %get-tuple-element.24.low_ref, f32[512,768]{1,0:T(8,128)S(1)} %shard_map.61.sum_in, ...), custom_call_target="tpu_custom_call", output_to_operand_aliasing={{}: (3, {})} | custom-call | flops 400000000 | bytes 1024 | tf_op jit(solution)/shard_map/pallas_call | solution.py:134
  26.5 0.3 shard_map.63
  26.8 0.3 shard_map.65
  27.1 2.1 %collective-permute-done.7.rest_0_ = bf16[176,768]{1,0:T(8,128)(2,1)S(1)} collective-permute-done((bf16[176,768]{1,0:T(8,128)(2,1)S(1)}, bf16[176,768]{1,0:T(8,128)(2,1)S(1)}, u32[]{:S(2)}, u32[]{:S(2)}) %collective-permute-start.7) | collective-permute-done | bytes 270368 | tf_op jit(solution)/shard_map/ppermute | solution.py:182
  29.2 0.0 collective-permute-done.5.rest_1_
  29.2 2.0 %collective-permute-start.9 = (bf16[176,768]{1,0:T(8,128)(2,1)S(1)}, bf16[176,768]{1,0:T(8,128)(2,1)S(1)}, u32[]{:S(2)}, u32[]{:S(2)}) collective-permute-start(bf16[176,768]{1,0:T(8,128)(2,1)S(1)} %collective-permute-done.7.rest_0_), channel_id=1, source_target_pairs={{0,2},{1,31},{2,4},{3,1},{4,6},{5,3},{6,8},{7,5},{8,10},{9,7},{10,... | collective-permute-start | bytes 811016 | tf_op jit(solution)/shard_map/ppermute | solution.py:182
  31.2 1.9 %collective-permute-start.10 = (bf16[160,768]{1,0:T(8,128)(2,1)S(1)}, bf16[160,768]{1,0:T(8,128)(2,1)S(1)}, u32[]{:S(2)}, u32[]{:S(2)}) collective-permute-start(bf16[160,768]{1,0:T(8,128)(2,1)S(1)} %slice.15), channel_id=1, source_target_pairs={{0,1},{1,0},{2,3},{3,2},{4,5},{5,4},{6,7},{7,6},{8,9},{9,8},{10,11... | collective-permute-start | bytes 737288 | tf_op jit(solution)/shard_map/ppermute | solution.py:182
  33.1 1.1 %shard_map.66.sum_in = f32[512,768]{1,0:T(8,128)S(1)} custom-call(f32[1]{0:T(128)S(6)} %copy.16.scale_ref, f32[1]{0:T(128)S(6)} %copy.17.offset_ref, bf16[512,768]{1,0:T(8,128)(2,1)S(1)} %get-tuple-element.37.low_ref, f32[512,768]{1,0:T(8,128)S(1)} %get-tuple-element.38.sum_in, ...), custom_call_target="tpu_custom_call", output_to_operand_aliasing={{}: (3, {})} | custom-call | flops 400000000 | bytes 1024 | tf_op jit(solution)/shard_map/pallas_call | solution.py:134
  34.2 2.8 %collective-permute-start.11 = (bf16[176,768]{1,0:T(8,128)(2,1)S(1)}, bf16[176,768]{1,0:T(8,128)(2,1)S(1)}, u32[]{:S(2)}, u32[]{:S(2)}) collective-permute-start(bf16[176,768]{1,0:T(8,128)(2,1)S(1)} %collective-permute-done.8.rest_0_), channel_id=1, source_target_pairs={{0,2},{1,31},{2,4},{3,1},{4,6},{5,3},{6,8},{7,5},{8,10},{9,7},{10,... | collective-permute-start | bytes 811016 | tf_op jit(solution)/shard_map/ppermute | solution.py:182
  37.0 1.9 %collective-permute-start.12 = (bf16[160,768]{1,0:T(8,128)(2,1)S(1)}, bf16[160,768]{1,0:T(8,128)(2,1)S(1)}, u32[]{:S(2)}, u32[]{:S(2)}) collective-permute-start(bf16[160,768]{1,0:T(8,128)(2,1)S(1)} %collective-permute-done), channel_id=1, source_target_pairs={{0,1},{1,0},{2,3},{3,2},{4,5},{5,4},{6,7},{7,6},{8,9},{9,8},{10,11... | collective-permute-start | bytes 737288 | tf_op jit(solution)/shard_map/ppermute | solution.py:182
  38.9 2.3 %shard_map.64 = f32[512,768]{1,0:T(8,128)} custom-call(f32[1]{0:T(128)S(6)} %copy.16.scale_ref, f32[1]{0:T(128)S(6)} %copy.17.offset_ref, f32[512,768]{1,0:T(8,128)S(1)} %get-tuple-element.30.unit_ref, f32[512,1]{1,0:T(8,128)S(1)} %get-tuple-element.31.recip_ref, bf16[512,768]{1,0:T(8,128)(2,1)S(1)} %get-tuple-element.24.low_ref, ...), custom_call_target="tpu_custom_call" | custom-call | flops 50000000 | bytes 1024 | tf_op jit(solution)/shard_map/pallas_call | solution.py:150
  41.2 0.0 collective-permute-done.9.rest_1_
  41.2 1.3 %shard_map.67.sum_in = f32[512,768]{1,0:T(8,128)S(1)} custom-call(f32[1]{0:T(128)S(6)} %copy.16.scale_ref, f32[1]{0:T(128)S(6)} %copy.17.offset_ref, bf16[512,768]{1,0:T(8,128)(2,1)S(1)} %get-tuple-element.37.low_ref, f32[512,768]{1,0:T(8,128)S(1)} %shard_map.66.sum_in, ...), custom_call_target="tpu_custom_call", output_to_operand_aliasing={{}: (3, {})} | custom-call | flops 400000000 | bytes 1024 | tf_op jit(solution)/shard_map/pallas_call | solution.py:134
  42.5 1.1 %shard_map.68.sum_ref = f32[512,768]{1,0:T(8,128)S(1)} custom-call(f32[1]{0:T(128)S(6)} %copy.16.scale_ref, f32[1]{0:T(128)S(6)} %copy.17.offset_ref, bf16[512,768]{1,0:T(8,128)(2,1)S(1)} %get-tuple-element.37.low_ref, f32[512,768]{1,0:T(8,128)S(1)} %shard_map.67.sum_in, ...), custom_call_target="tpu_custom_call", output_to_operand_aliasing={{}: (3, {})} | custom-call | flops 1000000000 | bytes 1024 | tf_op jit(solution)/shard_map/pallas_call | solution.py:134
  43.6 1.3 %collective-permute-done.12.rest_1_ = bf16[160,768]{1,0:T(8,128)(2,1)S(1)} collective-permute-done((bf16[160,768]{1,0:T(8,128)(2,1)S(1)}, bf16[160,768]{1,0:T(8,128)(2,1)S(1)}, u32[]{:S(2)}, u32[]{:S(2)}) %collective-permute-start.12) | collective-permute-done | bytes 245792 | tf_op jit(solution)/shard_map/ppermute | solution.py:182
  44.9 0.6 %collective-permute-done.11.rest_0_ = bf16[176,768]{1,0:T(8,128)(2,1)S(1)} collective-permute-done((bf16[176,768]{1,0:T(8,128)(2,1)S(1)}, bf16[176,768]{1,0:T(8,128)(2,1)S(1)}, u32[]{:S(2)}, u32[]{:S(2)}) %collective-permute-start.11) | collective-permute-done | bytes 270368 | tf_op jit(solution)/shard_map/ppermute | solution.py:182
  45.5 2.1 %shard_map.69 = f32[512,768]{1,0:T(8,128)} custom-call(f32[1]{0:T(128)S(6)} %copy.16.scale_ref, f32[1]{0:T(128)S(6)} %copy.17.offset_ref, f32[512,768]{1,0:T(8,128)S(1)} %get-tuple-element.35.unit_ref, f32[512,1]{1,0:T(8,128)S(1)} %get-tuple-element.36.recip_ref, bf16[512,768]{1,0:T(8,128)(2,1)S(1)} %get-tuple-element.37.low_ref, ...), custom_call_target="tpu_custom_call" | custom-call | flops 50000000 | bytes 1024 | tf_op jit(solution)/shard_map/pallas_call | solution.py:150
  (13 shorter events, 0.1 us)
Async XLA Ops:
  0.6 4.3 %copy-start = (bf16[512,768]{1,0:T(8,128)(2,1)S(1)}, bf16[512,768]{1,0:T(8,128)(2,1)}, u32[]{:S(2)}) copy-start(bf16[512,768]{1,0:T(8,128)(2,1)} %value_ref.2) | copy-start | bytes 2359300
  0.6 1.2 %copy-start.1 = (bf16[512,768]{1,0:T(8,128)(2,1)S(1)}, bf16[512,768]{1,0:T(8,128)(2,1)}, u32[]{:S(2)}) copy-start(bf16[512,768]{1,0:T(8,128)(2,1)} %value_ref.3) | copy-start | bytes 2359300
  1.9 10.4 %collective-permute-start.2 = (bf16[176,768]{1,0:T(8,128)(2,1)S(1)}, bf16[176,768]{1,0:T(8,128)(2,1)S(1)}, u32[]{:S(2)}, u32[]{:S(2)}) collective-permute-start(bf16[176,768]{1,0:T(8,128)(2,1)S(1)} %shard_map.60), channel_id=1, source_target_pairs={{0,1},{1,0},{2,3},{3,2},{4,5},{5,4},{6,7},{7,6},{8,9},{9,8},{10,11... | collective-permute-start | bytes 811016 | tf_op jit(solution)/shard_map/ppermute | solution.py:182
  4.9 14.7 %collective-permute-start = (bf16[160,768]{1,0:T(8,128)(2,1)S(1)}, bf16[160,768]{1,0:T(8,128)(2,1)S(1)}, u32[]{:S(2)}, u32[]{:S(2)}) collective-permute-start(bf16[160,768]{1,0:T(8,128)(2,1)S(1)} %slice.15), channel_id=1, source_target_pairs={{0,30},{1,3},{2,0},{3,5},{4,2},{5,7},{6,4},{7,9},{8,6},{9,11},{10,... | collective-permute-start | bytes 737288 | tf_op jit(solution)/shard_map/ppermute | solution.py:182
  8.7 8.9 %collective-permute-start.1 = (bf16[160,768]{1,0:T(8,128)(2,1)S(1)}, bf16[160,768]{1,0:T(8,128)(2,1)S(1)}, u32[]{:S(2)}, u32[]{:S(2)}) collective-permute-start(bf16[160,768]{1,0:T(8,128)(2,1)S(1)} %slice.16), channel_id=1, source_target_pairs={{0,1},{1,0},{2,3},{3,2},{4,5},{5,4},{6,7},{7,6},{8,9},{9,8},{10,11... | collective-permute-start | bytes 737288 | tf_op jit(solution)/shard_map/ppermute | solution.py:182
  8.8 14.6 %collective-permute-start.3 = (bf16[176,768]{1,0:T(8,128)(2,1)S(1)}, bf16[176,768]{1,0:T(8,128)(2,1)S(1)}, u32[]{:S(2)}, u32[]{:S(2)}) collective-permute-start(bf16[176,768]{1,0:T(8,128)(2,1)S(1)} %slice.17), channel_id=1, source_target_pairs={{0,1},{1,0},{2,3},{3,2},{4,5},{5,4},{6,7},{7,6},{8,9},{9,8},{10,11... | collective-permute-start | bytes 811016 | tf_op jit(solution)/shard_map/ppermute | solution.py:182
  10.9 18.2 %collective-permute-start.7 = (bf16[176,768]{1,0:T(8,128)(2,1)S(1)}, bf16[176,768]{1,0:T(8,128)(2,1)S(1)}, u32[]{:S(2)}, u32[]{:S(2)}) collective-permute-start(bf16[176,768]{1,0:T(8,128)(2,1)S(1)} %get-tuple-element.39), channel_id=1, source_target_pairs={{0,1},{1,0},{2,3},{3,2},{4,5},{5,4},{6,7},{7,6},{8,9},{9,8},{10,11... | collective-permute-start | bytes 811016 | tf_op jit(solution)/shard_map/ppermute | solution.py:182
  12.3 11.1 %collective-permute-start.4 = (bf16[176,768]{1,0:T(8,128)(2,1)S(1)}, bf16[176,768]{1,0:T(8,128)(2,1)S(1)}, u32[]{:S(2)}, u32[]{:S(2)}) collective-permute-start(bf16[176,768]{1,0:T(8,128)(2,1)S(1)} %collective-permute-done.2.rest_1_), channel_id=1, source_target_pairs={{0,2},{1,31},{2,4},{3,1},{4,6},{5,3},{6,8},{7,5},{8,10},{9,7},{10,... | collective-permute-start | bytes 811016 | tf_op jit(solution)/shard_map/ppermute | solution.py:182
  17.6 11.6 %collective-permute-start.5 = (bf16[160,768]{1,0:T(8,128)(2,1)S(1)}, bf16[160,768]{1,0:T(8,128)(2,1)S(1)}, u32[]{:S(2)}, u32[]{:S(2)}) collective-permute-start(bf16[160,768]{1,0:T(8,128)(2,1)S(1)} %collective-permute-done.1.rest_0_), channel_id=1, source_target_pairs={{0,2},{1,31},{2,4},{3,1},{4,6},{5,3},{6,8},{7,5},{8,10},{9,7},{10,... | collective-permute-start | bytes 737288 | tf_op jit(solution)/shard_map/ppermute | solution.py:182
  19.6 14.6 %collective-permute-start.8 = (bf16[176,768]{1,0:T(8,128)(2,1)S(1)}, bf16[176,768]{1,0:T(8,128)(2,1)S(1)}, u32[]{:S(2)}, u32[]{:S(2)}) collective-permute-start(bf16[176,768]{1,0:T(8,128)(2,1)S(1)} %get-tuple-element.41), channel_id=1, source_target_pairs={{0,1},{1,0},{2,3},{3,2},{4,5},{5,4},{6,7},{7,6},{8,9},{9,8},{10,11... | collective-permute-start | bytes 811016 | tf_op jit(solution)/shard_map/ppermute | solution.py:182
  23.4 15.5 %collective-permute-start.6 = (bf16[176,768]{1,0:T(8,128)(2,1)S(1)}, bf16[176,768]{1,0:T(8,128)(2,1)S(1)}, u32[]{:S(2)}, u32[]{:S(2)}) collective-permute-start(bf16[176,768]{1,0:T(8,128)(2,1)S(1)} %collective-permute-done.3.rest_0_), channel_id=1, source_target_pairs={{0,2},{1,31},{2,4},{3,1},{4,6},{5,3},{6,8},{7,5},{8,10},{9,7},{10,... | collective-permute-start | bytes 811016 | tf_op jit(solution)/shard_map/ppermute | solution.py:182
  29.2 12.0 %collective-permute-start.9 = (bf16[176,768]{1,0:T(8,128)(2,1)S(1)}, bf16[176,768]{1,0:T(8,128)(2,1)S(1)}, u32[]{:S(2)}, u32[]{:S(2)}) collective-permute-start(bf16[176,768]{1,0:T(8,128)(2,1)S(1)} %collective-permute-done.7.rest_0_), channel_id=1, source_target_pairs={{0,2},{1,31},{2,4},{3,1},{4,6},{5,3},{6,8},{7,5},{8,10},{9,7},{10,... | collective-permute-start | bytes 811016 | tf_op jit(solution)/shard_map/ppermute | solution.py:182
  31.2 11.3 %collective-permute-start.10 = (bf16[160,768]{1,0:T(8,128)(2,1)S(1)}, bf16[160,768]{1,0:T(8,128)(2,1)S(1)}, u32[]{:S(2)}, u32[]{:S(2)}) collective-permute-start(bf16[160,768]{1,0:T(8,128)(2,1)S(1)} %slice.15), channel_id=1, source_target_pairs={{0,1},{1,0},{2,3},{3,2},{4,5},{5,4},{6,7},{7,6},{8,9},{9,8},{10,11... | collective-permute-start | bytes 737288 | tf_op jit(solution)/shard_map/ppermute | solution.py:182
  34.2 11.3 %collective-permute-start.11 = (bf16[176,768]{1,0:T(8,128)(2,1)S(1)}, bf16[176,768]{1,0:T(8,128)(2,1)S(1)}, u32[]{:S(2)}, u32[]{:S(2)}) collective-permute-start(bf16[176,768]{1,0:T(8,128)(2,1)S(1)} %collective-permute-done.8.rest_0_), channel_id=1, source_target_pairs={{0,2},{1,31},{2,4},{3,1},{4,6},{5,3},{6,8},{7,5},{8,10},{9,7},{10,... | collective-permute-start | bytes 811016 | tf_op jit(solution)/shard_map/ppermute | solution.py:182
  37.0 7.9 %collective-permute-start.12 = (bf16[160,768]{1,0:T(8,128)(2,1)S(1)}, bf16[160,768]{1,0:T(8,128)(2,1)S(1)}, u32[]{:S(2)}, u32[]{:S(2)}) collective-permute-start(bf16[160,768]{1,0:T(8,128)(2,1)S(1)} %collective-permute-done), channel_id=1, source_target_pairs={{0,1},{1,0},{2,3},{3,2},{4,5},{5,4},{6,7},{7,6},{8,9},{9,8},{10,11... | collective-permute-start | bytes 737288 | tf_op jit(solution)/shard_map/ppermute | solution.py:182

commit v9 on v4

--- a/solution.py
+++ b/solution.py
@@ -206,8 +206,7 @@
     sum_txt = add_call(*args, txt_low, sum_txt, (near3,), 0.4)
     far4 = exchange(tied(near4, sum_txt), onward)
     grad_img = last_call(*args, images, img_low, sum_img, (far0, far1, far2,), 0.05)
-    sum_txt = add_call(*args, txt_low, tied(sum_txt, grad_img), (near4, far3,), 0.4)
-    sum_txt = add_call(*args, txt_low, sum_txt, (near_tail,), 1.0)
+    sum_txt = add_call(*args, txt_low, tied(sum_txt, grad_img), (near4, far3, near_tail), 0.4)
     grad_txt = last_call(*args, texts, txt_low, sum_txt, (far4, far_tail), 0.05)
     return grad_img, grad_txt
 

time: 48 us -> 50.6 us (1.054)
  waiting for transfers between devices: 6.57 us -> 11.4 us
  starting transfers between devices: 25.6 us -> 24.4 us
  Pallas kernels: 12.3 us -> 11.2 us
    ppermute x13, waiting for transfers between devices: 6.57 us -> 11.4 us  [exchange(): lax.ppermute(value, AXES, [(at, target(at) % count) for at in range(count)])]
    ppermute x13, starting transfers between devices: 25.6 us -> 24.4 us  [exchange(): lax.ppermute(value, AXES, [(at, target(at) % count) for at in range(count)])]
    pallas_call x5 -> x4, Pallas kernels: 5.83 us -> 4.78 us  [add_call(): pl.pallas_call(functools.partial(add_kernel, len(others)), out_shape=jax....]
  transfers between devices with their start and end apart: 13 -> 13, of which waited for: 5 -> 7; matrix products, arithmetic and copies ran while one was open for 0% -> 0% of each run, Pallas kernels for 21% -> 18%
where the time goes in v9:
time: 50.6 us; the launch traced here: 50.4 us
  starting transfers between devices  24.4 us (48%)
  waiting for transfers between devices  11.4 us (23%)
  Pallas kernels  11.2 us (22%)
  between operations  2.05 us (4%)
  local copies, waits for them, and re-layouts  1.29 us (3%)
    ppermute x13, starting transfers between devices, exchange(): lax.ppermute(value, AXES, [(at, target(at) % count) for at in range(count)])  24.4 us
    ppermute x13, waiting for transfers between devices, exchange(): lax.ppermute(value, AXES, [(at, target(at) % count) for at in range(count)])  11.4 us
    pallas_call x4, Pallas kernels, add_call(): pl.pallas_call(functools.partial(add_kernel, len(others)), out_shape=jax....  4.78 us
    pallas_call x2, Pallas kernels, last_call(): pl.pallas_call(functools.partial(last_kernel, len(others), blocks), out_s...  4.69 us
    pallas_call x1, Pallas kernels, own_call(): pl.pallas_call(own_kernel, out_shape=(low, low, total, total), in_specs=[...  1.74 us
    unnamed x4, local copies, waits for them, and re-layouts  1.2 us
  transfers between devices with their start and end apart: 13, of which 7 were waited for; matrix products, arithmetic and copies ran while one was open for 0% of the time, Pallas kernels for 18%

profile of v9, /device:TPU:0, one launch (start us, length us, event | category | flops | bytes accessed | tf_op | source)
XLA Modules:
  0.0 50.4 jit_solution(3600688515073892188)
XLA Ops:
  0.6 1.2 %copy-done.1 = bf16[512,768]{1,0:T(8,128)(2,1)S(1)} copy-done((bf16[512,768]{1,0:T(8,128)(2,1)S(1)}, bf16[512,768]{1,0:T(8,128)(2,1)}, u32[]{:S(2)}) %copy-start.1) | copy-done | bytes 786456
  1.9 3.0 %collective-permute-start.2 = (bf16[176,768]{1,0:T(8,128)(2,1)S(1)}, bf16[176,768]{1,0:T(8,128)(2,1)S(1)}, u32[]{:S(2)}, u32[]{:S(2)}) collective-permute-start(bf16[176,768]{1,0:T(8,128)(2,1)S(1)} %shard_map.60), channel_id=1, source_target_pairs={{0,1},{1,0},{2,3},{3,2},{4,5},{5,4},{6,7},{7,6},{8,9},{9,8},{10,11... | collective-permute-start | bytes 811016 | tf_op jit(solution)/shard_map/ppermute | solution.py:163
  4.9 3.7 %collective-permute-start = (bf16[160,768]{1,0:T(8,128)(2,1)S(1)}, bf16[160,768]{1,0:T(8,128)(2,1)S(1)}, u32[]{:S(2)}, u32[]{:S(2)}) collective-permute-start(bf16[160,768]{1,0:T(8,128)(2,1)S(1)} %slice.15), channel_id=1, source_target_pairs={{0,30},{1,3},{2,0},{3,5},{4,2},{5,7},{6,4},{7,9},{8,6},{9,11},{10,... | collective-permute-start | bytes 737288 | tf_op jit(solution)/shard_map/ppermute | solution.py:163
  8.7 0.1 collective-permute-start.1
  8.8 2.1 %collective-permute-start.3 = (bf16[176,768]{1,0:T(8,128)(2,1)S(1)}, bf16[176,768]{1,0:T(8,128)(2,1)S(1)}, u32[]{:S(2)}, u32[]{:S(2)}) collective-permute-start(bf16[176,768]{1,0:T(8,128)(2,1)S(1)} %slice.17), channel_id=1, source_target_pairs={{0,1},{1,0},{2,3},{3,2},{4,5},{5,4},{6,7},{7,6},{8,9},{9,8},{10,11... | collective-permute-start | bytes 811016 | tf_op jit(solution)/shard_map/ppermute | solution.py:163
  10.9 0.1 collective-permute-start.7
  12.3 2.0 %collective-permute-start.4 = (bf16[176,768]{1,0:T(8,128)(2,1)S(1)}, bf16[176,768]{1,0:T(8,128)(2,1)S(1)}, u32[]{:S(2)}, u32[]{:S(2)}) collective-permute-start(bf16[176,768]{1,0:T(8,128)(2,1)S(1)} %collective-permute-done.2.rest_1_), channel_id=1, source_target_pairs={{0,2},{1,31},{2,4},{3,1},{4,6},{5,3},{6,8},{7,5},{8,10},{9,7},{10,... | collective-permute-start | bytes 811016 | tf_op jit(solution)/shard_map/ppermute | solution.py:163
  14.3 1.7 %shard_map.59 = (bf16[512,768]{1,0:T(8,128)(2,1)S(1)}, bf16[512,768]{1,0:T(8,128)(2,1)S(1)}, f32[512,768]{1,0:T(8,128)S(1)}, f32[512,768]{1,0:T(8,128)S(1)}) custom-call(f32[1]{0:T(128)S(6)} %copy.14.scale_ref, f32[1]{0:T(128)S(6)} %copy.15.offset_ref, bf16[512,768]{1,0:T(8,128)(2,1)S(1)} %copy-done, bf16[512,768]{1,0:T(8,128)(2,1)S(1)} %copy-done.1), custom_call_target="tpu_custom_call" | custom-call | flops 800000000 | bytes 1024 | tf_op jit(solution)/shard_map/pallas_call | solution.py:117
  16.1 1.5 %collective-permute-done.1.rest_0_ = bf16[160,768]{1,0:T(8,128)(2,1)S(1)} collective-permute-done((bf16[160,768]{1,0:T(8,128)(2,1)S(1)}, bf16[160,768]{1,0:T(8,128)(2,1)S(1)}, u32[]{:S(2)}, u32[]{:S(2)}) %collective-permute-start.1) | collective-permute-done | bytes 245792 | tf_op jit(solution)/shard_map/ppermute | solution.py:163
  17.6 2.0 %collective-permute-start.5 = (bf16[160,768]{1,0:T(8,128)(2,1)S(1)}, bf16[160,768]{1,0:T(8,128)(2,1)S(1)}, u32[]{:S(2)}, u32[]{:S(2)}) collective-permute-start(bf16[160,768]{1,0:T(8,128)(2,1)S(1)} %collective-permute-done.1.rest_0_), channel_id=1, source_target_pairs={{0,2},{1,31},{2,4},{3,1},{4,6},{5,3},{6,8},{7,5},{8,10},{9,7},{10,... | collective-permute-start | bytes 737288 | tf_op jit(solution)/shard_map/ppermute | solution.py:163
  19.6 0.0 collective-permute-done
  19.6 1.9 %collective-permute-start.8 = (bf16[176,768]{1,0:T(8,128)(2,1)S(1)}, bf16[176,768]{1,0:T(8,128)(2,1)S(1)}, u32[]{:S(2)}, u32[]{:S(2)}) collective-permute-start(bf16[176,768]{1,0:T(8,128)(2,1)S(1)} %get-tuple-element.29), channel_id=1, source_target_pairs={{0,1},{1,0},{2,3},{3,2},{4,5},{5,4},{6,7},{7,6},{8,9},{9,8},{10,11... | collective-permute-start | bytes 811016 | tf_op jit(solution)/shard_map/ppermute | solution.py:163
  21.5 1.3 %shard_map.61.sum_in = f32[512,768]{1,0:T(8,128)S(1)} custom-call(f32[1]{0:T(128)S(6)} %copy.14.scale_ref, f32[1]{0:T(128)S(6)} %copy.15.offset_ref, bf16[512,768]{1,0:T(8,128)(2,1)S(1)} %get-tuple-element.18.low_ref, f32[512,768]{1,0:T(8,128)S(1)} %get-tuple-element.20.sum_in, ...), custom_call_target="tpu_custom_call", output_to_operand_aliasing={{}: (3, {})} | custom-call | flops 400000000 | bytes 1024 | tf_op jit(solution)/shard_map/pallas_call | solution.py:130
  22.8 0.6 %collective-permute-done.3.rest_0_ = bf16[176,768]{1,0:T(8,128)(2,1)S(1)} collective-permute-done((bf16[176,768]{1,0:T(8,128)(2,1)S(1)}, bf16[176,768]{1,0:T(8,128)(2,1)S(1)}, u32[]{:S(2)}, u32[]{:S(2)}) %collective-permute-start.3) | collective-permute-done | bytes 270368 | tf_op jit(solution)/shard_map/ppermute | solution.py:163
  23.4 2.0 %collective-permute-start.10 = (bf16[160,768]{1,0:T(8,128)(2,1)S(1)}, bf16[160,768]{1,0:T(8,128)(2,1)S(1)}, u32[]{:S(2)}, u32[]{:S(2)}) collective-permute-start(bf16[160,768]{1,0:T(8,128)(2,1)S(1)} %slice.15), channel_id=1, source_target_pairs={{0,1},{1,0},{2,3},{3,2},{4,5},{5,4},{6,7},{7,6},{8,9},{9,8},{10,11... | collective-permute-start | bytes 737288 | tf_op jit(solution)/shard_map/ppermute | solution.py:163
  25.3 0.0 collective-permute-done.4.rest_0_
  25.4 1.6 %collective-permute-start.6 = (bf16[176,768]{1,0:T(8,128)(2,1)S(1)}, bf16[176,768]{1,0:T(8,128)(2,1)S(1)}, u32[]{:S(2)}, u32[]{:S(2)}) collective-permute-start(bf16[176,768]{1,0:T(8,128)(2,1)S(1)} %collective-permute-done.3.rest_0_), channel_id=1, source_target_pairs={{0,2},{1,31},{2,4},{3,1},{4,6},{5,3},{6,8},{7,5},{8,10},{9,7},{10,... | collective-permute-start | bytes 811016 | tf_op jit(solution)/shard_map/ppermute | solution.py:163
  26.9 1.1 %shard_map.62.sum_ref = f32[512,768]{1,0:T(8,128)S(1)} custom-call(f32[1]{0:T(128)S(6)} %copy.14.scale_ref, f32[1]{0:T(128)S(6)} %copy.15.offset_ref, bf16[512,768]{1,0:T(8,128)(2,1)S(1)} %get-tuple-element.18.low_ref, f32[512,768]{1,0:T(8,128)S(1)} %shard_map.61.sum_in, ...), custom_call_target="tpu_custom_call", output_to_operand_aliasing={{}: (3, {})} | custom-call | flops 400000000 | bytes 1024 | tf_op jit(solution)/shard_map/pallas_call | solution.py:130
  28.0 1.2 %collective-permute-done.7.rest_0_ = bf16[176,768]{1,0:T(8,128)(2,1)S(1)} collective-permute-done((bf16[176,768]{1,0:T(8,128)(2,1)S(1)}, bf16[176,768]{1,0:T(8,128)(2,1)S(1)}, u32[]{:S(2)}, u32[]{:S(2)}) %collective-permute-start.7) | collective-permute-done | bytes 270368 | tf_op jit(solution)/shard_map/ppermute | solution.py:163
  29.2 2.0 %collective-permute-start.9 = (bf16[176,768]{1,0:T(8,128)(2,1)S(1)}, bf16[176,768]{1,0:T(8,128)(2,1)S(1)}, u32[]{:S(2)}, u32[]{:S(2)}) collective-permute-start(bf16[176,768]{1,0:T(8,128)(2,1)S(1)} %collective-permute-done.7.rest_0_), channel_id=1, source_target_pairs={{0,2},{1,31},{2,4},{3,1},{4,6},{5,3},{6,8},{7,5},{8,10},{9,7},{10,... | collective-permute-start | bytes 811016 | tf_op jit(solution)/shard_map/ppermute | solution.py:163
  31.2 1.1 %shard_map.64.sum_in = f32[512,768]{1,0:T(8,128)S(1)} custom-call(f32[1]{0:T(128)S(6)} %copy.14.scale_ref, f32[1]{0:T(128)S(6)} %copy.15.offset_ref, bf16[512,768]{1,0:T(8,128)(2,1)S(1)} %get-tuple-element.25.low_ref, f32[512,768]{1,0:T(8,128)S(1)} %get-tuple-element.26.sum_in, ...), custom_call_target="tpu_custom_call", output_to_operand_aliasing={{}: (3, {})} | custom-call | flops 400000000 | bytes 1024 | tf_op jit(solution)/shard_map/pallas_call | solution.py:130
  32.3 2.7 %collective-permute-done.8.rest_0_ = bf16[176,768]{1,0:T(8,128)(2,1)S(1)} collective-permute-done((bf16[176,768]{1,0:T(8,128)(2,1)S(1)}, bf16[176,768]{1,0:T(8,128)(2,1)S(1)}, u32[]{:S(2)}, u32[]{:S(2)}) %collective-permute-start.8) | collective-permute-done | bytes 270368 | tf_op jit(solution)/shard_map/ppermute | solution.py:163
  35.0 2.0 %collective-permute-start.11 = (bf16[176,768]{1,0:T(8,128)(2,1)S(1)}, bf16[176,768]{1,0:T(8,128)(2,1)S(1)}, u32[]{:S(2)}, u32[]{:S(2)}) collective-permute-start(bf16[176,768]{1,0:T(8,128)(2,1)S(1)} %collective-permute-done.8.rest_0_), channel_id=1, source_target_pairs={{0,2},{1,31},{2,4},{3,1},{4,6},{5,3},{6,8},{7,5},{8,10},{9,7},{10,... | collective-permute-start | bytes 811016 | tf_op jit(solution)/shard_map/ppermute | solution.py:163
  37.0 1.9 %collective-permute-start.12 = (bf16[160,768]{1,0:T(8,128)(2,1)S(1)}, bf16[160,768]{1,0:T(8,128)(2,1)S(1)}, u32[]{:S(2)}, u32[]{:S(2)}) collective-permute-start(bf16[160,768]{1,0:T(8,128)(2,1)S(1)} %collective-permute-done), channel_id=1, source_target_pairs={{0,1},{1,0},{2,3},{3,2},{4,5},{5,4},{6,7},{7,6},{8,9},{9,8},{10,11... | collective-permute-start | bytes 737288 | tf_op jit(solution)/shard_map/ppermute | solution.py:163
  38.9 0.0 collective-permute-done.6.rest_2_
  38.9 2.4 %shard_map.63 = f32[512,768]{1,0:T(8,128)} custom-call(f32[1]{0:T(128)S(6)} %copy.14.scale_ref, f32[1]{0:T(128)S(6)} %copy.15.offset_ref, bf16[512,768]{1,0:T(8,128)(2,1)S(1)} %copy-done, bf16[512,768]{1,0:T(8,128)(2,1)S(1)} %get-tuple-element.18.low_ref, f32[512,768]{1,0:T(8,128)S(1)} %shard_map.62.sum_ref, ...), custom_call_target="tpu_custom_call" | custom-call | flops 50000000 | bytes 1024 | tf_op jit(solution)/shard_map/pallas_call | solution.py:146
  41.3 0.0 collective-permute-done.10.rest_2_
  41.3 1.0 %collective-permute-done.9.rest_1_ = bf16[176,768]{1,0:T(8,128)(2,1)S(1)} collective-permute-done((bf16[176,768]{1,0:T(8,128)(2,1)S(1)}, bf16[176,768]{1,0:T(8,128)(2,1)S(1)}, u32[]{:S(2)}, u32[]{:S(2)}) %collective-permute-start.9) | collective-permute-done | bytes 270368 | tf_op jit(solution)/shard_map/ppermute | solution.py:163
  42.3 1.3 %shard_map.65.sum_ref = f32[512,768]{1,0:T(8,128)S(1)} custom-call(f32[1]{0:T(128)S(6)} %copy.14.scale_ref, f32[1]{0:T(128)S(6)} %copy.15.offset_ref, bf16[512,768]{1,0:T(8,128)(2,1)S(1)} %get-tuple-element.25.low_ref, f32[512,768]{1,0:T(8,128)S(1)} %shard_map.64.sum_in, ...), custom_call_target="tpu_custom_call", output_to_operand_aliasing={{}: (3, {})} | custom-call | flops 400000000 | bytes 1024 | tf_op jit(solution)/shard_map/pallas_call | solution.py:130
  43.7 1.2 %collective-permute-done.12.rest_1_ = bf16[160,768]{1,0:T(8,128)(2,1)S(1)} collective-permute-done((bf16[160,768]{1,0:T(8,128)(2,1)S(1)}, bf16[160,768]{1,0:T(8,128)(2,1)S(1)}, u32[]{:S(2)}, u32[]{:S(2)}) %collective-permute-start.12) | collective-permute-done | bytes 245792 | tf_op jit(solution)/shard_map/ppermute | solution.py:163
  44.9 3.2 %collective-permute-done.11.rest_0_ = bf16[176,768]{1,0:T(8,128)(2,1)S(1)} collective-permute-done((bf16[176,768]{1,0:T(8,128)(2,1)S(1)}, bf16[176,768]{1,0:T(8,128)(2,1)S(1)}, u32[]{:S(2)}, u32[]{:S(2)}) %collective-permute-start.11) | collective-permute-done | bytes 270368 | tf_op jit(solution)/shard_map/ppermute | solution.py:163
  48.1 2.3 %shard_map.66 = f32[512,768]{1,0:T(8,128)} custom-call(f32[1]{0:T(128)S(6)} %copy.14.scale_ref, f32[1]{0:T(128)S(6)} %copy.15.offset_ref, bf16[512,768]{1,0:T(8,128)(2,1)S(1)} %copy-done.1, bf16[512,768]{1,0:T(8,128)(2,1)S(1)} %get-tuple-element.25.low_ref, f32[512,768]{1,0:T(8,128)S(1)} %shard_map.65.sum_ref, ...), custom_call_target="tpu_custom_call" | custom-call | flops 50000000 | bytes 1024 | tf_op jit(solution)/shard_map/pallas_call | solution.py:146
  (10 shorter events, 0.1 us)
Async XLA Ops:
  0.6 4.3 %copy-start = (bf16[512,768]{1,0:T(8,128)(2,1)S(1)}, bf16[512,768]{1,0:T(8,128)(2,1)}, u32[]{:S(2)}) copy-start(bf16[512,768]{1,0:T(8,128)(2,1)} %raw_ref.2) | copy-start | bytes 2359300
  0.6 1.2 %copy-start.1 = (bf16[512,768]{1,0:T(8,128)(2,1)S(1)}, bf16[512,768]{1,0:T(8,128)(2,1)}, u32[]{:S(2)}) copy-start(bf16[512,768]{1,0:T(8,128)(2,1)} %raw_ref.3) | copy-start | bytes 2359300
  1.9 10.4 %collective-permute-start.2 = (bf16[176,768]{1,0:T(8,128)(2,1)S(1)}, bf16[176,768]{1,0:T(8,128)(2,1)S(1)}, u32[]{:S(2)}, u32[]{:S(2)}) collective-permute-start(bf16[176,768]{1,0:T(8,128)(2,1)S(1)} %shard_map.60), channel_id=1, source_target_pairs={{0,1},{1,0},{2,3},{3,2},{4,5},{5,4},{6,7},{7,6},{8,9},{9,8},{10,11... | collective-permute-start | bytes 811016 | tf_op jit(solution)/shard_map/ppermute | solution.py:163
  4.9 14.7 %collective-permute-start = (bf16[160,768]{1,0:T(8,128)(2,1)S(1)}, bf16[160,768]{1,0:T(8,128)(2,1)S(1)}, u32[]{:S(2)}, u32[]{:S(2)}) collective-permute-start(bf16[160,768]{1,0:T(8,128)(2,1)S(1)} %slice.15), channel_id=1, source_target_pairs={{0,30},{1,3},{2,0},{3,5},{4,2},{5,7},{6,4},{7,9},{8,6},{9,11},{10,... | collective-permute-start | bytes 737288 | tf_op jit(solution)/shard_map/ppermute | solution.py:163
  8.7 8.9 %collective-permute-start.1 = (bf16[160,768]{1,0:T(8,128)(2,1)S(1)}, bf16[160,768]{1,0:T(8,128)(2,1)S(1)}, u32[]{:S(2)}, u32[]{:S(2)}) collective-permute-start(bf16[160,768]{1,0:T(8,128)(2,1)S(1)} %slice.16), channel_id=1, source_target_pairs={{0,1},{1,0},{2,3},{3,2},{4,5},{5,4},{6,7},{7,6},{8,9},{9,8},{10,11... | collective-permute-start | bytes 737288 | tf_op jit(solution)/shard_map/ppermute | solution.py:163
  8.8 14.6 %collective-permute-start.3 = (bf16[176,768]{1,0:T(8,128)(2,1)S(1)}, bf16[176,768]{1,0:T(8,128)(2,1)S(1)}, u32[]{:S(2)}, u32[]{:S(2)}) collective-permute-start(bf16[176,768]{1,0:T(8,128)(2,1)S(1)} %slice.17), channel_id=1, source_target_pairs={{0,1},{1,0},{2,3},{3,2},{4,5},{5,4},{6,7},{7,6},{8,9},{9,8},{10,11... | collective-permute-start | bytes 811016 | tf_op jit(solution)/shard_map/ppermute | solution.py:163
  10.9 18.2 %collective-permute-start.7 = (bf16[176,768]{1,0:T(8,128)(2,1)S(1)}, bf16[176,768]{1,0:T(8,128)(2,1)S(1)}, u32[]{:S(2)}, u32[]{:S(2)}) collective-permute-start(bf16[176,768]{1,0:T(8,128)(2,1)S(1)} %get-tuple-element.27), channel_id=1, source_target_pairs={{0,1},{1,0},{2,3},{3,2},{4,5},{5,4},{6,7},{7,6},{8,9},{9,8},{10,11... | collective-permute-start | bytes 811016 | tf_op jit(solution)/shard_map/ppermute | solution.py:163
  12.3 13.0 %collective-permute-start.4 = (bf16[176,768]{1,0:T(8,128)(2,1)S(1)}, bf16[176,768]{1,0:T(8,128)(2,1)S(1)}, u32[]{:S(2)}, u32[]{:S(2)}) collective-permute-start(bf16[176,768]{1,0:T(8,128)(2,1)S(1)} %collective-permute-done.2.rest_1_), channel_id=1, source_target_pairs={{0,2},{1,31},{2,4},{3,1},{4,6},{5,3},{6,8},{7,5},{8,10},{9,7},{10,... | collective-permute-start | bytes 811016 | tf_op jit(solution)/shard_map/ppermute | solution.py:163
  17.6 11.6 %collective-permute-start.5 = (bf16[160,768]{1,0:T(8,128)(2,1)S(1)}, bf16[160,768]{1,0:T(8,128)(2,1)S(1)}, u32[]{:S(2)}, u32[]{:S(2)}) collective-permute-start(bf16[160,768]{1,0:T(8,128)(2,1)S(1)} %collective-permute-done.1.rest_0_), channel_id=1, source_target_pairs={{0,2},{1,31},{2,4},{3,1},{4,6},{5,3},{6,8},{7,5},{8,10},{9,7},{10,... | collective-permute-start | bytes 737288 | tf_op jit(solution)/shard_map/ppermute | solution.py:163
  19.6 15.4 %collective-permute-start.8 = (bf16[176,768]{1,0:T(8,128)(2,1)S(1)}, bf16[176,768]{1,0:T(8,128)(2,1)S(1)}, u32[]{:S(2)}, u32[]{:S(2)}) collective-permute-start(bf16[176,768]{1,0:T(8,128)(2,1)S(1)} %get-tuple-element.29), channel_id=1, source_target_pairs={{0,1},{1,0},{2,3},{3,2},{4,5},{5,4},{6,7},{7,6},{8,9},{9,8},{10,11... | collective-permute-start | bytes 811016 | tf_op jit(solution)/shard_map/ppermute | solution.py:163
  23.4 17.9 %collective-permute-start.10 = (bf16[160,768]{1,0:T(8,128)(2,1)S(1)}, bf16[160,768]{1,0:T(8,128)(2,1)S(1)}, u32[]{:S(2)}, u32[]{:S(2)}) collective-permute-start(bf16[160,768]{1,0:T(8,128)(2,1)S(1)} %slice.15), channel_id=1, source_target_pairs={{0,1},{1,0},{2,3},{3,2},{4,5},{5,4},{6,7},{7,6},{8,9},{9,8},{10,11... | collective-permute-start | bytes 737288 | tf_op jit(solution)/shard_map/ppermute | solution.py:163
  25.4 13.5 %collective-permute-start.6 = (bf16[176,768]{1,0:T(8,128)(2,1)S(1)}, bf16[176,768]{1,0:T(8,128)(2,1)S(1)}, u32[]{:S(2)}, u32[]{:S(2)}) collective-permute-start(bf16[176,768]{1,0:T(8,128)(2,1)S(1)} %collective-permute-done.3.rest_0_), channel_id=1, source_target_pairs={{0,2},{1,31},{2,4},{3,1},{4,6},{5,3},{6,8},{7,5},{8,10},{9,7},{10,... | collective-permute-start | bytes 811016 | tf_op jit(solution)/shard_map/ppermute | solution.py:163
  29.2 13.1 %collective-permute-start.9 = (bf16[176,768]{1,0:T(8,128)(2,1)S(1)}, bf16[176,768]{1,0:T(8,128)(2,1)S(1)}, u32[]{:S(2)}, u32[]{:S(2)}) collective-permute-start(bf16[176,768]{1,0:T(8,128)(2,1)S(1)} %collective-permute-done.7.rest_0_), channel_id=1, source_target_pairs={{0,2},{1,31},{2,4},{3,1},{4,6},{5,3},{6,8},{7,5},{8,10},{9,7},{10,... | collective-permute-start | bytes 811016 | tf_op jit(solution)/shard_map/ppermute | solution.py:163
  35.0 13.1 %collective-permute-start.11 = (bf16[176,768]{1,0:T(8,128)(2,1)S(1)}, bf16[176,768]{1,0:T(8,128)(2,1)S(1)}, u32[]{:S(2)}, u32[]{:S(2)}) collective-permute-start(bf16[176,768]{1,0:T(8,128)(2,1)S(1)} %collective-permute-done.8.rest_0_), channel_id=1, source_target_pairs={{0,2},{1,31},{2,4},{3,1},{4,6},{5,3},{6,8},{7,5},{8,10},{9,7},{10,... | collective-permute-start | bytes 811016 | tf_op jit(solution)/shard_map/ppermute | solution.py:163
  37.0 7.9 %collective-permute-start.12 = (bf16[160,768]{1,0:T(8,128)(2,1)S(1)}, bf16[160,768]{1,0:T(8,128)(2,1)S(1)}, u32[]{:S(2)}, u32[]{:S(2)}) collective-permute-start(bf16[160,768]{1,0:T(8,128)(2,1)S(1)} %collective-permute-done), channel_id=1, source_target_pairs={{0,1},{1,0},{2,3},{3,2},{4,5},{5,4},{6,7},{7,6},{8,9},{9,8},{10,11... | collective-permute-start | bytes 737288 | tf_op jit(solution)/shard_map/ppermute | solution.py:163
